TPU v7x, 256 devices: a whole 4x4x8 slice. The times are simulated.
256 devices in a mesh: gz: 32 (over z_lo, x, core), gy: 8 (over z_hi, y).
Axes of the slice: x: 4, y: 4, z: 8 (z_hi: 2, z_lo: 4; z = z_hi * 4 + z_lo), core: 2. Of those that a mesh axis runs over, the one named last changes fastest.
Arguments:
- features: bfloat16 [32, 320, 96, 128], P(None, 'gz', 'gy'), may hold values from -6 to 6
- labels: int32 [320, 96, 128], P('gz', 'gy'), may hold values from 0 to 65535
- weight: bfloat16 [16, 32, 3, 3, 3], replicated, may hold values from -0.21875 to 0.21875
- conv_bias: float32 [16], replicated, may hold values from -3 to 3
Outputs:
- feature_grad: bfloat16 [32, 320, 96, 128], P(None, 'gz', 'gy')
- weight_grad: float32 [16, 32, 3, 3, 3], replicated
- bias_grad: float32 [16], replicated
- loss: float32 [], replicated
All inputs are finite; a program needn't handle non-finite values.
Results may differ from a plain program's by a relative error of at most 0.0075.
Values may be sent and summed in bfloat16 or wider, within the bound.
No kernel may reach another device: no remote copies, remote signals or barrier semaphores. Data moves between devices by JAX's collectives and lax.ppermute only.
A program may use at most 128 MiB of HBM per device.

v0:
```python
import functools

import jax
import jax.numpy as jnp
from jax import lax
from jax.experimental import pallas as pl
from jax.experimental.pallas import tpu as pltpu
from jax.sharding import PartitionSpec as P

OFFSETS = (1, 3, 9)
REACH = 9
BF = jnp.bfloat16
F32 = jnp.float32
PARAMS = pltpu.CompilerParams(vmem_limit_bytes=48 * 1024 * 1024)
VM = pl.BlockSpec(memory_space=pltpu.VMEM)
SM = pl.BlockSpec(memory_space=pltpu.SMEM)


def call(body, outs, args, specs, scratch=(), flops=0):
    size = sum(a.size * a.dtype.itemsize for a in args)
    return pl.pallas_call(
        body,
        out_shape=outs,
        in_specs=specs,
        out_specs=jax.tree.map(lambda _: VM, outs),
        scratch_shapes=list(scratch),
        compiler_params=PARAMS,
        cost_estimate=pl.CostEstimate(flops=flops, bytes_accessed=size, transcendentals=0),
    )(*args)


def even_pairs(count):
    return [(i, i ^ 1) for i in range(count - count % 2)]


def odd_pairs(count):
    pairs = [(i, i + 1) for i in range(1, count - 1, 2)]
    return pairs + [(j, i) for i, j in pairs]


def lane_shift(value, step):
    lanes = value.shape[-1]
    moved = pltpu.roll(value, (-step) % lanes, value.ndim - 1)
    lane = lax.broadcasted_iota(jnp.int32, value.shape, value.ndim - 1)
    keep = (lane < lanes - step) if step > 0 else (lane >= -step)
    return jnp.where(keep, moved, 0)


def pair_terms(logits, same):
    target = same.astype(F32)
    small = jnp.exp(-jnp.abs(logits))
    inverse = 1.0 / (1.0 + small)
    sigmoid = jnp.where(logits >= 0, inverse, small * inverse)
    slopes = (sigmoid - target) * 0.25
    losses = jnp.maximum(logits, 0.0) + jnp.log(1.0 + small) - target * logits
    return slopes, losses


def dots(left, right):
    return jnp.sum(left * right, axis=1) * 0.25


def fill_rim(ext, own_ref, ze, zo, ye, yo, pz, py, planes, rows):
    ext[1 : planes + 1, 1 : rows + 1] = own_ref[...]
    ext[(1 - pz) * (planes + 1), 1 : rows + 1] = ze[...]
    ext[pz * (planes + 1), 1 : rows + 1] = zo[...]
    ext[:, (1 - py) * (rows + 1)] = ye[...]
    ext[:, py * (rows + 1)] = yo[...]


def conv_rows(ext, w_ref, z, y, width):
    stack = [
        jnp.concatenate([ext[z + a, y + i + b] for i in range(width)], axis=1)
        for a in range(3)
        for b in range(3)
    ]
    sums = jnp.dot(w_ref[...], jnp.concatenate(stack, axis=0), preferred_element_type=F32)
    third = sums.shape[0] // 3
    lanes = sums.shape[1] // width
    for i in range(width):
        part = sums[:, i * lanes : (i + 1) * lanes]
        yield (
            lane_shift(part[:third], -1)
            + part[third : 2 * third]
            + lane_shift(part[2 * third :], 1)
        )


def forward_kernel(pos, own, ze, zo, ye, yo, w, bias, emb, ext, se, so, te, to):
    planes, rows = own.shape[0], own.shape[1]
    pz, py = pos[0], pos[1]
    fill_rim(ext, own, ze, zo, ye, yo, pz, py, planes, rows)

    @pl.loop(0, planes)
    def _(z):
        for y in range(0, rows, 2):
            for i, value in enumerate(conv_rows(ext, w, z, y, 2)):
                emb[z, y + i] = (value + bias[...]).astype(BF)

    se[...] = emb[pl.ds((1 - pz) * (planes - REACH), REACH)]
    so[...] = emb[pl.ds(pz * (planes - REACH), REACH)]
    te[...] = emb[:, pl.ds((1 - py) * (rows - REACH), REACH)]
    to[...] = emb[:, pl.ds(py * (rows - REACH), REACH)]


def inner_kernel(emb, lab, grad, loss):
    planes, rows = emb.shape[0], emb.shape[1]
    lanes = emb.shape[3]
    lane = lax.broadcasted_iota(jnp.int32, (rows, lanes), 1)
    loss[...] = jnp.zeros_like(loss)

    @pl.loop(0, planes)
    def _(z):
        center = emb[z].astype(F32)
        here = lab[z]
        total = jnp.zeros(center.shape, F32)
        lost = jnp.zeros((rows, lanes), F32)
        for o in OFFSETS:
            if o < lanes:
                after = pltpu.roll(center, lanes - o, 2)
                before = pltpu.roll(center, o, 2)
                live = lane < lanes - o
                slopes, losses = pair_terms(
                    dots(center, after), here == pltpu.roll(here, lanes - o, 1)
                )
                slopes = jnp.where(live, slopes, 0.0)
                lost = lost + jnp.where(live, losses, 0.0)
                total = total + slopes[:, None, :] * after
                total = total + pltpu.roll(slopes, o, 1)[:, None, :] * before
        grad[z] = total
        for o in OFFSETS:
            if o < rows:
                low, high = center[: rows - o], center[o:]
                slopes, losses = pair_terms(dots(low, high), here[: rows - o] == here[o:])
                grad[z, : rows - o] += slopes[:, None, :] * high
                grad[z, o:] += slopes[:, None, :] * low
                loss[: rows - o] += losses
        loss[:rows] += lost

    for o in OFFSETS:

        @pl.loop(0, planes - o)
        def _(z):
            low, high = emb[z].astype(F32), emb[z + o].astype(F32)
            slopes, losses = pair_terms(dots(low, high), lab[z] == lab[z + o])
            grad[z] += slopes[:, None, :] * high
            grad[z + o] += slopes[:, None, :] * low
            loss[:rows] += losses


def outer_kernel(
    pos, emb, lab, grad, loss, ze, zo, ye, yo, labz, laby, out, shifted, fe, fo, sums
):
    planes, rows = emb.shape[0], emb.shape[1]
    pz, py = pos[0], pos[1]
    for halo, is_high in ((ze, 1 - pz), (zo, pz)):
        weight = (is_high * pos[2]).astype(F32)
        for o in OFFSETS:

            @pl.loop(0, o)
            def _(t):
                p = t + is_high * (planes - o)
                q = t + (1 - is_high) * (REACH - o)
                other = halo[q].astype(F32)
                slopes, losses = pair_terms(
                    dots(emb[p].astype(F32), other), lab[p] == labz[is_high, q]
                )
                grad[p] += slopes[:, None, :] * other
                loss[:rows] += losses * weight

    for halo, is_high in ((ye, 1 - py), (yo, py)):
        weight = (is_high * pos[3]).astype(F32)

        @pl.loop(0, planes)
        def _(z):
            for o in OFFSETS:
                p = is_high * (rows - o)
                q = (1 - is_high) * (REACH - o)
                other = halo[z, pl.ds(q, o)].astype(F32)
                mine = emb[z, pl.ds(p, o)].astype(F32)
                here = jnp.where(is_high == 1, lab[z, rows - o :], lab[z, :o])
                there = jnp.where(
                    is_high == 1, laby[1, z, :o], laby[0, z, REACH - o :]
                )
                slopes, losses = pair_terms(dots(mine, other), here == there)
                grad[z, pl.ds(p, o)] += slopes[:, None, :] * other
                loss[:o] += losses * weight

    shifted[...] = jnp.zeros_like(shifted)
    third = emb.shape[2]

    @pl.loop(0, planes)
    def _(z):
        value = grad[z].astype(BF)
        out[z] = value
        wide = value.astype(F32)
        shifted[z, 2 : rows + 2, :third] = lane_shift(wide, 1).astype(BF)
        shifted[z, 2 : rows + 2, third : 2 * third] = value
        shifted[z, 2 : rows + 2, 2 * third :] = lane_shift(wide, -1).astype(BF)

    fe[...] = out[(1 - pz) * (planes - 1)]
    fo[...] = out[pz * (planes - 1)]
    sums[...] = jnp.broadcast_to(
        jnp.sum(loss[...], keepdims=True), sums.shape
    )


def weight_kernel(shifted, ext, own, lost, out, acc):
    planes, rows = own.shape[0], own.shape[1]
    channels, lanes = own.shape[2], own.shape[3]
    acc[...] = jnp.zeros_like(acc)

    @pl.loop(0, planes)
    def _(z):
        total = acc[...]
        for y in range(0, rows + 2, 2):
            left = jnp.concatenate(
                [
                    jnp.concatenate([shifted[z, y + i + 2 - b] for b in range(3)], axis=0)
                    for i in range(2)
                ],
                axis=1,
            )
            right = jnp.concatenate(
                [
                    jnp.concatenate([ext[z + a, y + i] for a in range(3)], axis=0)
                    for i in range(2)
                ],
                axis=1,
            )
            total = total + lax.dot_general(
                left, right, (((1,), (1,)), ((), ())), preferred_element_type=F32
            )
        acc[...] = total

    height, width = acc.shape
    out[...] = jnp.zeros_like(out)
    out[:height, :width] = acc[...]
    tile = jnp.sum(own[...].astype(F32), axis=(0, 1))
    column = jnp.sum(tile, axis=1, keepdims=True)
    row = lax.broadcasted_iota(jnp.int32, (channels, lanes), 0)
    lane = lax.broadcasted_iota(jnp.int32, (channels, lanes), 1)
    line = jnp.sum(jnp.where(row == lane, column, 0.0), axis=0, keepdims=True)
    first = lax.broadcasted_iota(jnp.int32, (1, lanes), 1)
    out[height : height + 1, :] = jnp.where(first == channels, lost[0:1, :], line)


def backward_kernel(pos, own, ze, zo, ye, yo, w, out, ext):
    planes, rows = own.shape[0], own.shape[1]
    fill_rim(ext, own, ze, zo, ye, yo, pos[0], pos[1], planes, rows)

    @pl.loop(0, planes)
    def _(z):
        for y in range(0, rows, 2):
            for i, value in enumerate(conv_rows(ext, w, z, y, 2)):
                out[z, y + i] = value.astype(BF)


def final_kernel(voxels, pair_count, total, out, tail):
    groups, channels, width = out.shape
    per = groups // 3
    height = per * channels
    for a in range(3):
        part = total[:height, a * width : (a + 1) * width] * (1.0 / voxels)
        out[a * per : (a + 1) * per] = part.reshape(per, channels, width)
    line = total[height : height + 1, :]
    lane = lax.broadcasted_iota(jnp.int32, line.shape, 1)
    tail[...] = jnp.where(lane == channels, line * (1.0 / pair_count), line * (1.0 / voxels))


def rim_rows(block, low, high, index):
    own = lax.dynamic_index_in_dim(block, index, 1, keepdims=False)
    first = lax.dynamic_index_in_dim(low, index, 0)
    last = lax.dynamic_index_in_dim(high, index, 0)
    return jnp.concatenate([first, own, last], axis=0)


def swap_y(block, ze, zo, pz, py, gy):
    rows = block.shape[1]
    low = jnp.where(pz == 0, zo, ze)
    high = jnp.where(pz == 0, ze, zo)
    even = rim_rows(block, low, high, (1 - py) * (rows - 1))
    odd = rim_rows(block, low, high, py * (rows - 1))
    return (
        lax.ppermute(even, "gy", even_pairs(gy)),
        lax.ppermute(odd, "gy", odd_pairs(gy)),
    )


def total_of(value, gz, gy):
    rows = value.shape[0] // gz
    lanes = value.shape[1]
    mine = lax.all_to_all(value.reshape(gz, rows, lanes), "gz", 0, 0)
    mine = jnp.sum(mine, axis=0)
    mine = lax.all_to_all(jnp.broadcast_to(mine, (gy, rows, lanes)), "gy", 0, 0)
    mine = jnp.sum(mine, axis=0)
    mine = lax.all_to_all(jnp.broadcast_to(mine, (gz, rows, lanes)), "gz", 0, 0)
    return mine.reshape(gz * rows, lanes)


def per_device(features, labels, weight, conv_bias):
    ch_in, planes, rows, lanes = features.shape
    emb_ch = weight.shape[0]
    gz, gy = lax.axis_size("gz"), lax.axis_size("gy")
    depth, height = planes * gz, rows * gy
    voxels = depth * height * lanes
    pair_count = sum(
        (extent - o) * (voxels // extent)
        for extent in (depth, height, lanes)
        for o in OFFSETS
        if o < extent
    )
    iz, iy = lax.axis_index("gz"), lax.axis_index("gy")
    pz, py = lax.rem(iz, 2), lax.rem(iy, 2)
    pos = jnp.stack(
        [pz, py, (iz < gz - 1).astype(jnp.int32), (iy < gy - 1).astype(jnp.int32)]
    ).astype(jnp.int32)
    ze_pairs, zo_pairs = even_pairs(gz), odd_pairs(gz)
    ye_pairs, yo_pairs = even_pairs(gy), odd_pairs(gy)

    feat = jnp.transpose(features, (1, 2, 0, 3))
    taps = jnp.transpose(weight, (2, 3, 4, 0, 1))
    w_fwd = jnp.transpose(taps, (2, 3, 0, 1, 4)).reshape(3 * emb_ch, 9 * ch_in)
    w_bwd = jnp.transpose(taps[::-1, ::-1, ::-1], (2, 4, 0, 1, 3)).reshape(
        3 * ch_in, 9 * emb_ch
    )
    bias = jnp.broadcast_to(conv_bias[:, None], (emb_ch, lanes))

    fze = lax.ppermute(
        lax.dynamic_index_in_dim(feat, (1 - pz) * (planes - 1), 0, keepdims=False), "gz", ze_pairs
    )
    fzo = lax.ppermute(
        lax.dynamic_index_in_dim(feat, pz * (planes - 1), 0, keepdims=False), "gz", zo_pairs
    )
    fye, fyo = swap_y(feat, fze, fzo, pz, py, gy)

    def label_halo(dim, axis, parity, even, odd):
        room = labels.shape[dim] - REACH
        e = lax.dynamic_slice_in_dim(labels, (1 - parity) * room, REACH, dim)
        o = lax.dynamic_slice_in_dim(labels, parity * room, REACH, dim)
        e, o = lax.ppermute(e, axis, even), lax.ppermute(o, axis, odd)
        return jnp.stack([jnp.where(parity == 0, o, e), jnp.where(parity == 0, e, o)])

    labz = label_halo(0, "gz", pz, ze_pairs, zo_pairs)
    laby = label_halo(1, "gy", py, ye_pairs, yo_pairs)

    tile = (emb_ch, lanes)
    sds = jax.ShapeDtypeStruct
    conv_flops = 2 * planes * rows * lanes * 27 * ch_in * emb_ch
    emb, feat_ext, se, so, te, to = call(
        forward_kernel,
        (
            sds((planes, rows) + tile, BF),
            sds((planes + 2, rows + 2, ch_in, lanes), BF),
            sds((REACH, rows) + tile, BF),
            sds((REACH, rows) + tile, BF),
            sds((planes, REACH) + tile, BF),
            sds((planes, REACH) + tile, BF),
        ),
        (pos, feat, fze, fzo, fye, fyo, w_fwd, bias),
        [SM] + [VM] * 7,
        flops=conv_flops,
    )
    eyo = lax.ppermute(to, "gy", yo_pairs)
    eye = lax.ppermute(te, "gy", ye_pairs)
    ezo = lax.ppermute(so, "gz", zo_pairs)
    eze = lax.ppermute(se, "gz", ze_pairs)

    lost_rows = -(-rows // 8) * 8
    grad_in, loss_in = call(
        inner_kernel,
        (sds((planes, rows) + tile, F32), sds((lost_rows, lanes), F32)),
        (emb, labels),
        [VM] * 2,
        flops=conv_flops,
    )

    def outer(pos, emb, lab, g, l, ze, zo, ye, yo, lz, ly, out, shifted, fe, fo, sums, grad, loss):
        grad[...] = g[...]
        loss[...] = l[...]
        outer_kernel(
            pos, emb, lab, grad, loss, ze, zo, ye, yo, lz, ly, out, shifted, fe, fo, sums
        )

    grad, shifted, ge, go, lost = call(
        outer,
        (
            sds((planes, rows) + tile, BF),
            sds((planes, rows + 4, 3 * emb_ch, lanes), BF),
            sds((rows,) + tile, BF),
            sds((rows,) + tile, BF),
            sds((8, lanes), F32),
        ),
        (pos, emb, labels, grad_in, loss_in, eze, ezo, eye, eyo, labz, laby),
        [SM] + [VM] * 10,
        scratch=[pltpu.VMEM((planes, rows) + tile, F32), pltpu.VMEM((lost_rows, lanes), F32)],
        flops=conv_flops,
    )

    gze = lax.ppermute(ge, "gz", ze_pairs)
    gzo = lax.ppermute(go, "gz", zo_pairs)

    used = 9 * emb_ch + 1
    padded = -(-used // (8 * gz)) * 8 * gz
    partial = call(
        weight_kernel,
        sds((padded, lanes), F32),
        (shifted, feat_ext, grad, lost),
        [VM] * 4,
        scratch=[pltpu.VMEM((9 * emb_ch, 3 * ch_in), F32)],
        flops=conv_flops,
    )
    total = total_of(partial, gz, gy)

    gye, gyo = swap_y(grad, gze, gzo, pz, py, gy)
    feature_grad = call(
        backward_kernel,
        sds((planes, rows, ch_in, lanes), BF),
        (pos, grad, gze, gzo, gye, gyo, w_bwd),
        [SM] + [VM] * 6,
        scratch=[pltpu.VMEM((planes + 2, rows + 2) + tile, BF)],
        flops=conv_flops,
    )

    weight_grad, tail = call(
        functools.partial(final_kernel, voxels, pair_count),
        (sds((27, emb_ch, ch_in), F32), sds((1, lanes), F32)),
        (total,),
        [VM],
    )
    weight_grad = jnp.transpose(
        weight_grad.reshape(3, 3, 3, emb_ch, ch_in), (3, 4, 0, 1, 2)
    )
    return (
        jnp.transpose(feature_grad, (2, 0, 1, 3)),
        weight_grad,
        tail[0, :emb_ch],
        tail[0, emb_ch],
    )


def solution(mesh):
    return jax.shard_map(
        per_device,
        mesh=mesh,
        in_specs=(P(None, "gz", "gy", None), P("gz", "gy", None), P(), P()),
        out_specs=(P(None, "gz", "gy", None), P(), P(), P()),
        check_vma=False,
    )
```

profile of v0, /device:TPU:1, one launch (start us, length us, event | category | flops | bytes accessed | tf_op | source)
XLA Modules:
  0.0 130.2 jit_solution(6766703203770958375)
XLA Ops:
  0.7 1.0 dynamic-slice_bitcast_fusion
  1.7 3.3 %collective-permute-start = (bf16[12,32,128]{2,1,0:T(8,128)(2,1)S(1)}, bf16[12,32,128]{2,1,0:T(8,128)(2,1)S(1)}, u32[]{:S(2)}, u32[]{:S(2)}) collective-permute-start(bf16[12,32,128]{2,1,0:T(8,128)(2,1)S(1)} %get-tuple-element.37), channel_id=1, source_target_pairs={{0,8},{8,0},{16,24},{24,16},{32,40},{40,32},{48,56},{56,48},{64,72... | collective-permute-start | bytes 294920 | tf_op jit(solution)/shard_map/ppermute | solution.py:329
  5.0 1.9 %collective-permute-start.1 = (bf16[12,32,128]{2,1,0:T(8,128)(2,1)S(1)}, bf16[12,32,128]{2,1,0:T(8,128)(2,1)S(1)}, u32[]{:S(2)}, u32[]{:S(2)}) collective-permute-start(bf16[12,32,128]{2,1,0:T(8,128)(2,1)S(1)} %get-tuple-element.36), channel_id=1, source_target_pairs={{8,16},{24,32},{40,48},{56,64},{72,80},{88,96},{104,112},{120,128}... | collective-permute-start | bytes 294920 | tf_op jit(solution)/shard_map/ppermute | solution.py:332
  7.0 1.0 constant_dynamic-slice_fusion.5
  8.6 3.3 %collective-permute-start.11 = (s32[10,9,128]{2,1,0:T(8,128)S(1)}, s32[10,9,128]{2,1,0:T(8,128)S(1)}, u32[]{:S(2)}, u32[]{:S(2)}) collective-permute-start(s32[10,9,128]{2,1,0:T(8,128)S(1)} %get-tuple-element.53), channel_id=1, source_target_pairs={{0,1},{1,0},{2,3},{3,2},{4,5},{5,4},{6,7},{7,6},{8,9},{9,8},{10,11... | collective-permute-start | bytes 138248 | tf_op jit(solution)/shard_map/ppermute | solution.py:341
  12.9 3.1 %collective-permute-start.8 = (s32[9,12,128]{2,1,0:T(8,128)S(1)}, s32[9,12,128]{2,1,0:T(8,128)S(1)}, u32[]{:S(2)}, u32[]{:S(2)}) collective-permute-start(s32[9,12,128]{2,1,0:T(8,128)S(1)} %get-tuple-element.54), channel_id=1, source_target_pairs={{8,16},{24,32},{40,48},{56,64},{72,80},{88,96},{104,112},{120,128}... | collective-permute-start | bytes 165896 | tf_op jit(solution)/shard_map/ppermute | solution.py:341
  17.1 1.0 dynamic-slice_bitcast_fusion.2
  19.0 8.9 %collective-permute-start.2 = (bf16[12,32,128]{2,1,0:T(8,128)(2,1)S(1)}, bf16[12,32,128]{2,1,0:T(8,128)(2,1)S(1)}, u32[]{:S(2)}, u32[]{:S(2)}) collective-permute-start(bf16[12,32,128]{2,1,0:T(8,128)(2,1)S(1)} %pad_maximum_fusion), channel_id=1, source_target_pairs={{0,1},{1,0},{2,3},{3,2},{4,5},{5,4},{6,7},{7,6},{8,9},{9,8},{10,11... | collective-permute-start | bytes 294920 | tf_op jit(solution)/shard_map/ppermute | solution.py:285
  28.0 2.4 %collective-permute-done.2.ye = bf16[12,32,128]{2,1,0:T(8,128)(2,1)S(1)} collective-permute-done((bf16[12,32,128]{2,1,0:T(8,128)(2,1)S(1)}, bf16[12,32,128]{2,1,0:T(8,128)(2,1)S(1)}, u32[]{:S(2)}, u32[]{:S(2)}) %collective-permute-start.2) | collective-permute-done | bytes 98336 | tf_op jit(solution)/shard_map/ppermute | solution.py:285
  30.4 4.5 %shard_map.75 = (bf16[10,12,16,128]{3,2,1,0:T(8,128)(2,1)S(1)}, bf16[12,14,32,128]{3,2,1,0:T(8,128)(2,1)S(1)}, bf16[9,12,16,128]{3,2,1,0:T(8,128)(2,1)S(1)}, bf1...) custom-call(s32[4]{0:T(128)S(1)} %pad_add_fusion.2.pos, ...), custom_call_target="tpu_custom_call" | custom-call | flops 424673280 | bytes 1412112 | tf_op jit(solution)/shard_map/pallas_call | solution.py:21
  34.9 1.4 %collective-permute-start.4 = (bf16[9,12,16,128]{3,2,1,0:T(8,128)(2,1)S(1)}, bf16[9,12,16,128]{3,2,1,0:T(8,128)(2,1)S(1)}, u32[]{:S(2)}, u32[]{:S(2)}) collective-permute-start(bf16[9,12,16,128]{3,2,1,0:T(8,128)(2,1)S(1)} %get-tuple-element.22), channel_id=1, source_target_pairs={{0,8},{8,0},{16,24},{24,16},{32,40},{40,32},{48,56},{56,48},{64,72... | collective-permute-start | bytes 1327112 | tf_op jit(solution)/shard_map/ppermute | solution.py:367
  36.3 3.0 %collective-permute-start.5 = (bf16[9,12,16,128]{3,2,1,0:T(8,128)(2,1)S(1)}, bf16[9,12,16,128]{3,2,1,0:T(8,128)(2,1)S(1)}, u32[]{:S(2)}, u32[]{:S(2)}) collective-permute-start(bf16[9,12,16,128]{3,2,1,0:T(8,128)(2,1)S(1)} %get-tuple-element.23), channel_id=1, source_target_pairs={{8,16},{24,32},{40,48},{56,64},{72,80},{88,96},{104,112},{120,128}... | collective-permute-start | bytes 1327112 | tf_op jit(solution)/shard_map/ppermute | solution.py:366
  39.4 1.7 %collective-permute-start.6 = (bf16[10,9,16,128]{3,2,1,0:T(8,128)(2,1)S(1)}, bf16[10,9,16,128]{3,2,1,0:T(8,128)(2,1)S(1)}, u32[]{:S(2)}, u32[]{:S(2)}) collective-permute-start(bf16[10,9,16,128]{3,2,1,0:T(8,128)(2,1)S(1)} %get-tuple-element.24), channel_id=1, source_target_pairs={{0,1},{1,0},{2,3},{3,2},{4,5},{5,4},{6,7},{7,6},{8,9},{9,8},{10,11... | collective-permute-start | bytes 1105928 | tf_op jit(solution)/shard_map/ppermute | solution.py:365
  41.9 5.8 %shard_map.76 = (f32[10,12,16,128]{3,2,1,0:T(8,128)S(1)}, f32[16,128]{1,0:T(8,128)S(1)}) custom-call(bf16[10,12,16,128]{3,2,1,0:T(8,128)(2,1)S(1)} %get-tuple-element.19.emb, s32[10,12,128]{2,1,0:T(8,128)S(1)} %copy-done), custom_call_target="tpu_custom_call" | custom-call | flops 424673280 | bytes 552960 | tf_op jit(solution)/shard_map/pallas_call | solution.py:21
  48.0 5.6 %shard_map.77 = (bf16[10,12,16,128]{3,2,1,0:T(8,128)(2,1)S(1)}, bf16[10,16,48,128]{3,2,1,0:T(8,128)(2,1)S(1)}, bf16[12,16,128]{2,1,0:T(8,128)(2,1)S(1)}, bf16[12,16,128]{2,1,0:T(8,128)(2,1)S(1)}, f32[8,128]{1,0:T(8,128)S(1)}) custom-call(s32[4]{0:T(128)S(1)} %pad_add_fusion.2.pos, bf16[10,12,16,128]{3,2,1,0:T(8,128)(2,1)S(1)} %get-tuple-element.19.emb, ...), custom_call_target="tpu_custom_call" | custom-call | flops 424673280 | bytes 3368976 | tf_op jit(solution)/shard_map/pallas_call | solution.py:21
  53.6 5.4 %collective-permute-start.13 = (bf16[12,16,128]{2,1,0:T(8,128)(2,1)S(1)}, bf16[12,16,128]{2,1,0:T(8,128)(2,1)S(1)}, u32[]{:S(2)}, u32[]{:S(2)}) collective-permute-start(bf16[12,16,128]{2,1,0:T(8,128)(2,1)S(1)} %get-tuple-element.28), channel_id=1, source_target_pairs={{8,16},{24,32},{40,48},{56,64},{72,80},{88,96},{104,112},{120,128}... | collective-permute-start | bytes 147464 | tf_op jit(solution)/shard_map/ppermute | solution.py:401
  59.1 3.8 %shard_map.79 = f32[256,128]{1,0:T(8,128)} custom-call(bf16[10,16,48,128]{3,2,1,0:T(8,128)(2,1)S(1)} %get-tuple-element.29.shifted, bf16[12,14,32,128]{3,2,1,0:T(8,128)(2,1)S(1)} %get-tuple-element.30.ext, bf16[10,12,16,128]{3,2,1,0:T(8,128)(2,1)S(1)} %get-tuple-element.26.own, f32[8,128]{1,0:T(8,128)S(1)} %get-tuple-element.31.lost), custom_call_target="tpu_custom_call" | custom-call | flops 424673280 | bytes 3837952 | tf_op jit(solution)/shard_map/pallas_call | solution.py:21
  62.9 6.8 %all-to-all-start = ((f32[32,8,128]{2,1,0:T(8,128)}), f32[32,8,128]{2,1,0:T(8,128)S(1)}, u32[]{:S(2)}, u32[]{:S(2)}) async-start(f32[32,8,128]{2,1,0:T(8,128)} %bitcast.23), calls=%async_computation | async-start | bytes 262144 | tf_op jit(solution)/shard_map/all_to_all | solution.py:293
  69.9 8.5 %all-to-all-done = f32[32,8,128]{2,1,0:T(8,128)S(1)} async-done(((f32[32,8,128]{2,1,0:T(8,128)}), f32[32,8,128]{2,1,0:T(8,128)S(1)}, u32[]{:S(2)}, u32[]{:S(2)}) %all-to-all-start) | async-done | bytes 131104 | tf_op jit(solution)/shard_map/all_to_all | solution.py:293
  79.0 25.7 %all-to-all-start.1 = ((f32[8,8,128]{2,1,0:T(8,128)}), f32[8,8,128]{2,1,0:T(8,128)S(1)}, u32[]{:S(2)}, u32[]{:S(2)}) async-start(f32[8,8,128]{2,1,0:T(8,128)} %broadcast_in_dim.13), calls=%async_computation.1 | async-start | bytes 65536 | tf_op jit(solution)/shard_map/all_to_all | solution.py:295
  105.3 8.3 %all-to-all-done.1 = f32[8,8,128]{2,1,0:T(8,128)S(1)} async-done(((f32[8,8,128]{2,1,0:T(8,128)}), f32[8,8,128]{2,1,0:T(8,128)S(1)}, u32[]{:S(2)}, u32[]{:S(2)}) %all-to-all-start.1) | async-done | bytes 32800 | tf_op jit(solution)/shard_map/all_to_all | solution.py:295
  114.3 5.3 %all-to-all-start.2 = ((f32[32,8,128]{2,1,0:T(8,128)}), f32[32,8,128]{2,1,0:T(8,128)S(1)}, u32[]{:S(2)}, u32[]{:S(2)}) async-start(f32[32,8,128]{2,1,0:T(8,128)} %broadcast_in_dim.14), calls=%async_computation.2 | async-start | bytes 262144 | tf_op jit(solution)/shard_map/all_to_all | solution.py:297
  120.4 2.6 %collective-permute-done.14.ye = bf16[12,16,128]{2,1,0:T(8,128)(2,1)S(1)} collective-permute-done((bf16[12,16,128]{2,1,0:T(8,128)(2,1)S(1)}, bf16[12,16,128]{2,1,0:T(8,128)(2,1)S(1)}, u32[]{:S(2)}, u32[]{:S(2)}) %collective-permute-start.14) | collective-permute-done | bytes 49184 | tf_op jit(solution)/shard_map/ppermute | solution.py:285
  123.0 4.8 %shard_map.78 = bf16[10,12,32,128]{3,2,1,0:T(8,128)(2,1)} custom-call(s32[4]{0:T(128)S(1)} %pad_add_fusion.2.pos, bf16[10,12,16,128]{3,2,1,0:T(8,128)(2,1)S(1)} %get-tuple-element.26.own, bf16[12,16,128]{2,1,0:T(8,128)(2,1)S(1)} %collective-permute-done.12.ze, bf16[12,16,128]{2,1,0:T(8,128)(2,1)S(1)} %collective-permute-done.13.zo, ...), custom_call_target="tpu_custom_call" | custom-call | flops 424673280 | bytes 715792 | tf_op jit(solution)/shard_map/pallas_call | solution.py:21
  (60 shorter events, 9.9 us)
Async XLA Ops:
  0.6 29.8 %copy-start.1 = (bf16[32,10,12,128]{3,0,2,1:T(8,128)(2,1)S(1)}, bf16[32,10,12,128]{3,0,2,1:T(8,128)(2,1)}, u32[]{:S(2)}) copy-start(bf16[32,10,12,128]{3,0,2,1:T(8,128)(2,1)} %param.4) | copy-start | bytes 2949124
  0.6 29.7 %copy-start.3 = (f32[16]{0:T(128)S(1)}, f32[16]{0:T(128)}, u32[]{:S(2)}) copy-start(f32[16]{0:T(128)} %param.7) | copy-start | bytes 196
  1.7 16.5 %collective-permute-start = (bf16[12,32,128]{2,1,0:T(8,128)(2,1)S(1)}, bf16[12,32,128]{2,1,0:T(8,128)(2,1)S(1)}, u32[]{:S(2)}, u32[]{:S(2)}) collective-permute-start(bf16[12,32,128]{2,1,0:T(8,128)(2,1)S(1)} %get-tuple-element.37), channel_id=1, source_target_pairs={{0,8},{8,0},{16,24},{24,16},{32,40},{40,32},{48,56},{56,48},{64,72... | collective-permute-start | bytes 294920 | tf_op jit(solution)/shard_map/ppermute | solution.py:329
  5.0 13.2 %collective-permute-start.1 = (bf16[12,32,128]{2,1,0:T(8,128)(2,1)S(1)}, bf16[12,32,128]{2,1,0:T(8,128)(2,1)S(1)}, u32[]{:S(2)}, u32[]{:S(2)}) collective-permute-start(bf16[12,32,128]{2,1,0:T(8,128)(2,1)S(1)} %get-tuple-element.36), channel_id=1, source_target_pairs={{8,16},{24,32},{40,48},{56,64},{72,80},{88,96},{104,112},{120,128}... | collective-permute-start | bytes 294920 | tf_op jit(solution)/shard_map/ppermute | solution.py:332
  7.9 11.1 %collective-permute-start.10 = (s32[10,9,128]{2,1,0:T(8,128)S(1)}, s32[10,9,128]{2,1,0:T(8,128)S(1)}, u32[]{:S(2)}, u32[]{:S(2)}) collective-permute-start(s32[10,9,128]{2,1,0:T(8,128)S(1)} %get-tuple-element.52), channel_id=1, source_target_pairs={{1,2},{3,4},{5,6},{2,1},{4,3},{6,5},{9,10},{11,12},{13,14},{10,9},... | collective-permute-start | bytes 138248 | tf_op jit(solution)/shard_map/ppermute | solution.py:341
  8.6 19.3 %collective-permute-start.11 = (s32[10,9,128]{2,1,0:T(8,128)S(1)}, s32[10,9,128]{2,1,0:T(8,128)S(1)}, u32[]{:S(2)}, u32[]{:S(2)}) collective-permute-start(s32[10,9,128]{2,1,0:T(8,128)S(1)} %get-tuple-element.53), channel_id=1, source_target_pairs={{0,1},{1,0},{2,3},{3,2},{4,5},{5,4},{6,7},{7,6},{8,9},{9,8},{10,11... | collective-permute-start | bytes 138248 | tf_op jit(solution)/shard_map/ppermute | solution.py:341
  12.9 28.2 %collective-permute-start.8 = (s32[9,12,128]{2,1,0:T(8,128)S(1)}, s32[9,12,128]{2,1,0:T(8,128)S(1)}, u32[]{:S(2)}, u32[]{:S(2)}) collective-permute-start(s32[9,12,128]{2,1,0:T(8,128)S(1)} %get-tuple-element.54), channel_id=1, source_target_pairs={{8,16},{24,32},{40,48},{56,64},{72,80},{88,96},{104,112},{120,128}... | collective-permute-start | bytes 165896 | tf_op jit(solution)/shard_map/ppermute | solution.py:341
  17.1 24.7 %copy-start = (s32[10,12,128]{2,1,0:T(8,128)S(1)}, s32[10,12,128]{2,1,0:T(8,128)}, u32[]{:S(2)}) copy-start(s32[10,12,128]{2,1,0:T(8,128)} %lab.3) | copy-start | bytes 184324
  18.2 23.6 %collective-permute-start.9 = (s32[9,12,128]{2,1,0:T(8,128)S(1)}, s32[9,12,128]{2,1,0:T(8,128)S(1)}, u32[]{:S(2)}, u32[]{:S(2)}) collective-permute-start(s32[9,12,128]{2,1,0:T(8,128)S(1)} %get-tuple-element.55), channel_id=1, source_target_pairs={{0,8},{8,0},{16,24},{24,16},{32,40},{40,32},{48,56},{56,48},{64,72... | collective-permute-start | bytes 165896 | tf_op jit(solution)/shard_map/ppermute | solution.py:341
  18.3 9.6 %collective-permute-start.3 = (bf16[12,32,128]{2,1,0:T(8,128)(2,1)S(1)}, bf16[12,32,128]{2,1,0:T(8,128)(2,1)S(1)}, u32[]{:S(2)}, u32[]{:S(2)}) collective-permute-start(bf16[12,32,128]{2,1,0:T(8,128)(2,1)S(1)} %pad_maximum_fusion.1), channel_id=1, source_target_pairs={{1,2},{3,4},{5,6},{2,1},{4,3},{6,5},{9,10},{11,12},{13,14},{10,9},... | collective-permute-start | bytes 294920 | tf_op jit(solution)/shard_map/ppermute | solution.py:286
  19.0 11.3 %collective-permute-start.2 = (bf16[12,32,128]{2,1,0:T(8,128)(2,1)S(1)}, bf16[12,32,128]{2,1,0:T(8,128)(2,1)S(1)}, u32[]{:S(2)}, u32[]{:S(2)}) collective-permute-start(bf16[12,32,128]{2,1,0:T(8,128)(2,1)S(1)} %pad_maximum_fusion), channel_id=1, source_target_pairs={{0,1},{1,0},{2,3},{3,2},{4,5},{5,4},{6,7},{7,6},{8,9},{9,8},{10,11... | collective-permute-start | bytes 294920 | tf_op jit(solution)/shard_map/ppermute | solution.py:285
  34.9 13.0 %collective-permute-start.4 = (bf16[9,12,16,128]{3,2,1,0:T(8,128)(2,1)S(1)}, bf16[9,12,16,128]{3,2,1,0:T(8,128)(2,1)S(1)}, u32[]{:S(2)}, u32[]{:S(2)}) collective-permute-start(bf16[9,12,16,128]{3,2,1,0:T(8,128)(2,1)S(1)} %get-tuple-element.22), channel_id=1, source_target_pairs={{0,8},{8,0},{16,24},{24,16},{32,40},{40,32},{48,56},{56,48},{64,72... | collective-permute-start | bytes 1327112 | tf_op jit(solution)/shard_map/ppermute | solution.py:367
  36.3 11.6 %collective-permute-start.5 = (bf16[9,12,16,128]{3,2,1,0:T(8,128)(2,1)S(1)}, bf16[9,12,16,128]{3,2,1,0:T(8,128)(2,1)S(1)}, u32[]{:S(2)}, u32[]{:S(2)}) collective-permute-start(bf16[9,12,16,128]{3,2,1,0:T(8,128)(2,1)S(1)} %get-tuple-element.23), channel_id=1, source_target_pairs={{8,16},{24,32},{40,48},{56,64},{72,80},{88,96},{104,112},{120,128}... | collective-permute-start | bytes 1327112 | tf_op jit(solution)/shard_map/ppermute | solution.py:366
  39.4 8.5 %collective-permute-start.6 = (bf16[10,9,16,128]{3,2,1,0:T(8,128)(2,1)S(1)}, bf16[10,9,16,128]{3,2,1,0:T(8,128)(2,1)S(1)}, u32[]{:S(2)}, u32[]{:S(2)}) collective-permute-start(bf16[10,9,16,128]{3,2,1,0:T(8,128)(2,1)S(1)} %get-tuple-element.24), channel_id=1, source_target_pairs={{0,1},{1,0},{2,3},{3,2},{4,5},{5,4},{6,7},{7,6},{8,9},{9,8},{10,11... | collective-permute-start | bytes 1105928 | tf_op jit(solution)/shard_map/ppermute | solution.py:365
  41.1 6.8 %collective-permute-start.7 = (bf16[10,9,16,128]{3,2,1,0:T(8,128)(2,1)S(1)}, bf16[10,9,16,128]{3,2,1,0:T(8,128)(2,1)S(1)}, u32[]{:S(2)}, u32[]{:S(2)}) collective-permute-start(bf16[10,9,16,128]{3,2,1,0:T(8,128)(2,1)S(1)} %get-tuple-element.25), channel_id=1, source_target_pairs={{1,2},{3,4},{5,6},{2,1},{4,3},{6,5},{9,10},{11,12},{13,14},{10,9},... | collective-permute-start | bytes 1105928 | tf_op jit(solution)/shard_map/ppermute | solution.py:364
  53.5 16.3 %collective-permute-start.12 = (bf16[12,16,128]{2,1,0:T(8,128)(2,1)S(1)}, bf16[12,16,128]{2,1,0:T(8,128)(2,1)S(1)}, u32[]{:S(2)}, u32[]{:S(2)}) collective-permute-start(bf16[12,16,128]{2,1,0:T(8,128)(2,1)S(1)} %get-tuple-element.27), channel_id=1, source_target_pairs={{0,8},{8,0},{16,24},{24,16},{32,40},{40,32},{48,56},{56,48},{64,72... | collective-permute-start | bytes 147464 | tf_op jit(solution)/shard_map/ppermute | solution.py:400
  53.6 16.2 %collective-permute-start.13 = (bf16[12,16,128]{2,1,0:T(8,128)(2,1)S(1)}, bf16[12,16,128]{2,1,0:T(8,128)(2,1)S(1)}, u32[]{:S(2)}, u32[]{:S(2)}) collective-permute-start(bf16[12,16,128]{2,1,0:T(8,128)(2,1)S(1)} %get-tuple-element.28), channel_id=1, source_target_pairs={{8,16},{24,32},{40,48},{56,64},{72,80},{88,96},{104,112},{120,128}... | collective-permute-start | bytes 147464 | tf_op jit(solution)/shard_map/ppermute | solution.py:401
  59.1 61.0 %copy-start.2 = (bf16[16,32,3,3,3]{1,0,4,3,2:T(8,128)(2,1)S(1)}, bf16[16,32,3,3,3]{1,0,4,3,2:T(8,128)(2,1)}, u32[]{:S(2)}) copy-start(bf16[16,32,3,3,3]{1,0,4,3,2:T(8,128)(2,1)} %param.6) | copy-start | bytes 82948
  62.9 15.4 %all-to-all-start = ((f32[32,8,128]{2,1,0:T(8,128)}), f32[32,8,128]{2,1,0:T(8,128)S(1)}, u32[]{:S(2)}, u32[]{:S(2)}) async-start(f32[32,8,128]{2,1,0:T(8,128)} %bitcast.23), calls=%async_computation | async-start | bytes 262144 | tf_op jit(solution)/shard_map/all_to_all | solution.py:293
  79.0 34.7 %all-to-all-start.1 = ((f32[8,8,128]{2,1,0:T(8,128)}), f32[8,8,128]{2,1,0:T(8,128)S(1)}, u32[]{:S(2)}, u32[]{:S(2)}) async-start(f32[8,8,128]{2,1,0:T(8,128)} %broadcast_in_dim.13), calls=%async_computation.1 | async-start | bytes 65536 | tf_op jit(solution)/shard_map/all_to_all | solution.py:295
  104.6 15.7 %collective-permute-start.15 = (bf16[12,16,128]{2,1,0:T(8,128)(2,1)S(1)}, bf16[12,16,128]{2,1,0:T(8,128)(2,1)S(1)}, u32[]{:S(2)}, u32[]{:S(2)}) collective-permute-start(bf16[12,16,128]{2,1,0:T(8,128)(2,1)S(1)} %pad_maximum_fusion.3), channel_id=1, source_target_pairs={{1,2},{3,4},{5,6},{2,1},{4,3},{6,5},{9,10},{11,12},{13,14},{10,9},... | collective-permute-start | bytes 147464 | tf_op jit(solution)/shard_map/ppermute | solution.py:286
  114.3 14.0 %all-to-all-start.2 = ((f32[32,8,128]{2,1,0:T(8,128)}), f32[32,8,128]{2,1,0:T(8,128)S(1)}, u32[]{:S(2)}, u32[]{:S(2)}) async-start(f32[32,8,128]{2,1,0:T(8,128)} %broadcast_in_dim.14), calls=%async_computation.2 | async-start | bytes 262144 | tf_op jit(solution)/shard_map/all_to_all | solution.py:297
  119.7 3.3 %collective-permute-start.14 = (bf16[12,16,128]{2,1,0:T(8,128)(2,1)S(1)}, bf16[12,16,128]{2,1,0:T(8,128)(2,1)S(1)}, u32[]{:S(2)}, u32[]{:S(2)}) collective-permute-start(bf16[12,16,128]{2,1,0:T(8,128)(2,1)S(1)} %pad_maximum_fusion.2), channel_id=1, source_target_pairs={{0,1},{1,0},{2,3},{3,2},{4,5},{5,4},{6,7},{7,6},{8,9},{9,8},{10,11... | collective-permute-start | bytes 147464 | tf_op jit(solution)/shard_map/ppermute | solution.py:285
where the time goes:
time: 131 us; the launch traced here: 130 us
  starting transfers between devices  73.1 us (56%)
  Pallas kernels  25.3 us (19%)
  waiting for transfers between devices  22.6 us (17%)
  local copies, waits for them, and re-layouts  7.88 us (6%)
    all_to_all x1, starting transfers between devices, total_of(): mine = lax.all_to_all(jnp.broadcast_to(mine, (gy, rows, lanes)), 'gy', 0, 0)  25.7 us
    pallas_call x6, Pallas kernels, call(): pl.pallas_call(body, out_shape=outs, in_specs=specs, out_specs=jax.tree.m...  25.3 us
    ppermute x2, starting transfers between devices, swap_y(): lax.ppermute(even, 'gy', even_pairs(gy))  9.27 us
    all_to_all x1, waiting for transfers between devices, total_of(): mine = lax.all_to_all(value.reshape(gz, rows, lanes), 'gz', 0, 0)  8.47 us
    all_to_all x1, waiting for transfers between devices, total_of(): mine = lax.all_to_all(jnp.broadcast_to(mine, (gy, rows, lanes)), 'gy', 0, 0)  8.33 us
    ppermute x4, starting transfers between devices, label_halo(): e, o = (lax.ppermute(e, axis, even), lax.ppermute(o, axis, odd))  7.09 us
    all_to_all x1, starting transfers between devices, total_of(): mine = lax.all_to_all(value.reshape(gz, rows, lanes), 'gz', 0, 0)  6.83 us
    ppermute x1, starting transfers between devices, per_device(): gzo = lax.ppermute(go, 'gz', zo_pairs)  5.44 us
  transfers between devices with their start and end apart: 19, of which 6 were waited for; matrix products, arithmetic and copies ran while one was open for 4% of the time, Pallas kernels for 15%

commit v1 on v0

v1 whole, which is shorter than its diff:
```python
import functools

import jax
import jax.numpy as jnp
from jax import lax
from jax.experimental import pallas as pl
from jax.experimental.pallas import tpu as pltpu
from jax.sharding import PartitionSpec as P

OFFSETS = (1, 3, 9)
REACH = 9
BF = jnp.bfloat16
F32 = jnp.float32
PEAK = 1.15e9
PARAMS = pltpu.CompilerParams(vmem_limit_bytes=48 * 1024 * 1024)
VM = pl.BlockSpec(memory_space=pltpu.VMEM)
HELD = pl.BlockSpec(memory_space=pl.ANY)
SM = pl.BlockSpec(memory_space=pltpu.SMEM)


def call(body, outs, args, specs, scratch=(), micros=1.0, aliases={}):
    return pl.pallas_call(
        body,
        out_shape=outs,
        in_specs=specs,
        out_specs=jax.tree.map(lambda _: VM, outs),
        scratch_shapes=list(scratch),
        input_output_aliases=aliases,
        compiler_params=PARAMS,
        cost_estimate=pl.CostEstimate(
            flops=int(micros * PEAK), bytes_accessed=1, transcendentals=0
        ),
    )(*args)


def even_pairs(count):
    return [(i, i ^ 1) for i in range(count - count % 2)]


def odd_pairs(count):
    pairs = [(i, i + 1) for i in range(1, count - 1, 2)]
    return pairs + [(j, i) for i, j in pairs]


def lane_shift(value, step):
    lanes = value.shape[-1]
    moved = pltpu.roll(value, (-step) % lanes, value.ndim - 1)
    lane = lax.broadcasted_iota(jnp.int32, value.shape, value.ndim - 1)
    keep = (lane < lanes - step) if step > 0 else (lane >= -step)
    return jnp.where(keep, moved, 0)


def pair_terms(logits, same):
    target = same.astype(F32)
    small = jnp.exp(-jnp.abs(logits))
    inverse = 1.0 / (1.0 + small)
    sigmoid = jnp.where(logits >= 0, inverse, small * inverse)
    slopes = (sigmoid - target) * 0.25
    losses = jnp.maximum(logits, 0.0) + jnp.log(1.0 + small) - target * logits
    return slopes, losses


def dots(left, right):
    return jnp.sum(left * right, axis=1) * 0.25


def fill_rim(ext, ye, yo, ze, zo, pz, py, planes, rows):
    ext[1 : planes + 1, (1 - py) * (rows + 1)] = ye[...]
    ext[1 : planes + 1, py * (rows + 1)] = yo[...]
    ext[(1 - pz) * (planes + 1)] = ze[: rows + 2]
    ext[pz * (planes + 1)] = zo[: rows + 2]


def conv_rows(ext, w_ref, z, rows):
    stack = [
        jnp.concatenate([ext[z + a, y + b] for y in rows], axis=1)
        for a in range(3)
        for b in range(3)
    ]
    sums = jnp.dot(w_ref[...], jnp.concatenate(stack, axis=0), preferred_element_type=F32)
    third = sums.shape[0] // 3
    lanes = sums.shape[1] // len(rows)
    for i, y in enumerate(rows):
        part = sums[:, i * lanes : (i + 1) * lanes]
        yield (
            y,
            lane_shift(part[:third], -1)
            + part[third : 2 * third]
            + lane_shift(part[2 * third :], 1),
        )


def pack_labels(wide, blocks):
    at = 0
    for block in blocks:
        count = block.shape[0]
        wide[at : at + count] = lax.shift_right_logical(block, 8).astype(F32)
        wide[at + count : at + 2 * count] = jnp.bitwise_and(block, 255).astype(F32)
        at += 2 * count
    if at < wide.shape[0]:
        wide[at:] = jnp.zeros((wide.shape[0] - at, wide.shape[1]), F32)


def first_kernel(pos, feat, even, odd, sems):
    py, rows = pos[1], feat.shape[1]
    copies = [
        pltpu.make_async_copy(feat.at[:, (1 - py) * (rows - 1)], even, sems.at[0]),
        pltpu.make_async_copy(feat.at[:, py * (rows - 1)], odd, sems.at[1]),
    ]
    for copy in copies:
        copy.start()
    for copy in copies:
        copy.wait()


def second_kernel(pos, feat, lab, w, bias, emb, ext, even, odd, wide):
    planes, rows = feat.shape[0], feat.shape[1]
    py = pos[1]
    cells = (planes - 2) * (REACH - 1)
    ext[1 : planes + 1, 1 : rows + 1] = feat[...]
    for out, high in ((even, 1 - py), (odd, py)):
        pack_labels(
            wide,
            [
                jnp.where(high == 1, lab[z, rows - REACH :], lab[z, :REACH])
                for z in range(planes)
            ],
        )
        out[cells:] = wide[...].astype(BF).reshape(out.shape[0] - cells, *out.shape[1:])

    @pl.loop(0, planes - 2)
    def _(z):
        for y in range(0, rows - 2, 2):
            for i, value in conv_rows(feat, w, z, (y, y + 1)):
                emb[z + 1, i + 1] = (value + bias[...]).astype(BF)

    for out, high in ((even, 1 - py), (odd, py)):
        part = emb[1 : planes - 1, pl.ds(1 + high * (rows - 1 - REACH), REACH - 1)]
        out[:cells] = part.reshape(cells, *part.shape[2:])


def edge_planes(pos, own, ye, yo, even, odd):
    planes, rows = own.shape[0], own.shape[1]
    pz, py = pos[0], pos[1]
    for out, high in ((even, 1 - pz), (odd, pz)):
        plane = high * (planes - 1)
        out[1 : rows + 1] = own[plane]
        out[(1 - py) * (rows + 1)] = ye[plane]
        out[py * (rows + 1)] = yo[plane]


def third_kernel(pos, feat, ye, yo, lab, after, even, odd, wide):
    planes, rows = feat.shape[0], feat.shape[1]
    pz = pos[0]
    edge_planes(pos, feat, ye, yo, even, odd)
    for out, high in ((even, 1 - pz), (odd, pz)):
        base = high * (planes - REACH)
        pack_labels(wide, [lab[base + p] for p in range(REACH)])
        labels = wide[...].astype(BF)
        out[rows + 2 :] = labels.reshape(out.shape[0] - rows - 2, *out.shape[1:])


def forward_kernel(
    pos, part, ext_in, ye, yo, ze, zo, w, bias, emb, ext, se, so, te, to
):
    planes, rows = emb.shape[0], emb.shape[1]
    pz, py = pos[0], pos[1]
    fill_rim(ext, ye, yo, ze, zo, pz, py, planes, rows)

    @pl.loop(0, planes)
    def _(z):
        for i, value in conv_rows(ext, w, z, (0, rows - 1)):
            emb[z, i] = (value + bias[...]).astype(BF)

    @pl.loop(0, 2)
    def _(side):
        z = side * (planes - 1)
        for y in range(1, rows - 1, 2):
            for i, value in conv_rows(ext, w, z, (y, y + 1)):
                emb[z, i] = (value + bias[...]).astype(BF)

    for out, high in ((se, 1 - pz), (so, pz)):
        out[...] = emb[pl.ds(high * (planes - REACH), REACH)]
    for out, high in ((te, 1 - py), (to, py)):
        part = pl.ds(high * (rows - REACH), REACH)
        out[:REACH] = emb[0, part]
        out[REACH : 2 * REACH] = emb[planes - 1, part]
        out[2 * REACH :] = emb[1 : planes - 1, high * (rows - 1)]


def inner_kernel(pos, emb, lab, ze, zo, grad, loss, labz, widez):
    planes, rows = emb.shape[0], emb.shape[1]
    lanes = emb.shape[3]
    pz = pos[0]
    for halo, side in ((ze, 1 - pz), (zo, pz)):
        widez[...] = halo[rows + 2 :].reshape(widez.shape).astype(F32)
        for p in range(REACH):
            at = 2 * rows * p
            labz[side, p] = widez[at : at + rows] * 256.0 + widez[at + rows : at + 2 * rows]

    lane = lax.broadcasted_iota(jnp.int32, (rows, lanes), 1)
    loss[...] = jnp.zeros_like(loss)

    @pl.loop(0, planes)
    def _(z):
        center = emb[z].astype(F32)
        here = lab[z]
        total = jnp.zeros(center.shape, F32)
        lost = jnp.zeros((rows, lanes), F32)
        for o in OFFSETS:
            if o < lanes:
                after = pltpu.roll(center, lanes - o, 2)
                before = pltpu.roll(center, o, 2)
                live = lane < lanes - o
                slopes, losses = pair_terms(
                    dots(center, after), here == pltpu.roll(here, lanes - o, 1)
                )
                slopes = jnp.where(live, slopes, 0.0)
                lost = lost + jnp.where(live, losses, 0.0)
                total = total + slopes[:, None, :] * after
                total = total + pltpu.roll(slopes, o, 1)[:, None, :] * before
        grad[z] = total
        for o in OFFSETS:
            if o < rows:
                low, high = center[: rows - o], center[o:]
                slopes, losses = pair_terms(dots(low, high), here[: rows - o] == here[o:])
                grad[z, : rows - o] += slopes[:, None, :] * high
                grad[z, o:] += slopes[:, None, :] * low
                loss[: rows - o] += losses
        loss[:rows] += lost

    for o in OFFSETS:

        @pl.loop(0, planes - o)
        def _(z):
            low, high = emb[z].astype(F32), emb[z + o].astype(F32)
            slopes, losses = pair_terms(dots(low, high), lab[z] == lab[z + o])
            grad[z] += slopes[:, None, :] * high
            grad[z + o] += slopes[:, None, :] * low
            loss[:rows] += losses


def outer_kernel(
    pos,
    emb,
    lab,
    grad_in,
    loss_in,
    ze,
    zo,
    labz,
    fe,
    fo,
    ye,
    yo,
    out,
    shifted,
    ge,
    go,
    sums,
    grad,
    total,
    laby,
    wide,
    halos,
):
    planes, rows = emb.shape[0], emb.shape[1]
    pz, py = pos[0], pos[1]
    third = emb.shape[2]
    cells = (planes - 2) * (REACH - 1)
    grad[...] = grad_in[...]
    total[...] = loss_in[...]
    for halo, side in ((fe, 1 - py), (fo, py)):
        wide[...] = halo[cells:].reshape(wide.shape).astype(F32)
        for z in range(planes):
            at = 2 * REACH * z
            laby[side, z] = wide[at : at + REACH] * 256.0 + wide[at + REACH : at + 2 * REACH]

    for halo, is_high in ((ze, 1 - pz), (zo, pz)):
        weight = (is_high * pos[2]).astype(F32)
        for o in OFFSETS:

            @pl.loop(0, o)
            def _(t):
                p = t + is_high * (planes - o)
                q = t + (1 - is_high) * (REACH - o)
                other = halo[q].astype(F32)
                slopes, losses = pair_terms(
                    dots(emb[p].astype(F32), other),
                    lab[p].astype(F32) == labz[is_high, q],
                )
                grad[p] += slopes[:, None, :] * other
                total[:rows] += losses * weight

    shifted[:, :2] = jnp.zeros((planes, 2) + shifted.shape[2:], BF)
    shifted[:, rows + 2 :] = jnp.zeros((planes, 2) + shifted.shape[2:], BF)
    for early, late, is_high in ((fe, ye, 1 - py), (fo, yo, py)):
        halos[is_high, 0] = late[:REACH]
        halos[is_high, planes - 1] = late[REACH : 2 * REACH]
        halos[is_high, 1 : planes - 1, (1 - is_high) * (REACH - 1)] = late[2 * REACH :]
        part = early[: (planes - 2) * (REACH - 1)]
        halos[is_high, 1 : planes - 1, pl.ds(is_high, REACH - 1)] = part.reshape(
            planes - 2, REACH - 1, *part.shape[1:]
        )
    live = pos[3].astype(F32)

    @pl.loop(0, planes)
    def _(z):
        center = emb[z].astype(F32)
        here = lab[z].astype(F32)
        sum_z = grad[z]
        low = halos[0, z].astype(F32)
        high = halos[1, z].astype(F32)
        lower, upper = [], []
        for o in OFFSETS:
            lower.append((center[:o], low[REACH - o :], here[:o], laby[0, z, REACH - o :]))
            upper.append((center[rows - o :], high[:o], here[rows - o :], laby[1, z, :o]))
        logits = [dots(a, b) for a, b, _, _ in lower + upper]
        mine = jnp.concatenate([c for _, _, c, _ in lower + upper], axis=0)
        theirs = jnp.concatenate([d for _, _, _, d in lower + upper], axis=0)
        slopes, losses = pair_terms(jnp.concatenate(logits, axis=0), mine == theirs)
        half = sum(OFFSETS)
        total[:1] += jnp.sum(losses[half:], axis=0, keepdims=True) * live
        at = 0
        for o, (_, other, _, _) in zip(OFFSETS, lower):
            sum_z = jnp.concatenate(
                [sum_z[:o] + slopes[at : at + o, None, :] * other, sum_z[o:]], axis=0
            )
            at += o
        for o, (_, other, _, _) in zip(OFFSETS, upper):
            sum_z = jnp.concatenate(
                [
                    sum_z[: rows - o],
                    sum_z[rows - o :] + slopes[at : at + o, None, :] * other,
                ],
                axis=0,
            )
            at += o
        value = sum_z.astype(BF)
        out[z] = value
        wide = value.astype(F32)
        shifted[z, 2 : rows + 2, :third] = lane_shift(wide, 1).astype(BF)
        shifted[z, 2 : rows + 2, third : 2 * third] = value
        shifted[z, 2 : rows + 2, 2 * third :] = lane_shift(wide, -1).astype(BF)

    ge[...] = out[:, (1 - py) * (rows - 1)]
    go[...] = out[:, py * (rows - 1)]
    sums[...] = jnp.broadcast_to(jnp.sum(total[...], keepdims=True), sums.shape)


def weight_kernel(shifted, ext, own, lost, out, acc):
    planes, rows = own.shape[0], own.shape[1]
    channels, lanes = own.shape[2], own.shape[3]
    acc[...] = jnp.zeros_like(acc)

    @pl.loop(0, planes)
    def _(z):
        total = acc[...]
        for y in range(0, rows + 2, 2):
            left = jnp.concatenate(
                [
                    jnp.concatenate([shifted[z, y + i + 2 - b] for b in range(3)], axis=0)
                    for i in range(2)
                ],
                axis=1,
            )
            right = jnp.concatenate(
                [
                    jnp.concatenate([ext[z + a, y + i] for a in range(3)], axis=0)
                    for i in range(2)
                ],
                axis=1,
            )
            total = total + lax.dot_general(
                left, right, (((1,), (1,)), ((), ())), preferred_element_type=F32
            )
        acc[...] = total

    height, width = acc.shape
    out[...] = jnp.zeros_like(out)
    out[:height, :width] = acc[...]
    tile = jnp.sum(own[...].astype(F32), axis=(0, 1))
    column = jnp.sum(tile, axis=1, keepdims=True)
    row = lax.broadcasted_iota(jnp.int32, (channels, lanes), 0)
    lane = lax.broadcasted_iota(jnp.int32, (channels, lanes), 1)
    line = jnp.sum(jnp.where(row == lane, column, 0.0), axis=0, keepdims=True)
    first = lax.broadcasted_iota(jnp.int32, (1, lanes), 1)
    out[height : height + 1, :] = jnp.where(first == channels, lost[0:1, :], line)


def backward_kernel(pos, own, ye, yo, ze, zo, w, after, out, ext):
    planes, rows = own.shape[0], own.shape[1]
    ext[1 : planes + 1, 1 : rows + 1] = own[...]
    fill_rim(ext, ye, yo, ze, zo, pos[0], pos[1], planes, rows)

    @pl.loop(0, planes)
    def _(z):
        for y in range(0, rows, 2):
            for i, value in conv_rows(ext, w, z, (y, y + 1)):
                out[z, i] = value.astype(BF)


def spread_kernel(parts, out):
    out[...] = jnp.broadcast_to(jnp.sum(parts[...], axis=0), out.shape)


def final_kernel(voxels, pair_count, total, out, bias, loss):
    groups, channels, width = out.shape
    per = groups // 3
    height = per * channels
    for a in range(3):
        part = total[:height, a * width : (a + 1) * width] * (1.0 / voxels)
        out[a * per : (a + 1) * per] = part.reshape(per, channels, width)
    bias[...] = total[height : height + 1, :channels] * (1.0 / voxels)
    loss[...] = total[height : height + 1, channels : channels + 1] * (1.0 / pair_count)


def per_device(features, labels, weight, conv_bias):
    ch_in, planes, rows, lanes = features.shape
    emb_ch = weight.shape[0]
    gz, gy = lax.axis_size("gz"), lax.axis_size("gy")
    depth, height = planes * gz, rows * gy
    voxels = depth * height * lanes
    pair_count = sum(
        (extent - o) * (voxels // extent)
        for extent in (depth, height, lanes)
        for o in OFFSETS
        if o < extent
    )
    iz, iy = lax.axis_index("gz"), lax.axis_index("gy")
    pos = jnp.stack(
        [
            lax.rem(iz, 2),
            lax.rem(iy, 2),
            (iz < gz - 1).astype(jnp.int32),
            (iy < gy - 1).astype(jnp.int32),
        ]
    ).astype(jnp.int32)
    z_even, z_odd = even_pairs(gz), odd_pairs(gz)
    y_even, y_odd = even_pairs(gy), odd_pairs(gy)

    feat = jnp.transpose(features, (1, 2, 0, 3))
    taps = jnp.transpose(weight, (2, 3, 4, 0, 1))
    w_fwd = jnp.transpose(taps, (2, 3, 0, 1, 4)).reshape(3 * emb_ch, 9 * ch_in)
    w_bwd = jnp.transpose(taps[::-1, ::-1, ::-1], (2, 4, 0, 1, 3)).reshape(
        3 * ch_in, 9 * emb_ch
    )
    bias = jnp.broadcast_to(conv_bias[:, None], (emb_ch, lanes))

    sds = jax.ShapeDtypeStruct
    tile = (emb_ch, lanes)
    cells = (ch_in, lanes)
    z_blocks = -(-2 * REACH * rows // ch_in)
    y_blocks = -(-2 * REACH * planes // ch_in)

    y_message = sds((planes,) + cells, BF)
    me, mo = call(
        first_kernel, (y_message, y_message), (pos, feat), [SM, HELD],
        scratch=[pltpu.SemaphoreType.DMA((2,))],
    )
    fye = lax.ppermute(me, "gy", y_even)
    fyo = lax.ppermute(mo, "gy", y_odd)
    emb_shape = sds((planes, rows) + tile, BF)
    ext_shape = sds((planes + 2, rows + 2) + cells, BF)
    y_early = sds(
        ((planes - 2) * (REACH - 1) + y_blocks * (ch_in // emb_ch),) + tile, BF
    )
    emb_part, ext_part, me, mo = call(
        second_kernel,
        (emb_shape, ext_shape, y_early, y_early),
        (pos, feat, labels, w_fwd, bias),
        [SM] + [VM] * 4,
        scratch=[pltpu.VMEM((y_blocks * ch_in, lanes), F32)],
        micros=3.4,
    )
    aye = lax.ppermute(me, "gy", y_even)
    ayo = lax.ppermute(mo, "gy", y_odd)
    z_message = sds((rows + 2 + z_blocks,) + cells, BF)
    me, mo = call(
        third_kernel,
        (z_message, z_message),
        (pos, feat, fye, fyo, labels, me),
        [SM] + [VM] * 4 + [HELD],
        scratch=[pltpu.VMEM((z_blocks * ch_in, lanes), F32)],
    )
    fze = lax.ppermute(me, "gz", z_even)
    fzo = lax.ppermute(mo, "gz", z_odd)

    z_halo = sds((REACH, rows) + tile, BF)
    y_late = sds((2 * REACH + planes - 2,) + tile, BF)
    emb, feat_ext, se, so, te, to = call(
        forward_kernel,
        (emb_shape, ext_shape, z_halo, z_halo, y_late, y_late),
        (pos, emb_part, ext_part, fye, fyo, fze, fzo, w_fwd, bias),
        [SM] + [VM] * 8,
        micros=3.6,
        aliases={1: 0, 2: 1},
    )
    eze = lax.ppermute(se, "gz", z_even)
    ezo = lax.ppermute(so, "gz", z_odd)
    eye = lax.ppermute(te, "gy", y_even)
    eyo = lax.ppermute(to, "gy", y_odd)

    lost_rows = -(-rows // 8) * 8
    grad_shape = sds((planes, rows) + tile, F32)
    loss_shape = sds((lost_rows, lanes), F32)
    grad_a, loss_a, labz = call(
        inner_kernel,
        (
            grad_shape,
            loss_shape,
            sds((2, REACH, rows, lanes), F32),
        ),
        (pos, emb, labels, fze, fzo),
        [SM] + [VM] * 4,
        scratch=[pltpu.VMEM((z_blocks * ch_in, lanes), F32)],
        micros=6.4,
    )
    grad, shifted, ge, go, lost = call(
        outer_kernel,
        (
            sds((planes, rows) + tile, BF),
            sds((planes, rows + 4, 3 * emb_ch, lanes), BF),
            sds((planes,) + tile, BF),
            sds((planes,) + tile, BF),
            sds((8, lanes), F32),
        ),
        (pos, emb, labels, grad_a, loss_a, eze, ezo, labz, aye, ayo, eye, eyo),
        [SM] + [VM] * 11,
        scratch=[
            pltpu.VMEM((planes, rows) + tile, F32),
            pltpu.VMEM((lost_rows, lanes), F32),
            pltpu.VMEM((2, planes, REACH, lanes), F32),
            pltpu.VMEM((y_blocks * ch_in, lanes), F32),
            pltpu.VMEM((2, planes, REACH) + tile, BF),
        ],
        micros=5.0,
    )
    gye = lax.ppermute(ge, "gy", y_even)
    gyo = lax.ppermute(go, "gy", y_odd)

    used = 9 * emb_ch + 1
    padded = -(-used // (8 * gz)) * 8 * gz
    share = padded // gz
    partial = call(
        weight_kernel,
        sds((padded, lanes), F32),
        (shifted, feat_ext, grad, lost),
        [VM] * 4,
        scratch=[pltpu.VMEM((9 * emb_ch, 3 * ch_in), F32)],
        micros=3.8,
    )
    z_edge = sds((rows + 2,) + tile, BF)
    me, mo = call(edge_planes, (z_edge, z_edge), (pos, grad, gye, gyo), [SM] + [VM] * 3)
    gze = lax.ppermute(me, "gz", z_even)
    gzo = lax.ppermute(mo, "gz", z_odd)

    parts = lax.all_to_all(partial.reshape(gz, share, lanes), "gz", 0, 0)
    mine = call(spread_kernel, sds((gy, share, lanes), F32), (parts,), [VM])
    feature_grad = call(
        backward_kernel,
        sds((planes, rows) + cells, BF),
        (pos, grad, gye, gyo, gze, gzo, w_bwd, mine),
        [SM] + [VM] * 6 + [HELD],
        scratch=[pltpu.VMEM((planes + 2, rows + 2) + tile, BF)],
        micros=4.9,
    )
    parts = lax.all_to_all(mine, "gy", 0, 0)
    mine = call(spread_kernel, sds((gz, share, lanes), F32), (parts,), [VM])
    total = lax.all_to_all(mine, "gz", 0, 0).reshape(padded, lanes)

    weight_grad, bias_grad, loss = call(
        functools.partial(final_kernel, voxels, pair_count),
        (sds((27, emb_ch, ch_in), F32), sds((1, emb_ch), F32), sds((1, 1), F32)),
        (total,),
        [VM],
    )
    weight_grad = jnp.transpose(
        weight_grad.reshape(3, 3, 3, emb_ch, ch_in), (3, 4, 0, 1, 2)
    )
    return (
        jnp.transpose(feature_grad, (2, 0, 1, 3)),
        weight_grad,
        bias_grad.reshape(emb_ch),
        loss.reshape(()),
    )


def solution(mesh):
    return jax.shard_map(
        per_device,
        mesh=mesh,
        in_specs=(P(None, "gz", "gy", None), P("gz", "gy", None), P(), P()),
        out_specs=(P(None, "gz", "gy", None), P(), P(), P()),
        check_vma=False,
    )
```

time: 131 us -> 112 us (0.85)
  waiting for transfers between devices: 22.6 us -> 9.32 us
  local copies, waits for them, and re-layouts: 7.88 us -> 1.77 us
  Pallas kernels: 25.3 us -> 30.5 us
  starting transfers between devices: 73.1 us -> 69 us
    all_to_all x3, waiting for transfers between devices: 17.3 us -> 9.29 us  [the longest x1 5.57 us: per_device(): parts = lax.all_to_all(mine, 'gy', 0, 0)]
    ppermute x16 -> x14, waiting for transfers between devices: 5.28 us -> 0.04 us  [the longest x1 0.01 us: per_device(): fye = lax.ppermute(me, 'gy', y_even)]
    pallas_call x6 -> x12, Pallas kernels: 25.3 us -> 30.5 us  [call(): pl.pallas_call(body, out_shape=outs, in_specs=specs, out_specs=jax.tree.m...]
    all_to_all x3, starting transfers between devices: 37.8 us -> 33 us  [the longest x1 18.3 us: per_device(): parts = lax.all_to_all(mine, 'gy', 0, 0)]
    squeeze x4 -> x0, local copies, waits for them, and re-layouts: 2.55 us -> none  [the longest x1 1.04 us: per_device(): lax.dynamic_index_in_dim(feat, pz * (planes - 1), 0, keepdims=False)]
    dynamic_slice x5 -> x0, local copies, waits for them, and re-layouts: 1.99 us -> none  [the longest x2 1.95 us: label_halo(): o = lax.dynamic_slice_in_dim(labels, parity * room, REACH, dim)]
    ppermute x16 -> x14, starting transfers between devices: 35.3 us -> 36 us  [the longest x1 9.18 us: per_device(): eye = lax.ppermute(te, 'gy', y_even)]
  transfers between devices with their start and end apart: 19 -> 17, of which waited for: 6 -> 2; matrix products, arithmetic and copies ran while one was open for 4% -> 0% of each run, Pallas kernels for 15% -> 18%
where the time goes in v1:
time: 112 us
  starting transfers between devices  69 us (62%)
  Pallas kernels  30.5 us (27%)
  waiting for transfers between devices  9.32 us (8%)
  local copies, waits for them, and re-layouts  1.77 us (2%)
    pallas_call x12, Pallas kernels, call(): pl.pallas_call(body, out_shape=outs, in_specs=specs, out_specs=jax.tree.m...  30.5 us
    all_to_all x1, starting transfers between devices, per_device(): parts = lax.all_to_all(mine, 'gy', 0, 0)  18.3 us
    ppermute x1, starting transfers between devices, per_device(): eye = lax.ppermute(te, 'gy', y_even)  9.18 us
    all_to_all x1, starting transfers between devices, per_device(): parts = lax.all_to_all(partial.reshape(gz, share, lanes), 'gz', 0, 0)  8.28 us
    ppermute x1, starting transfers between devices, per_device(): gye = lax.ppermute(ge, 'gy', y_even)  7.57 us
    all_to_all x1, starting transfers between devices, per_device(): total = lax.all_to_all(mine, 'gz', 0, 0).reshape(padded, lanes)  6.46 us
    all_to_all x1, waiting for transfers between devices, per_device(): parts = lax.all_to_all(mine, 'gy', 0, 0)  5.57 us
    ppermute x1, starting transfers between devices, per_device(): aye = lax.ppermute(me, 'gy', y_even)  3.91 us
  transfers between devices with their start and end apart: 17, of which 2 were waited for; matrix products, arithmetic and copies ran while one was open for 0% of the time, Pallas kernels for 18%

profile of v1, /device:TPU:1, one launch (start us, length us, event | category | flops | bytes accessed | tf_op | source)
XLA Modules:
  0.0 111.6 jit_solution(13000614334504869386)
XLA Ops:
  0.7 1.2 %copy-done = bf16[32,10,12,128]{3,0,2,1:T(8,128)(2,1)S(1)} copy-done((bf16[32,10,12,128]{3,0,2,1:T(8,128)(2,1)S(1)}, bf16[32,10,12,128]{3,0,2,1:T(8,128)(2,1)}, u32[]{:S(2)}) %copy-start) | copy-done | bytes 983064
  2.5 2.2 %collective-permute-start = (bf16[10,32,128]{2,1,0:T(8,128)(2,1)S(1)}, bf16[10,32,128]{2,1,0:T(8,128)(2,1)S(1)}, u32[]{:S(2)}, u32[]{:S(2)}) collective-permute-start(bf16[10,32,128]{2,1,0:T(8,128)(2,1)S(1)} %get-tuple-element.33), channel_id=1, source_target_pairs={{0,1},{1,0},{2,3},{3,2},{4,5},{5,4},{6,7},{7,6},{8,9},{9,8},{10,11... | collective-permute-start | bytes 245768 | tf_op jit(solution)/shard_map/ppermute | solution.py:461
  5.7 3.3 %shard_map.75 = (bf16[10,12,16,128]{3,2,1,0:T(8,128)(2,1)S(1)}, bf16[12,14,32,128]{3,2,1,0:T(8,128)(2,1)S(1)}, bf16[76,16,128]{2,1,0:T(8,128)(2,1)S(1)}, bf16[76,16,128]{2,1,0:T(8,128)(2,1)S(1)}) custom-call(s32[4]{0:T(128)S(1)} %pad_add_fusion.pos, bf16[10,12,32,128]{3,2,1,0:T(8,128)(2,1)S(1)} %bitcast.21, s32[10,12,128]{2,1,0:T(8,128)S(1)} %copy-done.2, ...), custom_call_target="tpu_custom_call" | custom-call | flops 3910000128 | bytes 1 | tf_op jit(solution)/shard_map/pallas_call | solution.py:22
  9.6 1.3 %collective-permute-start.2 = (bf16[21,32,128]{2,1,0:T(8,128)(2,1)S(1)}, bf16[21,32,128]{2,1,0:T(8,128)(2,1)S(1)}, u32[]{:S(2)}, u32[]{:S(2)}) collective-permute-start(bf16[21,32,128]{2,1,0:T(8,128)(2,1)S(1)} %get-tuple-element.36), channel_id=1, source_target_pairs={{0,8},{8,0},{16,24},{24,16},{32,40},{40,32},{48,56},{56,48},{64,72... | collective-permute-start | bytes 516104 | tf_op jit(solution)/shard_map/ppermute | solution.py:486
  11.0 2.7 %collective-permute-start.3 = (bf16[21,32,128]{2,1,0:T(8,128)(2,1)S(1)}, bf16[21,32,128]{2,1,0:T(8,128)(2,1)S(1)}, u32[]{:S(2)}, u32[]{:S(2)}) collective-permute-start(bf16[21,32,128]{2,1,0:T(8,128)(2,1)S(1)} %get-tuple-element.37), channel_id=1, source_target_pairs={{8,16},{24,32},{40,48},{56,64},{72,80},{88,96},{104,112},{120,128}... | collective-permute-start | bytes 516104 | tf_op jit(solution)/shard_map/ppermute | solution.py:487
  13.7 3.9 %collective-permute-start.6 = (bf16[76,16,128]{2,1,0:T(8,128)(2,1)S(1)}, bf16[76,16,128]{2,1,0:T(8,128)(2,1)S(1)}, u32[]{:S(2)}, u32[]{:S(2)}) collective-permute-start(bf16[76,16,128]{2,1,0:T(8,128)(2,1)S(1)} %get-tuple-element.35.after), channel_id=1, source_target_pairs={{0,1},{1,0},{2,3},{3,2},{4,5},{5,4},{6,7},{7,6},{8,9},{9,8},{10,11... | collective-permute-start | bytes 933896 | tf_op jit(solution)/shard_map/ppermute | solution.py:476
  17.6 0.7 collective-permute-start.7
  18.3 3.6 %shard_map.78 = (bf16[10,12,16,128]{3,2,1,0:T(8,128)(2,1)S(1)}, bf16[12,14,32,128]{3,2,1,0:T(8,128)(2,1)S(1)}, bf16[9,12,16,128]{3,2,1,0:T(8,128)(2,1)S(1)}, bf1...) custom-call(s32[4]{0:T(128)S(1)} %pad_add_fusion.pos, ...), custom_call_target="tpu_custom_call", output_to_operand_aliasing={{0}: (1, {}), {1}: (2, {})} | custom-call | flops 4140000000 | bytes 1 | tf_op jit(solution)/shard_map/pallas_call | solution.py:22
  22.1 3.5 %collective-permute-start.5 = (bf16[9,12,16,128]{3,2,1,0:T(8,128)(2,1)S(1)}, bf16[9,12,16,128]{3,2,1,0:T(8,128)(2,1)S(1)}, u32[]{:S(2)}, u32[]{:S(2)}) collective-permute-start(bf16[9,12,16,128]{3,2,1,0:T(8,128)(2,1)S(1)} %get-tuple-element.42), channel_id=1, source_target_pairs={{8,16},{24,32},{40,48},{56,64},{72,80},{88,96},{104,112},{120,128}... | collective-permute-start | bytes 1327112 | tf_op jit(solution)/shard_map/ppermute | solution.py:500
  25.6 9.2 %collective-permute-start.8 = (bf16[26,16,128]{2,1,0:T(8,128)(2,1)S(1)}, bf16[26,16,128]{2,1,0:T(8,128)(2,1)S(1)}, u32[]{:S(2)}, u32[]{:S(2)}) collective-permute-start(bf16[26,16,128]{2,1,0:T(8,128)(2,1)S(1)} %get-tuple-element.45), channel_id=1, source_target_pairs={{0,1},{1,0},{2,3},{3,2},{4,5},{5,4},{6,7},{7,6},{8,9},{9,8},{10,11... | collective-permute-start | bytes 319496 | tf_op jit(solution)/shard_map/ppermute | solution.py:501
  35.4 6.4 %shard_map.79 = (f32[10,12,16,128]{3,2,1,0:T(8,128)S(1)}, f32[16,128]{1,0:T(8,128)S(1)}, f32[2,9,12,128]{3,2,1,0:T(8,128)S(1)}) custom-call(s32[4]{0:T(128)S(1)} %pad_add_fusion.pos, bf16[10,12,16,128]{3,2,1,0:T(8,128)(2,1)S(1)} %get-tuple-element.38.emb, s32[10,12,128]{2,1,0:T(8,128)S(1)} %copy-done.2, bf16[21,32,128]{2,1,0:T(8,128)(2,1)S(1)} %collective-permute-done.2.ze, ...), custom_call_target="tpu_custom_call" | custom-call | flops 7360000000 | bytes 1 | tf_op jit(solution)/shard_map/pallas_call | solution.py:22
  41.9 4.6 %shard_map.80 = (bf16[10,12,16,128]{3,2,1,0:T(8,128)(2,1)S(1)}, bf16[10,16,48,128]{3,2,1,0:T(8,128)(2,1)S(1)}, bf16[10,16,128]{2,1,0:T(8,128)(2,1)S(1)}, bf16[10,16,128]{2,1,0:T(8,128)(2,1)S(1)}, f32[8,128]{1,0:T(8,128)S(1)}) custom-call(s32[4]{0:T(128)S(1)} %pad_add_fusion.pos, bf16[10,12,16,128]{3,2,1,0:T(8,128)(2,1)S(1)} %get-tuple-element.38.emb, ...), custom_call_target="tpu_custom_call" | custom-call | flops 5750000128 | bytes 1 | tf_op jit(solution)/shard_map/pallas_call | solution.py:22
  46.5 3.8 %shard_map.82 = f32[256,128]{1,0:T(8,128)} custom-call(bf16[10,16,48,128]{3,2,1,0:T(8,128)(2,1)S(1)} %get-tuple-element.52.shifted, bf16[12,14,32,128]{3,2,1,0:T(8,128)(2,1)S(1)} %get-tuple-element.53.ext, bf16[10,12,16,128]{3,2,1,0:T(8,128)(2,1)S(1)} %get-tuple-element.47.own, f32[8,128]{1,0:T(8,128)S(1)} %get-tuple-element.54.lost), custom_call_target="tpu_custom_call" | custom-call | flops 4369999872 | bytes 1 | tf_op jit(solution)/shard_map/pallas_call | solution.py:22
  50.3 8.3 %all-to-all-start = ((f32[32,8,128]{2,1,0:T(8,128)}), f32[32,8,128]{2,1,0:T(8,128)S(1)}, u32[]{:S(2)}, u32[]{:S(2)}) async-start(f32[32,8,128]{2,1,0:T(8,128)} %bitcast.8), calls=%async_computation | async-start | bytes 262144 | tf_op jit(solution)/shard_map/all_to_all | solution.py:558
  58.9 7.6 %collective-permute-start.10 = (bf16[10,16,128]{2,1,0:T(8,128)(2,1)S(1)}, bf16[10,16,128]{2,1,0:T(8,128)(2,1)S(1)}, u32[]{:S(2)}, u32[]{:S(2)}) collective-permute-start(bf16[10,16,128]{2,1,0:T(8,128)(2,1)S(1)} %get-tuple-element.48), channel_id=1, source_target_pairs={{0,1},{1,0},{2,3},{3,2},{4,5},{5,4},{6,7},{7,6},{8,9},{9,8},{10,11... | collective-permute-start | bytes 122888 | tf_op jit(solution)/shard_map/ppermute | solution.py:539
  67.8 18.3 %all-to-all-start.1 = ((f32[8,8,128]{2,1,0:T(8,128)}), f32[8,8,128]{2,1,0:T(8,128)S(1)}, u32[]{:S(2)}, u32[]{:S(2)}) async-start(f32[8,8,128]{2,1,0:T(8,128)} %shard_map.83.after), calls=%async_computation.1 | async-start | bytes 65536 | tf_op jit(solution)/shard_map/all_to_all | solution.py:568
  86.7 0.8 collective-permute-start.12
  87.4 2.1 %collective-permute-start.13 = (bf16[14,16,128]{2,1,0:T(8,128)(2,1)S(1)}, bf16[14,16,128]{2,1,0:T(8,128)(2,1)S(1)}, u32[]{:S(2)}, u32[]{:S(2)}) collective-permute-start(bf16[14,16,128]{2,1,0:T(8,128)(2,1)S(1)} %get-tuple-element.51), channel_id=1, source_target_pairs={{8,16},{24,32},{40,48},{56,64},{72,80},{88,96},{104,112},{120,128}... | collective-permute-start | bytes 172040 | tf_op jit(solution)/shard_map/ppermute | solution.py:556
  89.5 5.6 %all-to-all-done.1.parts = f32[8,8,128]{2,1,0:T(8,128)S(1)} async-done(((f32[8,8,128]{2,1,0:T(8,128)}), f32[8,8,128]{2,1,0:T(8,128)S(1)}, u32[]{:S(2)}, u32[]{:S(2)}) %all-to-all-start.1) | async-done | bytes 32800 | tf_op jit(solution)/shard_map/all_to_all | solution.py:568
  95.1 0.7 shard_map.85
  95.8 6.5 %all-to-all-start.2 = ((f32[32,8,128]{2,1,0:T(8,128)}), f32[32,8,128]{2,1,0:T(8,128)S(1)}, u32[]{:S(2)}, u32[]{:S(2)}) async-start(f32[32,8,128]{2,1,0:T(8,128)} %shard_map.85), calls=%async_computation.2 | async-start | bytes 262144 | tf_op jit(solution)/shard_map/all_to_all | solution.py:570
  102.3 4.8 %shard_map.84 = bf16[10,12,32,128]{3,2,1,0:T(8,128)(2,1)} custom-call(s32[4]{0:T(128)S(1)} %pad_add_fusion.pos, bf16[10,12,16,128]{3,2,1,0:T(8,128)(2,1)S(1)} %get-tuple-element.47.own, bf16[10,16,128]{2,1,0:T(8,128)(2,1)S(1)} %collective-permute-done.10.ye, bf16[10,16,128]{2,1,0:T(8,128)(2,1)S(1)} %collective-permute-done.11.yo, ...), custom_call_target="tpu_custom_call" | custom-call | flops 5634999808 | bytes 1 | tf_op jit(solution)/shard_map/pallas_call | solution.py:22
  107.1 3.7 %all-to-all-done.2 = f32[32,8,128]{2,1,0:T(8,128)S(1)} async-done(((f32[32,8,128]{2,1,0:T(8,128)}), f32[32,8,128]{2,1,0:T(8,128)S(1)}, u32[]{:S(2)}, u32[]{:S(2)}) %all-to-all-start.2) | async-done | bytes 131104 | tf_op jit(solution)/shard_map/all_to_all | solution.py:570
  110.8 0.8 shard_map.86
  (40 shorter events, 5.1 us)
Async XLA Ops:
  0.7 1.2 %copy-start = (bf16[32,10,12,128]{3,0,2,1:T(8,128)(2,1)S(1)}, bf16[32,10,12,128]{3,0,2,1:T(8,128)(2,1)}, u32[]{:S(2)}) copy-start(bf16[32,10,12,128]{3,0,2,1:T(8,128)(2,1)} %param.4) | copy-start | bytes 2949124
  1.9 3.5 %copy-start.3 = (bf16[16,32,3,3,3]{1,0,4,3,2:T(8,128)(2,1)S(1)}, bf16[16,32,3,3,3]{1,0,4,3,2:T(8,128)(2,1)}, u32[]{:S(2)}) copy-start(bf16[16,32,3,3,3]{1,0,4,3,2:T(8,128)(2,1)} %param.6) | copy-start | bytes 82948
  1.9 3.7 %copy-start.4 = (f32[16]{0:T(128)S(1)}, f32[16]{0:T(128)}, u32[]{:S(2)}) copy-start(f32[16]{0:T(128)} %param.7) | copy-start | bytes 196
  1.9 3.8 %copy-start.1 = (bf16[32,10,12,128]{3,0,2,1:T(8,128)(2,1)S(1)}, bf16[32,10,12,128]{3,0,2,1:T(8,128)(2,1)}, u32[]{:S(2)}) copy-start(bf16[32,10,12,128]{3,0,2,1:T(8,128)(2,1)} %param.4) | copy-start | bytes 2949124
  1.9 3.8 %copy-start.2 = (s32[10,12,128]{2,1,0:T(8,128)S(1)}, s32[10,12,128]{2,1,0:T(8,128)}, u32[]{:S(2)}) copy-start(s32[10,12,128]{2,1,0:T(8,128)} %lab.7) | copy-start | bytes 184324
  2.5 6.5 %collective-permute-start = (bf16[10,32,128]{2,1,0:T(8,128)(2,1)S(1)}, bf16[10,32,128]{2,1,0:T(8,128)(2,1)S(1)}, u32[]{:S(2)}, u32[]{:S(2)}) collective-permute-start(bf16[10,32,128]{2,1,0:T(8,128)(2,1)S(1)} %get-tuple-element.33), channel_id=1, source_target_pairs={{0,1},{1,0},{2,3},{3,2},{4,5},{5,4},{6,7},{7,6},{8,9},{9,8},{10,11... | collective-permute-start | bytes 245768 | tf_op jit(solution)/shard_map/ppermute | solution.py:461
  4.8 4.3 %collective-permute-start.1 = (bf16[10,32,128]{2,1,0:T(8,128)(2,1)S(1)}, bf16[10,32,128]{2,1,0:T(8,128)(2,1)S(1)}, u32[]{:S(2)}, u32[]{:S(2)}) collective-permute-start(bf16[10,32,128]{2,1,0:T(8,128)(2,1)S(1)} %get-tuple-element.34), channel_id=1, source_target_pairs={{1,2},{3,4},{5,6},{2,1},{4,3},{6,5},{9,10},{11,12},{13,14},{10,9},... | collective-permute-start | bytes 245768 | tf_op jit(solution)/shard_map/ppermute | solution.py:462
  9.6 8.7 %collective-permute-start.2 = (bf16[21,32,128]{2,1,0:T(8,128)(2,1)S(1)}, bf16[21,32,128]{2,1,0:T(8,128)(2,1)S(1)}, u32[]{:S(2)}, u32[]{:S(2)}) collective-permute-start(bf16[21,32,128]{2,1,0:T(8,128)(2,1)S(1)} %get-tuple-element.36), channel_id=1, source_target_pairs={{0,8},{8,0},{16,24},{24,16},{32,40},{40,32},{48,56},{56,48},{64,72... | collective-permute-start | bytes 516104 | tf_op jit(solution)/shard_map/ppermute | solution.py:486
  11.0 7.3 %collective-permute-start.3 = (bf16[21,32,128]{2,1,0:T(8,128)(2,1)S(1)}, bf16[21,32,128]{2,1,0:T(8,128)(2,1)S(1)}, u32[]{:S(2)}, u32[]{:S(2)}) collective-permute-start(bf16[21,32,128]{2,1,0:T(8,128)(2,1)S(1)} %get-tuple-element.37), channel_id=1, source_target_pairs={{8,16},{24,32},{40,48},{56,64},{72,80},{88,96},{104,112},{120,128}... | collective-permute-start | bytes 516104 | tf_op jit(solution)/shard_map/ppermute | solution.py:487
  13.7 21.0 %collective-permute-start.6 = (bf16[76,16,128]{2,1,0:T(8,128)(2,1)S(1)}, bf16[76,16,128]{2,1,0:T(8,128)(2,1)S(1)}, u32[]{:S(2)}, u32[]{:S(2)}) collective-permute-start(bf16[76,16,128]{2,1,0:T(8,128)(2,1)S(1)} %get-tuple-element.35.after), channel_id=1, source_target_pairs={{0,1},{1,0},{2,3},{3,2},{4,5},{5,4},{6,7},{7,6},{8,9},{9,8},{10,11... | collective-permute-start | bytes 933896 | tf_op jit(solution)/shard_map/ppermute | solution.py:476
  17.6 24.2 %collective-permute-start.7 = (bf16[76,16,128]{2,1,0:T(8,128)(2,1)S(1)}, bf16[76,16,128]{2,1,0:T(8,128)(2,1)S(1)}, u32[]{:S(2)}, u32[]{:S(2)}) collective-permute-start(bf16[76,16,128]{2,1,0:T(8,128)(2,1)S(1)} %get-tuple-element.44), channel_id=1, source_target_pairs={{1,2},{3,4},{5,6},{2,1},{4,3},{6,5},{9,10},{11,12},{13,14},{10,9},... | collective-permute-start | bytes 933896 | tf_op jit(solution)/shard_map/ppermute | solution.py:477
  22.0 19.9 %collective-permute-start.4 = (bf16[9,12,16,128]{3,2,1,0:T(8,128)(2,1)S(1)}, bf16[9,12,16,128]{3,2,1,0:T(8,128)(2,1)S(1)}, u32[]{:S(2)}, u32[]{:S(2)}) collective-permute-start(bf16[9,12,16,128]{3,2,1,0:T(8,128)(2,1)S(1)} %get-tuple-element.41), channel_id=1, source_target_pairs={{0,8},{8,0},{16,24},{24,16},{32,40},{40,32},{48,56},{56,48},{64,72... | collective-permute-start | bytes 1327112 | tf_op jit(solution)/shard_map/ppermute | solution.py:499
  22.1 19.8 %collective-permute-start.5 = (bf16[9,12,16,128]{3,2,1,0:T(8,128)(2,1)S(1)}, bf16[9,12,16,128]{3,2,1,0:T(8,128)(2,1)S(1)}, u32[]{:S(2)}, u32[]{:S(2)}) collective-permute-start(bf16[9,12,16,128]{3,2,1,0:T(8,128)(2,1)S(1)} %get-tuple-element.42), channel_id=1, source_target_pairs={{8,16},{24,32},{40,48},{56,64},{72,80},{88,96},{104,112},{120,128}... | collective-permute-start | bytes 1327112 | tf_op jit(solution)/shard_map/ppermute | solution.py:500
  25.6 16.3 %collective-permute-start.8 = (bf16[26,16,128]{2,1,0:T(8,128)(2,1)S(1)}, bf16[26,16,128]{2,1,0:T(8,128)(2,1)S(1)}, u32[]{:S(2)}, u32[]{:S(2)}) collective-permute-start(bf16[26,16,128]{2,1,0:T(8,128)(2,1)S(1)} %get-tuple-element.45), channel_id=1, source_target_pairs={{0,1},{1,0},{2,3},{3,2},{4,5},{5,4},{6,7},{7,6},{8,9},{9,8},{10,11... | collective-permute-start | bytes 319496 | tf_op jit(solution)/shard_map/ppermute | solution.py:501
  34.8 7.1 %collective-permute-start.9 = (bf16[26,16,128]{2,1,0:T(8,128)(2,1)S(1)}, bf16[26,16,128]{2,1,0:T(8,128)(2,1)S(1)}, u32[]{:S(2)}, u32[]{:S(2)}) collective-permute-start(bf16[26,16,128]{2,1,0:T(8,128)(2,1)S(1)} %get-tuple-element.46), channel_id=1, source_target_pairs={{1,2},{3,4},{5,6},{2,1},{4,3},{6,5},{9,10},{11,12},{13,14},{10,9},... | collective-permute-start | bytes 319496 | tf_op jit(solution)/shard_map/ppermute | solution.py:502
  50.3 16.8 %all-to-all-start = ((f32[32,8,128]{2,1,0:T(8,128)}), f32[32,8,128]{2,1,0:T(8,128)S(1)}, u32[]{:S(2)}, u32[]{:S(2)}) async-start(f32[32,8,128]{2,1,0:T(8,128)} %bitcast.8), calls=%async_computation | async-start | bytes 262144 | tf_op jit(solution)/shard_map/all_to_all | solution.py:558
  58.9 27.2 %collective-permute-start.10 = (bf16[10,16,128]{2,1,0:T(8,128)(2,1)S(1)}, bf16[10,16,128]{2,1,0:T(8,128)(2,1)S(1)}, u32[]{:S(2)}, u32[]{:S(2)}) collective-permute-start(bf16[10,16,128]{2,1,0:T(8,128)(2,1)S(1)} %get-tuple-element.48), channel_id=1, source_target_pairs={{0,1},{1,0},{2,3},{3,2},{4,5},{5,4},{6,7},{7,6},{8,9},{9,8},{10,11... | collective-permute-start | bytes 122888 | tf_op jit(solution)/shard_map/ppermute | solution.py:539
  66.5 19.6 %collective-permute-start.11 = (bf16[10,16,128]{2,1,0:T(8,128)(2,1)S(1)}, bf16[10,16,128]{2,1,0:T(8,128)(2,1)S(1)}, u32[]{:S(2)}, u32[]{:S(2)}) collective-permute-start(bf16[10,16,128]{2,1,0:T(8,128)(2,1)S(1)} %get-tuple-element.49), channel_id=1, source_target_pairs={{1,2},{3,4},{5,6},{2,1},{4,3},{6,5},{9,10},{11,12},{13,14},{10,9},... | collective-permute-start | bytes 122888 | tf_op jit(solution)/shard_map/ppermute | solution.py:540
  67.8 27.3 %all-to-all-start.1 = ((f32[8,8,128]{2,1,0:T(8,128)}), f32[8,8,128]{2,1,0:T(8,128)S(1)}, u32[]{:S(2)}, u32[]{:S(2)}) async-start(f32[8,8,128]{2,1,0:T(8,128)} %shard_map.83.after), calls=%async_computation.1 | async-start | bytes 65536 | tf_op jit(solution)/shard_map/all_to_all | solution.py:568
  86.7 15.6 %collective-permute-start.12 = (bf16[14,16,128]{2,1,0:T(8,128)(2,1)S(1)}, bf16[14,16,128]{2,1,0:T(8,128)(2,1)S(1)}, u32[]{:S(2)}, u32[]{:S(2)}) collective-permute-start(bf16[14,16,128]{2,1,0:T(8,128)(2,1)S(1)} %get-tuple-element.50), channel_id=1, source_target_pairs={{0,8},{8,0},{16,24},{24,16},{32,40},{40,32},{48,56},{56,48},{64,72... | collective-permute-start | bytes 172040 | tf_op jit(solution)/shard_map/ppermute | solution.py:555
  87.4 14.8 %collective-permute-start.13 = (bf16[14,16,128]{2,1,0:T(8,128)(2,1)S(1)}, bf16[14,16,128]{2,1,0:T(8,128)(2,1)S(1)}, u32[]{:S(2)}, u32[]{:S(2)}) collective-permute-start(bf16[14,16,128]{2,1,0:T(8,128)(2,1)S(1)} %get-tuple-element.51), channel_id=1, source_target_pairs={{8,16},{24,32},{40,48},{56,64},{72,80},{88,96},{104,112},{120,128}... | collective-permute-start | bytes 172040 | tf_op jit(solution)/shard_map/ppermute | solution.py:556
  95.8 15.0 %all-to-all-start.2 = ((f32[32,8,128]{2,1,0:T(8,128)}), f32[32,8,128]{2,1,0:T(8,128)S(1)}, u32[]{:S(2)}, u32[]{:S(2)}) async-start(f32[32,8,128]{2,1,0:T(8,128)} %shard_map.85), calls=%async_computation.2 | async-start | bytes 262144 | tf_op jit(solution)/shard_map/all_to_all | solution.py:570

commit v2 on v1

--- a/solution.py
+++ b/solution.py
@@ -18,15 +18,15 @@
 SM = pl.BlockSpec(memory_space=pltpu.SMEM)
 
 
-def call(body, outs, args, specs, scratch=(), micros=1.0, aliases={}):
+def call(body, outs, args, specs, scratch=(), micros=1.0):
     return pl.pallas_call(
         body,
         out_shape=outs,
         in_specs=specs,
         out_specs=jax.tree.map(lambda _: VM, outs),
         scratch_shapes=list(scratch),
-        input_output_aliases=aliases,
         compiler_params=PARAMS,
+        name=getattr(body, "__name__", "final_kernel"),
         cost_estimate=pl.CostEstimate(
             flops=int(micros * PEAK), bytes_accessed=1, transcendentals=0
         ),
@@ -61,7 +61,28 @@
 
 
 def dots(left, right):
-    return jnp.sum(left * right, axis=1) * 0.25
+    count = left.shape[0]
+    parts = []
+    for i in range(count):
+        part = left[i] * right[i]
+        parts.append(part[:8] + part[8:])
+    parts += [None] * (-count % 8)
+    sub = lax.broadcasted_iota(jnp.int32, parts[0].shape, 0)
+    for step in (1, 2, 4):
+        own = jnp.bitwise_and(sub, step) == 0
+        merged = []
+        for first, second in zip(parts[::2], parts[1::2]):
+            if first is None:
+                merged.append(None)
+            elif second is None:
+                merged.append(first + pltpu.roll(first, 8 - step, 0))
+            else:
+                merged.append(
+                    jnp.where(own, first, second)
+                    + pltpu.roll(jnp.where(own, second, first), 8 - step, 0)
+                )
+        parts = merged
+    return jnp.concatenate(parts, axis=0)[:count] * 0.25
 
 
 def fill_rim(ext, ye, yo, ze, zo, pz, py, planes, rows):
@@ -113,11 +134,10 @@
         copy.wait()
 
 
-def second_kernel(pos, feat, lab, w, bias, emb, ext, even, odd, wide):
+def second_kernel(pos, feat, lab, w, bias, emb, even, odd, wide):
     planes, rows = feat.shape[0], feat.shape[1]
     py = pos[1]
     cells = (planes - 2) * (REACH - 1)
-    ext[1 : planes + 1, 1 : rows + 1] = feat[...]
     for out, high in ((even, 1 - py), (odd, py)):
         pack_labels(
             wide,
@@ -128,7 +148,7 @@
         )
         out[cells:] = wide[...].astype(BF).reshape(out.shape[0] - cells, *out.shape[1:])
 
-    @pl.loop(0, planes - 2)
+    @pl.loop(0, planes - 2, unroll=True)
     def _(z):
         for y in range(0, rows - 2, 2):
             for i, value in conv_rows(feat, w, z, (y, y + 1)):
@@ -161,18 +181,20 @@
 
 
 def forward_kernel(
-    pos, part, ext_in, ye, yo, ze, zo, w, bias, emb, ext, se, so, te, to
+    pos, part, feat, ye, yo, ze, zo, w, bias, emb, ext, se, so, te, to
 ):
     planes, rows = emb.shape[0], emb.shape[1]
     pz, py = pos[0], pos[1]
+    ext[1 : planes + 1, 1 : rows + 1] = feat[...]
     fill_rim(ext, ye, yo, ze, zo, pz, py, planes, rows)
-
-    @pl.loop(0, planes)
+    emb[1 : planes - 1, 1 : rows - 1] = part[1 : planes - 1, 1 : rows - 1]
+
+    @pl.loop(0, planes, unroll=True)
     def _(z):
         for i, value in conv_rows(ext, w, z, (0, rows - 1)):
             emb[z, i] = (value + bias[...]).astype(BF)
 
-    @pl.loop(0, 2)
+    @pl.loop(0, 2, unroll=True)
     def _(side):
         z = side * (planes - 1)
         for y in range(1, rows - 1, 2):
@@ -201,7 +223,7 @@
     lane = lax.broadcasted_iota(jnp.int32, (rows, lanes), 1)
     loss[...] = jnp.zeros_like(loss)
 
-    @pl.loop(0, planes)
+    @pl.loop(0, planes, unroll=2)
     def _(z):
         center = emb[z].astype(F32)
         here = lab[z]
@@ -231,7 +253,7 @@
 
     for o in OFFSETS:
 
-        @pl.loop(0, planes - o)
+        @pl.loop(0, planes - o, unroll=True)
         def _(z):
             low, high = emb[z].astype(F32), emb[z + o].astype(F32)
             slopes, losses = pair_terms(dots(low, high), lab[z] == lab[z + o])
@@ -280,7 +302,7 @@
         weight = (is_high * pos[2]).astype(F32)
         for o in OFFSETS:
 
-            @pl.loop(0, o)
+            @pl.loop(0, o, unroll=True)
             def _(t):
                 p = t + is_high * (planes - o)
                 q = t + (1 - is_high) * (REACH - o)
@@ -304,7 +326,7 @@
         )
     live = pos[3].astype(F32)
 
-    @pl.loop(0, planes)
+    @pl.loop(0, planes, unroll=True)
     def _(z):
         center = emb[z].astype(F32)
         here = lab[z].astype(F32)
@@ -353,7 +375,7 @@
     channels, lanes = own.shape[2], own.shape[3]
     acc[...] = jnp.zeros_like(acc)
 
-    @pl.loop(0, planes)
+    @pl.loop(0, planes, unroll=True)
     def _(z):
         total = acc[...]
         for y in range(0, rows + 2, 2):
@@ -393,7 +415,7 @@
     ext[1 : planes + 1, 1 : rows + 1] = own[...]
     fill_rim(ext, ye, yo, ze, zo, pos[0], pos[1], planes, rows)
 
-    @pl.loop(0, planes)
+    @pl.loop(0, planes, unroll=True)
     def _(z):
         for y in range(0, rows, 2):
             for i, value in conv_rows(ext, w, z, (y, y + 1)):
@@ -465,9 +487,9 @@
     y_early = sds(
         ((planes - 2) * (REACH - 1) + y_blocks * (ch_in // emb_ch),) + tile, BF
     )
-    emb_part, ext_part, me, mo = call(
+    emb_part, me, mo = call(
         second_kernel,
-        (emb_shape, ext_shape, y_early, y_early),
+        (emb_shape, y_early, y_early),
         (pos, feat, labels, w_fwd, bias),
         [SM] + [VM] * 4,
         scratch=[pltpu.VMEM((y_blocks * ch_in, lanes), F32)],
@@ -491,10 +513,9 @@
     emb, feat_ext, se, so, te, to = call(
         forward_kernel,
         (emb_shape, ext_shape, z_halo, z_halo, y_late, y_late),
-        (pos, emb_part, ext_part, fye, fyo, fze, fzo, w_fwd, bias),
+        (pos, emb_part, feat, fye, fyo, fze, fzo, w_fwd, bias),
         [SM] + [VM] * 8,
         micros=3.6,
-        aliases={1: 0, 2: 1},
     )
     eze = lax.ppermute(se, "gz", z_even)
     ezo = lax.ppermute(so, "gz", z_odd)

time: 112 us -> 109 us (0.973)
  Pallas kernels: 30.5 us -> 19.4 us
  starting transfers between devices: 69 us -> 74.2 us
  waiting for transfers between devices: 9.32 us -> 12 us
    pallas_call x12, Pallas kernels: 30.5 us -> 19.4 us  [call(): pl.pallas_call(body, out_shape=outs, in_specs=specs, out_specs=jax.tree.m...]
    all_to_all x1, starting transfers between devices: 18.3 us -> 22.9 us  [per_device(): parts = lax.all_to_all(mine, 'gy', 0, 0)]
    all_to_all x1, waiting for transfers between devices: 3.71 us -> 5.69 us  [per_device(): total = lax.all_to_all(mine, 'gz', 0, 0).reshape(padded, lanes)]
    ppermute x1, starting transfers between devices: 1.35 us -> 2.69 us  [per_device(): fze = lax.ppermute(me, 'gz', z_even)]
  transfers between devices with their start and end apart: 17 -> 17, of which waited for: 2 -> 3; matrix products, arithmetic and copies ran while one was open for 0% -> 1% of each run, Pallas kernels for 18% -> 11%
where the time goes in v2:
time: 109 us; the launch traced here: 108 us
  starting transfers between devices  74.2 us (68%)
  Pallas kernels  19.4 us (18%)
  waiting for transfers between devices  12 us (11%)
  local copies, waits for them, and re-layouts  1.77 us (2%)
    all_to_all x1, starting transfers between devices, per_device(): parts = lax.all_to_all(mine, 'gy', 0, 0)  22.9 us
    pallas_call x12, Pallas kernels, call(): pl.pallas_call(body, out_shape=outs, in_specs=specs, out_specs=jax.tree.m...  19.4 us
    ppermute x1, starting transfers between devices, per_device(): eye = lax.ppermute(te, 'gy', y_even)  8.97 us
    all_to_all x1, starting transfers between devices, per_device(): parts = lax.all_to_all(partial.reshape(gz, share, lanes), 'gz', 0, 0)  8.96 us
    ppermute x1, starting transfers between devices, per_device(): gye = lax.ppermute(ge, 'gy', y_even)  7.67 us
    all_to_all x1, starting transfers between devices, per_device(): total = lax.all_to_all(mine, 'gz', 0, 0).reshape(padded, lanes)  6.41 us
    all_to_all x1, waiting for transfers between devices, per_device(): total = lax.all_to_all(mine, 'gz', 0, 0).reshape(padded, lanes)  5.69 us
    all_to_all x1, waiting for transfers between devices, per_device(): parts = lax.all_to_all(mine, 'gy', 0, 0)  5.63 us
  transfers between devices with their start and end apart: 17, of which 3 were waited for; matrix products, arithmetic and copies ran while one was open for 1% of the time, Pallas kernels for 11%

profile of v2, /device:TPU:1, one launch (start us, length us, event | category | flops | bytes accessed | tf_op | source)
XLA Modules:
  0.0 108.4 jit_solution(12310251218221262793)
XLA Ops:
  0.7 1.2 %copy-done = bf16[32,10,12,128]{3,0,2,1:T(8,128)(2,1)S(1)} copy-done((bf16[32,10,12,128]{3,0,2,1:T(8,128)(2,1)S(1)}, bf16[32,10,12,128]{3,0,2,1:T(8,128)(2,1)}, u32[]{:S(2)}) %copy-start) | copy-done | bytes 983064
  2.5 2.2 %collective-permute-start = (bf16[10,32,128]{2,1,0:T(8,128)(2,1)S(1)}, bf16[10,32,128]{2,1,0:T(8,128)(2,1)S(1)}, u32[]{:S(2)}, u32[]{:S(2)}) collective-permute-start(bf16[10,32,128]{2,1,0:T(8,128)(2,1)S(1)} %get-tuple-element.31), channel_id=1, source_target_pairs={{0,1},{1,0},{2,3},{3,2},{4,5},{5,4},{6,7},{7,6},{8,9},{9,8},{10,11... | collective-permute-start | bytes 245768 | tf_op jit(solution)/shard_map/ppermute | solution.py:483
  5.7 2.0 %second_kernel.1 = (bf16[10,12,16,128]{3,2,1,0:T(8,128)(2,1)S(1)}, bf16[76,16,128]{2,1,0:T(8,128)(2,1)S(1)}, bf16[76,16,128]{2,1,0:T(8,128)(2,1)S(1)}) custom-call(s32[4]{0:T(128)S(1)} %pad_add_fusion.pos, bf16[10,12,32,128]{3,2,1,0:T(8,128)(2,1)S(1)} %bitcast.21, s32[10,12,128]{2,1,0:T(8,128)S(1)} %copy-done.2, bf16[48,288]{1,0:T(8,128)(2,1)S(1)} %reshape.30.w, ...), custom_call_target="tpu_custom_call" | custom-call | flops 3910000128 | bytes 1 | tf_op jit(solution)/shard_map/second_kernel/pallas_call | solution.py:22
  8.3 2.7 %collective-permute-start.2 = (bf16[21,32,128]{2,1,0:T(8,128)(2,1)S(1)}, bf16[21,32,128]{2,1,0:T(8,128)(2,1)S(1)}, u32[]{:S(2)}, u32[]{:S(2)}) collective-permute-start(bf16[21,32,128]{2,1,0:T(8,128)(2,1)S(1)} %get-tuple-element.34), channel_id=1, source_target_pairs={{0,8},{8,0},{16,24},{24,16},{32,40},{40,32},{48,56},{56,48},{64,72... | collective-permute-start | bytes 516104 | tf_op jit(solution)/shard_map/ppermute | solution.py:508
  11.0 1.9 %collective-permute-start.3 = (bf16[21,32,128]{2,1,0:T(8,128)(2,1)S(1)}, bf16[21,32,128]{2,1,0:T(8,128)(2,1)S(1)}, u32[]{:S(2)}, u32[]{:S(2)}) collective-permute-start(bf16[21,32,128]{2,1,0:T(8,128)(2,1)S(1)} %get-tuple-element.35), channel_id=1, source_target_pairs={{8,16},{24,32},{40,48},{56,64},{72,80},{88,96},{104,112},{120,128}... | collective-permute-start | bytes 516104 | tf_op jit(solution)/shard_map/ppermute | solution.py:509
  12.9 3.7 %collective-permute-start.6 = (bf16[76,16,128]{2,1,0:T(8,128)(2,1)S(1)}, bf16[76,16,128]{2,1,0:T(8,128)(2,1)S(1)}, u32[]{:S(2)}, u32[]{:S(2)}) collective-permute-start(bf16[76,16,128]{2,1,0:T(8,128)(2,1)S(1)} %get-tuple-element.33.after), channel_id=1, source_target_pairs={{0,1},{1,0},{2,3},{3,2},{4,5},{5,4},{6,7},{7,6},{8,9},{9,8},{10,11... | collective-permute-start | bytes 933896 | tf_op jit(solution)/shard_map/ppermute | solution.py:498
  17.3 0.7 collective-permute-done.3.zo
  18.0 1.5 %forward_kernel.1 = (bf16[10,12,16,128]{3,2,1,0:T(8,128)(2,1)S(1)}, bf16[12,14,32,128]{3,2,1,0:T(8,128)(2,1)S(1)}, bf16[9,12,16,128]{3,2,1,0:T(8,128)(2,1)S(1)},...) custom-call(s32[4]{0:T(128)S(1)} %pad_add_fusion.pos, ...), custom_call_target="tpu_custom_call" | custom-call | flops 4140000000 | bytes 1 | tf_op jit(solution)/shard_map/forward_kernel/pallas_call | solution.py:22
  19.6 3.2 %collective-permute-start.5 = (bf16[9,12,16,128]{3,2,1,0:T(8,128)(2,1)S(1)}, bf16[9,12,16,128]{3,2,1,0:T(8,128)(2,1)S(1)}, u32[]{:S(2)}, u32[]{:S(2)}) collective-permute-start(bf16[9,12,16,128]{3,2,1,0:T(8,128)(2,1)S(1)} %get-tuple-element.40), channel_id=1, source_target_pairs={{8,16},{24,32},{40,48},{56,64},{72,80},{88,96},{104,112},{120,128}... | collective-permute-start | bytes 1327112 | tf_op jit(solution)/shard_map/ppermute | solution.py:521
  22.9 9.0 %collective-permute-start.8 = (bf16[26,16,128]{2,1,0:T(8,128)(2,1)S(1)}, bf16[26,16,128]{2,1,0:T(8,128)(2,1)S(1)}, u32[]{:S(2)}, u32[]{:S(2)}) collective-permute-start(bf16[26,16,128]{2,1,0:T(8,128)(2,1)S(1)} %get-tuple-element.43), channel_id=1, source_target_pairs={{0,1},{1,0},{2,3},{3,2},{4,5},{5,4},{6,7},{7,6},{8,9},{9,8},{10,11... | collective-permute-start | bytes 319496 | tf_op jit(solution)/shard_map/ppermute | solution.py:522
  32.5 4.1 %inner_kernel.1 = (f32[10,12,16,128]{3,2,1,0:T(8,128)S(1)}, f32[16,128]{1,0:T(8,128)S(1)}, f32[2,9,12,128]{3,2,1,0:T(8,128)S(1)}) custom-call(s32[4]{0:T(128)S(1)} %pad_add_fusion.pos, bf16[10,12,16,128]{3,2,1,0:T(8,128)(2,1)S(1)} %get-tuple-element.36.emb, s32[10,12,128]{2,1,0:T(8,128)S(1)} %copy-done.2, ...), custom_call_target="tpu_custom_call" | custom-call | flops 7360000000 | bytes 1 | tf_op jit(solution)/shard_map/inner_kernel/pallas_call | solution.py:22
  36.6 2.9 %outer_kernel.1 = (bf16[10,12,16,128]{3,2,1,0:T(8,128)(2,1)S(1)}, bf16[10,16,48,128]{3,2,1,0:T(8,128)(2,1)S(1)}, bf16[10,16,128]{2,1,0:T(8,128)(2,1)S(1)}, bf16[10,16,128]{2,1,0:T(8,128)(2,1)S(1)}, f32[8,128]{1,0:T(8,128)S(1)}) custom-call(s32[4]{0:T(128)S(1)} %pad_add_fusion.pos, bf16[10,12,16,128]{3,2,1,0:T(8,128)(2,1)S(1)} %get-tuple-element.36.emb, ...), custom_call_target="tpu_custom_call" | custom-call | flops 5750000128 | bytes 1 | tf_op jit(solution)/shard_map/outer_kernel/pallas_call | solution.py:22
  39.5 2.2 %weight_kernel.1 = f32[256,128]{1,0:T(8,128)} custom-call(bf16[10,16,48,128]{3,2,1,0:T(8,128)(2,1)S(1)} %get-tuple-element.50.shifted, bf16[12,14,32,128]{3,2,1,0:T(8,128)(2,1)S(1)} %get-tuple-element.51.ext, bf16[10,12,16,128]{3,2,1,0:T(8,128)(2,1)S(1)} %get-tuple-element.45.own, f32[8,128]{1,0:T(8,128)S(1)} %get-tuple-element.52.lost), custom_call_target="tpu_custom_call" | custom-call | flops 4369999872 | bytes 1 | tf_op jit(solution)/shard_map/weight_kernel/pallas_call | solution.py:22
  41.8 9.0 %all-to-all-start = ((f32[32,8,128]{2,1,0:T(8,128)}), f32[32,8,128]{2,1,0:T(8,128)S(1)}, u32[]{:S(2)}, u32[]{:S(2)}) async-start(f32[32,8,128]{2,1,0:T(8,128)} %bitcast.8), calls=%async_computation | async-start | bytes 262144 | tf_op jit(solution)/shard_map/all_to_all | solution.py:579
  51.0 7.7 %collective-permute-start.10 = (bf16[10,16,128]{2,1,0:T(8,128)(2,1)S(1)}, bf16[10,16,128]{2,1,0:T(8,128)(2,1)S(1)}, u32[]{:S(2)}, u32[]{:S(2)}) collective-permute-start(bf16[10,16,128]{2,1,0:T(8,128)(2,1)S(1)} %get-tuple-element.46), channel_id=1, source_target_pairs={{0,1},{1,0},{2,3},{3,2},{4,5},{5,4},{6,7},{7,6},{8,9},{9,8},{10,11... | collective-permute-start | bytes 122888 | tf_op jit(solution)/shard_map/ppermute | solution.py:560
  60.0 22.9 %all-to-all-start.1 = ((f32[8,8,128]{2,1,0:T(8,128)}), f32[8,8,128]{2,1,0:T(8,128)S(1)}, u32[]{:S(2)}, u32[]{:S(2)}) async-start(f32[8,8,128]{2,1,0:T(8,128)} %spread_kernel.2.after), calls=%async_computation.1 | async-start | bytes 65536 | tf_op jit(solution)/shard_map/all_to_all | solution.py:589
  83.5 0.7 collective-permute-start.12
  84.2 2.1 %collective-permute-start.13 = (bf16[14,16,128]{2,1,0:T(8,128)(2,1)S(1)}, bf16[14,16,128]{2,1,0:T(8,128)(2,1)S(1)}, u32[]{:S(2)}, u32[]{:S(2)}) collective-permute-start(bf16[14,16,128]{2,1,0:T(8,128)(2,1)S(1)} %get-tuple-element.49), channel_id=1, source_target_pairs={{8,16},{24,32},{40,48},{56,64},{72,80},{88,96},{104,112},{120,128}... | collective-permute-start | bytes 172040 | tf_op jit(solution)/shard_map/ppermute | solution.py:577
  86.3 5.6 %all-to-all-done.1.parts = f32[8,8,128]{2,1,0:T(8,128)S(1)} async-done(((f32[8,8,128]{2,1,0:T(8,128)}), f32[8,8,128]{2,1,0:T(8,128)S(1)}, u32[]{:S(2)}, u32[]{:S(2)}) %all-to-all-start.1) | async-done | bytes 32800 | tf_op jit(solution)/shard_map/all_to_all | solution.py:589
  92.0 0.7 spread_kernel.3
  92.6 6.4 %all-to-all-start.2 = ((f32[32,8,128]{2,1,0:T(8,128)}), f32[32,8,128]{2,1,0:T(8,128)S(1)}, u32[]{:S(2)}, u32[]{:S(2)}) async-start(f32[32,8,128]{2,1,0:T(8,128)} %spread_kernel.3), calls=%async_computation.2 | async-start | bytes 262144 | tf_op jit(solution)/shard_map/all_to_all | solution.py:591
  99.1 2.8 %backward_kernel.1 = bf16[10,12,32,128]{3,2,1,0:T(8,128)(2,1)} custom-call(s32[4]{0:T(128)S(1)} %pad_add_fusion.pos, bf16[10,12,16,128]{3,2,1,0:T(8,128)(2,1)S(1)} %get-tuple-element.45.own, bf16[10,16,128]{2,1,0:T(8,128)(2,1)S(1)} %collective-permute-done.10.ye, bf16[10,16,128]{2,1,0:T(8,128)(2,1)S(1)} %collective-permute-done.11.yo, ...), custom_call_target="tpu_custom_call" | custom-call | flops 5634999808 | bytes 1 | tf_op jit(solution)/shard_map/backward_kernel/pallas_call | solution.py:22
  101.9 5.7 %all-to-all-done.2 = f32[32,8,128]{2,1,0:T(8,128)S(1)} async-done(((f32[32,8,128]{2,1,0:T(8,128)}), f32[32,8,128]{2,1,0:T(8,128)S(1)}, u32[]{:S(2)}, u32[]{:S(2)}) %all-to-all-start.2) | async-done | bytes 131104 | tf_op jit(solution)/shard_map/all_to_all | solution.py:591
  107.6 0.8 final_kernel.1
  (40 shorter events, 5.8 us)
Async XLA Ops:
  0.7 1.2 %copy-start = (bf16[32,10,12,128]{3,0,2,1:T(8,128)(2,1)S(1)}, bf16[32,10,12,128]{3,0,2,1:T(8,128)(2,1)}, u32[]{:S(2)}) copy-start(bf16[32,10,12,128]{3,0,2,1:T(8,128)(2,1)} %param.4) | copy-start | bytes 2949124
  1.9 3.5 %copy-start.3 = (bf16[16,32,3,3,3]{1,0,4,3,2:T(8,128)(2,1)S(1)}, bf16[16,32,3,3,3]{1,0,4,3,2:T(8,128)(2,1)}, u32[]{:S(2)}) copy-start(bf16[16,32,3,3,3]{1,0,4,3,2:T(8,128)(2,1)} %param.6) | copy-start | bytes 82948
  1.9 3.7 %copy-start.4 = (f32[16]{0:T(128)S(1)}, f32[16]{0:T(128)}, u32[]{:S(2)}) copy-start(f32[16]{0:T(128)} %param.7) | copy-start | bytes 196
  1.9 3.8 %copy-start.1 = (bf16[32,10,12,128]{3,0,2,1:T(8,128)(2,1)S(1)}, bf16[32,10,12,128]{3,0,2,1:T(8,128)(2,1)}, u32[]{:S(2)}) copy-start(bf16[32,10,12,128]{3,0,2,1:T(8,128)(2,1)} %param.4) | copy-start | bytes 2949124
  1.9 3.8 %copy-start.2 = (s32[10,12,128]{2,1,0:T(8,128)S(1)}, s32[10,12,128]{2,1,0:T(8,128)}, u32[]{:S(2)}) copy-start(s32[10,12,128]{2,1,0:T(8,128)} %lab.7) | copy-start | bytes 184324
  2.5 5.1 %collective-permute-start = (bf16[10,32,128]{2,1,0:T(8,128)(2,1)S(1)}, bf16[10,32,128]{2,1,0:T(8,128)(2,1)S(1)}, u32[]{:S(2)}, u32[]{:S(2)}) collective-permute-start(bf16[10,32,128]{2,1,0:T(8,128)(2,1)S(1)} %get-tuple-element.31), channel_id=1, source_target_pairs={{0,1},{1,0},{2,3},{3,2},{4,5},{5,4},{6,7},{7,6},{8,9},{9,8},{10,11... | collective-permute-start | bytes 245768 | tf_op jit(solution)/shard_map/ppermute | solution.py:483
  4.8 2.9 %collective-permute-start.1 = (bf16[10,32,128]{2,1,0:T(8,128)(2,1)S(1)}, bf16[10,32,128]{2,1,0:T(8,128)(2,1)S(1)}, u32[]{:S(2)}, u32[]{:S(2)}) collective-permute-start(bf16[10,32,128]{2,1,0:T(8,128)(2,1)S(1)} %get-tuple-element.32), channel_id=1, source_target_pairs={{1,2},{3,4},{5,6},{2,1},{4,3},{6,5},{9,10},{11,12},{13,14},{10,9},... | collective-permute-start | bytes 245768 | tf_op jit(solution)/shard_map/ppermute | solution.py:484
  8.3 9.0 %collective-permute-start.2 = (bf16[21,32,128]{2,1,0:T(8,128)(2,1)S(1)}, bf16[21,32,128]{2,1,0:T(8,128)(2,1)S(1)}, u32[]{:S(2)}, u32[]{:S(2)}) collective-permute-start(bf16[21,32,128]{2,1,0:T(8,128)(2,1)S(1)} %get-tuple-element.34), channel_id=1, source_target_pairs={{0,8},{8,0},{16,24},{24,16},{32,40},{40,32},{48,56},{56,48},{64,72... | collective-permute-start | bytes 516104 | tf_op jit(solution)/shard_map/ppermute | solution.py:508
  11.0 7.0 %collective-permute-start.3 = (bf16[21,32,128]{2,1,0:T(8,128)(2,1)S(1)}, bf16[21,32,128]{2,1,0:T(8,128)(2,1)S(1)}, u32[]{:S(2)}, u32[]{:S(2)}) collective-permute-start(bf16[21,32,128]{2,1,0:T(8,128)(2,1)S(1)} %get-tuple-element.35), channel_id=1, source_target_pairs={{8,16},{24,32},{40,48},{56,64},{72,80},{88,96},{104,112},{120,128}... | collective-permute-start | bytes 516104 | tf_op jit(solution)/shard_map/ppermute | solution.py:509
  12.9 18.9 %collective-permute-start.6 = (bf16[76,16,128]{2,1,0:T(8,128)(2,1)S(1)}, bf16[76,16,128]{2,1,0:T(8,128)(2,1)S(1)}, u32[]{:S(2)}, u32[]{:S(2)}) collective-permute-start(bf16[76,16,128]{2,1,0:T(8,128)(2,1)S(1)} %get-tuple-element.33.after), channel_id=1, source_target_pairs={{0,1},{1,0},{2,3},{3,2},{4,5},{5,4},{6,7},{7,6},{8,9},{9,8},{10,11... | collective-permute-start | bytes 933896 | tf_op jit(solution)/shard_map/ppermute | solution.py:498
  16.6 19.9 %collective-permute-start.7 = (bf16[76,16,128]{2,1,0:T(8,128)(2,1)S(1)}, bf16[76,16,128]{2,1,0:T(8,128)(2,1)S(1)}, u32[]{:S(2)}, u32[]{:S(2)}) collective-permute-start(bf16[76,16,128]{2,1,0:T(8,128)(2,1)S(1)} %get-tuple-element.42), channel_id=1, source_target_pairs={{1,2},{3,4},{5,6},{2,1},{4,3},{6,5},{9,10},{11,12},{13,14},{10,9},... | collective-permute-start | bytes 933896 | tf_op jit(solution)/shard_map/ppermute | solution.py:499
  19.5 17.1 %collective-permute-start.4 = (bf16[9,12,16,128]{3,2,1,0:T(8,128)(2,1)S(1)}, bf16[9,12,16,128]{3,2,1,0:T(8,128)(2,1)S(1)}, u32[]{:S(2)}, u32[]{:S(2)}) collective-permute-start(bf16[9,12,16,128]{3,2,1,0:T(8,128)(2,1)S(1)} %get-tuple-element.39), channel_id=1, source_target_pairs={{0,8},{8,0},{16,24},{24,16},{32,40},{40,32},{48,56},{56,48},{64,72... | collective-permute-start | bytes 1327112 | tf_op jit(solution)/shard_map/ppermute | solution.py:520
  19.6 17.0 %collective-permute-start.5 = (bf16[9,12,16,128]{3,2,1,0:T(8,128)(2,1)S(1)}, bf16[9,12,16,128]{3,2,1,0:T(8,128)(2,1)S(1)}, u32[]{:S(2)}, u32[]{:S(2)}) collective-permute-start(bf16[9,12,16,128]{3,2,1,0:T(8,128)(2,1)S(1)} %get-tuple-element.40), channel_id=1, source_target_pairs={{8,16},{24,32},{40,48},{56,64},{72,80},{88,96},{104,112},{120,128}... | collective-permute-start | bytes 1327112 | tf_op jit(solution)/shard_map/ppermute | solution.py:521
  22.9 13.7 %collective-permute-start.8 = (bf16[26,16,128]{2,1,0:T(8,128)(2,1)S(1)}, bf16[26,16,128]{2,1,0:T(8,128)(2,1)S(1)}, u32[]{:S(2)}, u32[]{:S(2)}) collective-permute-start(bf16[26,16,128]{2,1,0:T(8,128)(2,1)S(1)} %get-tuple-element.43), channel_id=1, source_target_pairs={{0,1},{1,0},{2,3},{3,2},{4,5},{5,4},{6,7},{7,6},{8,9},{9,8},{10,11... | collective-permute-start | bytes 319496 | tf_op jit(solution)/shard_map/ppermute | solution.py:522
  31.8 4.8 %collective-permute-start.9 = (bf16[26,16,128]{2,1,0:T(8,128)(2,1)S(1)}, bf16[26,16,128]{2,1,0:T(8,128)(2,1)S(1)}, u32[]{:S(2)}, u32[]{:S(2)}) collective-permute-start(bf16[26,16,128]{2,1,0:T(8,128)(2,1)S(1)} %get-tuple-element.44), channel_id=1, source_target_pairs={{1,2},{3,4},{5,6},{2,1},{4,3},{6,5},{9,10},{11,12},{13,14},{10,9},... | collective-permute-start | bytes 319496 | tf_op jit(solution)/shard_map/ppermute | solution.py:523
  41.8 17.6 %all-to-all-start = ((f32[32,8,128]{2,1,0:T(8,128)}), f32[32,8,128]{2,1,0:T(8,128)S(1)}, u32[]{:S(2)}, u32[]{:S(2)}) async-start(f32[32,8,128]{2,1,0:T(8,128)} %bitcast.8), calls=%async_computation | async-start | bytes 262144 | tf_op jit(solution)/shard_map/all_to_all | solution.py:579
  51.0 31.9 %collective-permute-start.10 = (bf16[10,16,128]{2,1,0:T(8,128)(2,1)S(1)}, bf16[10,16,128]{2,1,0:T(8,128)(2,1)S(1)}, u32[]{:S(2)}, u32[]{:S(2)}) collective-permute-start(bf16[10,16,128]{2,1,0:T(8,128)(2,1)S(1)} %get-tuple-element.46), channel_id=1, source_target_pairs={{0,1},{1,0},{2,3},{3,2},{4,5},{5,4},{6,7},{7,6},{8,9},{9,8},{10,11... | collective-permute-start | bytes 122888 | tf_op jit(solution)/shard_map/ppermute | solution.py:560
  58.7 24.2 %collective-permute-start.11 = (bf16[10,16,128]{2,1,0:T(8,128)(2,1)S(1)}, bf16[10,16,128]{2,1,0:T(8,128)(2,1)S(1)}, u32[]{:S(2)}, u32[]{:S(2)}) collective-permute-start(bf16[10,16,128]{2,1,0:T(8,128)(2,1)S(1)} %get-tuple-element.47), channel_id=1, source_target_pairs={{1,2},{3,4},{5,6},{2,1},{4,3},{6,5},{9,10},{11,12},{13,14},{10,9},... | collective-permute-start | bytes 122888 | tf_op jit(solution)/shard_map/ppermute | solution.py:561
  60.0 31.9 %all-to-all-start.1 = ((f32[8,8,128]{2,1,0:T(8,128)}), f32[8,8,128]{2,1,0:T(8,128)S(1)}, u32[]{:S(2)}, u32[]{:S(2)}) async-start(f32[8,8,128]{2,1,0:T(8,128)} %spread_kernel.2.after), calls=%async_computation.1 | async-start | bytes 65536 | tf_op jit(solution)/shard_map/all_to_all | solution.py:589
  83.5 15.5 %collective-permute-start.12 = (bf16[14,16,128]{2,1,0:T(8,128)(2,1)S(1)}, bf16[14,16,128]{2,1,0:T(8,128)(2,1)S(1)}, u32[]{:S(2)}, u32[]{:S(2)}) collective-permute-start(bf16[14,16,128]{2,1,0:T(8,128)(2,1)S(1)} %get-tuple-element.48), channel_id=1, source_target_pairs={{0,8},{8,0},{16,24},{24,16},{32,40},{40,32},{48,56},{56,48},{64,72... | collective-permute-start | bytes 172040 | tf_op jit(solution)/shard_map/ppermute | solution.py:576
  84.2 14.8 %collective-permute-start.13 = (bf16[14,16,128]{2,1,0:T(8,128)(2,1)S(1)}, bf16[14,16,128]{2,1,0:T(8,128)(2,1)S(1)}, u32[]{:S(2)}, u32[]{:S(2)}) collective-permute-start(bf16[14,16,128]{2,1,0:T(8,128)(2,1)S(1)} %get-tuple-element.49), channel_id=1, source_target_pairs={{8,16},{24,32},{40,48},{56,64},{72,80},{88,96},{104,112},{120,128}... | collective-permute-start | bytes 172040 | tf_op jit(solution)/shard_map/ppermute | solution.py:577
  92.6 15.0 %all-to-all-start.2 = ((f32[32,8,128]{2,1,0:T(8,128)}), f32[32,8,128]{2,1,0:T(8,128)S(1)}, u32[]{:S(2)}, u32[]{:S(2)}) async-start(f32[32,8,128]{2,1,0:T(8,128)} %spread_kernel.3), calls=%async_computation.2 | async-start | bytes 262144 | tf_op jit(solution)/shard_map/all_to_all | solution.py:591

commit v3 on v2

--- a/solution.py
+++ b/solution.py
@@ -85,11 +85,12 @@
     return jnp.concatenate(parts, axis=0)[:count] * 0.25
 
 
-def fill_rim(ext, ye, yo, ze, zo, pz, py, planes, rows):
-    ext[1 : planes + 1, (1 - py) * (rows + 1)] = ye[...]
-    ext[1 : planes + 1, py * (rows + 1)] = yo[...]
-    ext[(1 - pz) * (planes + 1)] = ze[: rows + 2]
-    ext[pz * (planes + 1)] = zo[: rows + 2]
+def fill_rim(ext, ze, zo, ye, yo, pz, py):
+    planes, rows = ext.shape[0] - 2, ext.shape[1] - 2
+    ext[(1 - pz) * (planes + 1), 1 : rows + 1] = ze[...]
+    ext[pz * (planes + 1), 1 : rows + 1] = zo[...]
+    ext[:, (1 - py) * (rows + 1)] = ye[...]
+    ext[:, py * (rows + 1)] = yo[...]
 
 
 def conv_rows(ext, w_ref, z, rows):
@@ -123,10 +124,10 @@
 
 
 def first_kernel(pos, feat, even, odd, sems):
-    py, rows = pos[1], feat.shape[1]
+    pz, planes = pos[0], feat.shape[0]
     copies = [
-        pltpu.make_async_copy(feat.at[:, (1 - py) * (rows - 1)], even, sems.at[0]),
-        pltpu.make_async_copy(feat.at[:, py * (rows - 1)], odd, sems.at[1]),
+        pltpu.make_async_copy(feat.at[(1 - pz) * (planes - 1)], even, sems.at[0]),
+        pltpu.make_async_copy(feat.at[pz * (planes - 1)], odd, sems.at[1]),
     ]
     for copy in copies:
         copy.start()
@@ -134,9 +135,13 @@
         copy.wait()
 
 
-def second_kernel(pos, feat, lab, w, bias, emb, even, odd, wide):
+def second_kernel(pos, feat, lab, w, bias, emb, even, odd, lze, lzo, wide, widez):
     planes, rows = feat.shape[0], feat.shape[1]
-    py = pos[1]
+    pz, py = pos[0], pos[1]
+    for out, high in ((lze, 1 - pz), (lzo, pz)):
+        base = high * (planes - REACH)
+        pack_labels(widez, [lab[base + p] for p in range(REACH)])
+        out[...] = widez[...].astype(BF).reshape(out.shape)
     cells = (planes - 2) * (REACH - 1)
     for out, high in ((even, 1 - py), (odd, py)):
         pack_labels(
@@ -159,34 +164,23 @@
         out[:cells] = part.reshape(cells, *part.shape[2:])
 
 
-def edge_planes(pos, own, ye, yo, even, odd):
+def edge_rows(pos, own, ze, zo, after, even, odd):
     planes, rows = own.shape[0], own.shape[1]
     pz, py = pos[0], pos[1]
-    for out, high in ((even, 1 - pz), (odd, pz)):
-        plane = high * (planes - 1)
-        out[1 : rows + 1] = own[plane]
-        out[(1 - py) * (rows + 1)] = ye[plane]
-        out[py * (rows + 1)] = yo[plane]
-
-
-def third_kernel(pos, feat, ye, yo, lab, after, even, odd, wide):
-    planes, rows = feat.shape[0], feat.shape[1]
-    pz = pos[0]
-    edge_planes(pos, feat, ye, yo, even, odd)
-    for out, high in ((even, 1 - pz), (odd, pz)):
-        base = high * (planes - REACH)
-        pack_labels(wide, [lab[base + p] for p in range(REACH)])
-        labels = wide[...].astype(BF)
-        out[rows + 2 :] = labels.reshape(out.shape[0] - rows - 2, *out.shape[1:])
+    for out, high in ((even, 1 - py), (odd, py)):
+        row = high * (rows - 1)
+        out[1 : planes + 1] = own[:, row]
+        out[(1 - pz) * (planes + 1)] = ze[row]
+        out[pz * (planes + 1)] = zo[row]
 
 
 def forward_kernel(
-    pos, part, feat, ye, yo, ze, zo, w, bias, emb, ext, se, so, te, to
+    pos, part, feat, ze, zo, ye, yo, w, bias, lze, lzo, emb, ext, se, so, te, to
 ):
     planes, rows = emb.shape[0], emb.shape[1]
     pz, py = pos[0], pos[1]
     ext[1 : planes + 1, 1 : rows + 1] = feat[...]
-    fill_rim(ext, ye, yo, ze, zo, pz, py, planes, rows)
+    fill_rim(ext, ze, zo, ye, yo, pz, py)
     emb[1 : planes - 1, 1 : rows - 1] = part[1 : planes - 1, 1 : rows - 1]
 
     @pl.loop(0, planes, unroll=True)
@@ -201,8 +195,10 @@
             for i, value in conv_rows(ext, w, z, (y, y + 1)):
                 emb[z, i] = (value + bias[...]).astype(BF)
 
-    for out, high in ((se, 1 - pz), (so, pz)):
-        out[...] = emb[pl.ds(high * (planes - REACH), REACH)]
+    for out, labels, high in ((se, lze, 1 - pz), (so, lzo, pz)):
+        halo = emb[pl.ds(high * (planes - REACH), REACH)]
+        out[: REACH * rows] = halo.reshape(REACH * rows, *halo.shape[2:])
+        out[REACH * rows :] = labels[...]
     for out, high in ((te, 1 - py), (to, py)):
         part = pl.ds(high * (rows - REACH), REACH)
         out[:REACH] = emb[0, part]
@@ -210,16 +206,9 @@
         out[2 * REACH :] = emb[1 : planes - 1, high * (rows - 1)]
 
 
-def inner_kernel(pos, emb, lab, ze, zo, grad, loss, labz, widez):
+def inner_kernel(emb, lab, ae, ao, grad, loss):
     planes, rows = emb.shape[0], emb.shape[1]
     lanes = emb.shape[3]
-    pz = pos[0]
-    for halo, side in ((ze, 1 - pz), (zo, pz)):
-        widez[...] = halo[rows + 2 :].reshape(widez.shape).astype(F32)
-        for p in range(REACH):
-            at = 2 * rows * p
-            labz[side, p] = widez[at : at + rows] * 256.0 + widez[at + rows : at + 2 * rows]
-
     lane = lax.broadcasted_iota(jnp.int32, (rows, lanes), 1)
     loss[...] = jnp.zeros_like(loss)
 
@@ -270,7 +259,6 @@
     loss_in,
     ze,
     zo,
-    labz,
     fe,
     fo,
     ye,
@@ -285,6 +273,8 @@
     laby,
     wide,
     halos,
+    labz,
+    widez,
 ):
     planes, rows = emb.shape[0], emb.shape[1]
     pz, py = pos[0], pos[1]
@@ -299,6 +289,10 @@
             laby[side, z] = wide[at : at + REACH] * 256.0 + wide[at + REACH : at + 2 * REACH]
 
     for halo, is_high in ((ze, 1 - pz), (zo, pz)):
+        widez[...] = halo[REACH * rows :].reshape(widez.shape).astype(F32)
+        for p in range(REACH):
+            at = 2 * rows * p
+            labz[p] = widez[at : at + rows] * 256.0 + widez[at + rows : at + 2 * rows]
         weight = (is_high * pos[2]).astype(F32)
         for o in OFFSETS:
 
@@ -306,10 +300,10 @@
             def _(t):
                 p = t + is_high * (planes - o)
                 q = t + (1 - is_high) * (REACH - o)
-                other = halo[q].astype(F32)
+                other = halo[pl.ds(q * rows, rows)].astype(F32)
                 slopes, losses = pair_terms(
                     dots(emb[p].astype(F32), other),
-                    lab[p].astype(F32) == labz[is_high, q],
+                    lab[p].astype(F32) == labz[q],
                 )
                 grad[p] += slopes[:, None, :] * other
                 total[:rows] += losses * weight
@@ -365,8 +359,8 @@
         shifted[z, 2 : rows + 2, third : 2 * third] = value
         shifted[z, 2 : rows + 2, 2 * third :] = lane_shift(wide, -1).astype(BF)
 
-    ge[...] = out[:, (1 - py) * (rows - 1)]
-    go[...] = out[:, py * (rows - 1)]
+    ge[...] = out[(1 - pz) * (planes - 1)]
+    go[...] = out[pz * (planes - 1)]
     sums[...] = jnp.broadcast_to(jnp.sum(total[...], keepdims=True), sums.shape)
 
 
@@ -413,7 +407,7 @@
 def backward_kernel(pos, own, ye, yo, ze, zo, w, after, out, ext):
     planes, rows = own.shape[0], own.shape[1]
     ext[1 : planes + 1, 1 : rows + 1] = own[...]
-    fill_rim(ext, ye, yo, ze, zo, pos[0], pos[1], planes, rows)
+    fill_rim(ext, ze, zo, ye, yo, pos[0], pos[1])
 
     @pl.loop(0, planes, unroll=True)
     def _(z):
@@ -475,46 +469,49 @@
     z_blocks = -(-2 * REACH * rows // ch_in)
     y_blocks = -(-2 * REACH * planes // ch_in)
 
-    y_message = sds((planes,) + cells, BF)
+    z_message = sds((rows,) + cells, BF)
     me, mo = call(
-        first_kernel, (y_message, y_message), (pos, feat), [SM, HELD],
+        first_kernel,
+        (z_message, z_message),
+        (pos, feat),
+        [SM, pl.BlockSpec(memory_space=pltpu.HBM)],
         scratch=[pltpu.SemaphoreType.DMA((2,))],
     )
-    fye = lax.ppermute(me, "gy", y_even)
-    fyo = lax.ppermute(mo, "gy", y_odd)
+    fze = lax.ppermute(me, "gz", z_even)
+    fzo = lax.ppermute(mo, "gz", z_odd)
     emb_shape = sds((planes, rows) + tile, BF)
     ext_shape = sds((planes + 2, rows + 2) + cells, BF)
     y_early = sds(
         ((planes - 2) * (REACH - 1) + y_blocks * (ch_in // emb_ch),) + tile, BF
     )
-    emb_part, me, mo = call(
+    z_labels = sds((z_blocks * (ch_in // emb_ch),) + tile, BF)
+    emb_part, me, mo, lze, lzo = call(
         second_kernel,
-        (emb_shape, y_early, y_early),
+        (emb_shape, y_early, y_early, z_labels, z_labels),
         (pos, feat, labels, w_fwd, bias),
         [SM] + [VM] * 4,
-        scratch=[pltpu.VMEM((y_blocks * ch_in, lanes), F32)],
+        scratch=[
+            pltpu.VMEM((y_blocks * ch_in, lanes), F32),
+            pltpu.VMEM((z_blocks * ch_in, lanes), F32),
+        ],
         micros=3.4,
     )
     aye = lax.ppermute(me, "gy", y_even)
     ayo = lax.ppermute(mo, "gy", y_odd)
-    z_message = sds((rows + 2 + z_blocks,) + cells, BF)
+    y_message = sds((planes + 2,) + cells, BF)
     me, mo = call(
-        third_kernel,
-        (z_message, z_message),
-        (pos, feat, fye, fyo, labels, me),
-        [SM] + [VM] * 4 + [HELD],
-        scratch=[pltpu.VMEM((z_blocks * ch_in, lanes), F32)],
-    )
-    fze = lax.ppermute(me, "gz", z_even)
-    fzo = lax.ppermute(mo, "gz", z_odd)
-
-    z_halo = sds((REACH, rows) + tile, BF)
+        edge_rows, (y_message, y_message), (pos, feat, fze, fzo, me), [SM] + [VM] * 3 + [HELD]
+    )
+    fye = lax.ppermute(me, "gy", y_even)
+    fyo = lax.ppermute(mo, "gy", y_odd)
+
+    z_halo = sds((REACH * rows + z_labels.shape[0],) + tile, BF)
     y_late = sds((2 * REACH + planes - 2,) + tile, BF)
     emb, feat_ext, se, so, te, to = call(
         forward_kernel,
         (emb_shape, ext_shape, z_halo, z_halo, y_late, y_late),
-        (pos, emb_part, feat, fye, fyo, fze, fzo, w_fwd, bias),
-        [SM] + [VM] * 8,
+        (pos, emb_part, feat, fze, fzo, fye, fyo, w_fwd, bias, lze, lzo),
+        [SM] + [VM] * 10,
         micros=3.6,
     )
     eze = lax.ppermute(se, "gz", z_even)
@@ -525,40 +522,37 @@
     lost_rows = -(-rows // 8) * 8
     grad_shape = sds((planes, rows) + tile, F32)
     loss_shape = sds((lost_rows, lanes), F32)
-    grad_a, loss_a, labz = call(
+    grad_a, loss_a = call(
         inner_kernel,
-        (
-            grad_shape,
-            loss_shape,
-            sds((2, REACH, rows, lanes), F32),
-        ),
-        (pos, emb, labels, fze, fzo),
-        [SM] + [VM] * 4,
-        scratch=[pltpu.VMEM((z_blocks * ch_in, lanes), F32)],
-        micros=6.4,
+        (grad_shape, loss_shape),
+        (emb, labels, aye, ayo),
+        [VM] * 2 + [HELD] * 2,
+        micros=4.0,
     )
     grad, shifted, ge, go, lost = call(
         outer_kernel,
         (
             sds((planes, rows) + tile, BF),
             sds((planes, rows + 4, 3 * emb_ch, lanes), BF),
-            sds((planes,) + tile, BF),
-            sds((planes,) + tile, BF),
+            sds((rows,) + tile, BF),
+            sds((rows,) + tile, BF),
             sds((8, lanes), F32),
         ),
-        (pos, emb, labels, grad_a, loss_a, eze, ezo, labz, aye, ayo, eye, eyo),
-        [SM] + [VM] * 11,
+        (pos, emb, labels, grad_a, loss_a, eze, ezo, aye, ayo, eye, eyo),
+        [SM] + [VM] * 10,
         scratch=[
             pltpu.VMEM((planes, rows) + tile, F32),
             pltpu.VMEM((lost_rows, lanes), F32),
             pltpu.VMEM((2, planes, REACH, lanes), F32),
             pltpu.VMEM((y_blocks * ch_in, lanes), F32),
             pltpu.VMEM((2, planes, REACH) + tile, BF),
+            pltpu.VMEM((REACH, rows, lanes), F32),
+            pltpu.VMEM((z_blocks * ch_in, lanes), F32),
         ],
         micros=5.0,
     )
-    gye = lax.ppermute(ge, "gy", y_even)
-    gyo = lax.ppermute(go, "gy", y_odd)
+    gze = lax.ppermute(ge, "gz", z_even)
+    gzo = lax.ppermute(go, "gz", z_odd)
 
     used = 9 * emb_ch + 1
     padded = -(-used // (8 * gz)) * 8 * gz
@@ -571,10 +565,12 @@
         scratch=[pltpu.VMEM((9 * emb_ch, 3 * ch_in), F32)],
         micros=3.8,
     )
-    z_edge = sds((rows + 2,) + tile, BF)
-    me, mo = call(edge_planes, (z_edge, z_edge), (pos, grad, gye, gyo), [SM] + [VM] * 3)
-    gze = lax.ppermute(me, "gz", z_even)
-    gzo = lax.ppermute(mo, "gz", z_odd)
+    y_edge = sds((planes + 2,) + tile, BF)
+    me, mo = call(
+        edge_rows, (y_edge, y_edge), (pos, grad, gze, gzo, lost), [SM] + [VM] * 3 + [HELD]
+    )
+    gye = lax.ppermute(me, "gy", y_even)
+    gyo = lax.ppermute(mo, "gy", y_odd)
 
     parts = lax.all_to_all(partial.reshape(gz, share, lanes), "gz", 0, 0)
     mine = call(spread_kernel, sds((gy, share, lanes), F32), (parts,), [VM])

time: 109 us -> 105 us (0.963)
  starting transfers between devices: 74.2 us -> 63.9 us
  waiting for transfers between devices: 12 us -> 18.3 us
    ppermute x4, starting transfers between devices: 11.1 us -> 5.96 us  [the longest x1 3.44 us: per_device(): gzo = lax.ppermute(go, 'gz', z_odd)]
    all_to_all x1, waiting for transfers between devices: 0.01 us -> 4.46 us  [per_device(): parts = lax.all_to_all(partial.reshape(gz, share, lanes), 'gz', 0, 0)]
    all_to_all x1, starting transfers between devices: 8.96 us -> 6.82 us  [per_device(): parts = lax.all_to_all(partial.reshape(gz, share, lanes), 'gz', 0, 0)]
    ppermute x1, starting transfers between devices: 2.21 us -> 0.09 us  [per_device(): fye = lax.ppermute(me, 'gy', y_even)]
  transfers between devices with their start and end apart: 17 -> 17, of which waited for: 3 -> 5; matrix products, arithmetic and copies ran while one was open for 1% -> 1% of each run, Pallas kernels for 11% -> 11%
where the time goes in v3:
time: 105 us; the launch traced here: 104 us
  starting transfers between devices  63.9 us (61%)
  Pallas kernels  19.1 us (18%)
  waiting for transfers between devices  18.3 us (17%)
  local copies, waits for them, and re-layouts  1.77 us (2%)
    all_to_all x1, starting transfers between devices, per_device(): parts = lax.all_to_all(mine, 'gy', 0, 0)  21.9 us
    pallas_call x12, Pallas kernels, call(): pl.pallas_call(body, out_shape=outs, in_specs=specs, out_specs=jax.tree.m...  19.1 us
    ppermute x1, starting transfers between devices, per_device(): eye = lax.ppermute(te, 'gy', y_even)  9.46 us
    all_to_all x1, starting transfers between devices, per_device(): parts = lax.all_to_all(partial.reshape(gz, share, lanes), 'gz', 0, 0)  6.82 us
    all_to_all x1, waiting for transfers between devices, per_device(): parts = lax.all_to_all(mine, 'gy', 0, 0)  6.23 us
    all_to_all x1, waiting for transfers between devices, per_device(): total = lax.all_to_all(mine, 'gz', 0, 0).reshape(padded, lanes)  5.79 us
    all_to_all x1, starting transfers between devices, per_device(): total = lax.all_to_all(mine, 'gz', 0, 0).reshape(padded, lanes)  5.33 us
    all_to_all x1, waiting for transfers between devices, per_device(): parts = lax.all_to_all(partial.reshape(gz, share, lanes), 'gz', 0, 0)  4.46 us
  transfers between devices with their start and end apart: 17, of which 5 were waited for; matrix products, arithmetic and copies ran while one was open for 1% of the time, Pallas kernels for 11%

profile of v3, /device:TPU:1, one launch (start us, length us, event | category | flops | bytes accessed | tf_op | source)
XLA Modules:
  0.0 104.0 jit_solution(13871828688063023969)
XLA Ops:
  0.7 1.2 %copy-done = bf16[32,10,12,128]{3,0,2,1:T(8,128)(2,1)S(1)} copy-done((bf16[32,10,12,128]{3,0,2,1:T(8,128)(2,1)S(1)}, bf16[32,10,12,128]{3,0,2,1:T(8,128)(2,1)}, u32[]{:S(2)}) %copy-start) | copy-done | bytes 983064
  1.9 0.8 first_kernel.1
  2.8 3.3 %collective-permute-start = (bf16[12,32,128]{2,1,0:T(8,128)(2,1)S(1)}, bf16[12,32,128]{2,1,0:T(8,128)(2,1)S(1)}, u32[]{:S(2)}, u32[]{:S(2)}) collective-permute-start(bf16[12,32,128]{2,1,0:T(8,128)(2,1)S(1)} %get-tuple-element.32), channel_id=1, source_target_pairs={{0,8},{8,0},{16,24},{24,16},{32,40},{40,32},{48,56},{56,48},{64,72... | collective-permute-start | bytes 294920 | tf_op jit(solution)/shard_map/ppermute | solution.py:480
  6.1 1.9 %collective-permute-start.1 = (bf16[12,32,128]{2,1,0:T(8,128)(2,1)S(1)}, bf16[12,32,128]{2,1,0:T(8,128)(2,1)S(1)}, u32[]{:S(2)}, u32[]{:S(2)}) collective-permute-start(bf16[12,32,128]{2,1,0:T(8,128)(2,1)S(1)} %get-tuple-element.33), channel_id=1, source_target_pairs={{8,16},{24,32},{40,48},{56,64},{72,80},{88,96},{104,112},{120,128}... | collective-permute-start | bytes 294920 | tf_op jit(solution)/shard_map/ppermute | solution.py:481
  8.3 2.0 %second_kernel.1 = (bf16[10,12,16,128]{3,2,1,0:T(8,128)(2,1)S(1)}, bf16[76,16,128]{2,1,0:T(8,128)(2,1)S(1)}, bf16[76,16,128]{2,1,0:T(8,128)(2,1)S(1)}, bf16[14,1...) custom-call(s32[4]{0:T(128)S(1)} %pad_add_fusion.pos, bf16[10,12,32,128]{3,2,1,0:T(8,128)(2,1)S(1)} %bitcast.21, ...), custom_call_target="tpu_custom_call" | custom-call | flops 3910000128 | bytes 1 | tf_op jit(solution)/shard_map/second_kernel/pallas_call | solution.py:22
  10.3 1.7 %collective-permute-done.1.zo = bf16[12,32,128]{2,1,0:T(8,128)(2,1)S(1)} collective-permute-done((bf16[12,32,128]{2,1,0:T(8,128)(2,1)S(1)}, bf16[12,32,128]{2,1,0:T(8,128)(2,1)S(1)}, u32[]{:S(2)}, u32[]{:S(2)}) %collective-permute-start.1) | collective-permute-done | bytes 98336 | tf_op jit(solution)/shard_map/ppermute | solution.py:481
  13.4 3.2 %collective-permute-start.4 = (bf16[76,16,128]{2,1,0:T(8,128)(2,1)S(1)}, bf16[76,16,128]{2,1,0:T(8,128)(2,1)S(1)}, u32[]{:S(2)}, u32[]{:S(2)}) collective-permute-start(bf16[76,16,128]{2,1,0:T(8,128)(2,1)S(1)} %get-tuple-element.34.after), channel_id=1, source_target_pairs={{0,1},{1,0},{2,3},{3,2},{4,5},{5,4},{6,7},{7,6},{8,9},{9,8},{10,11... | collective-permute-start | bytes 933896 | tf_op jit(solution)/shard_map/ppermute | solution.py:499
  17.3 1.5 %forward_kernel.1 = (bf16[10,12,16,128]{3,2,1,0:T(8,128)(2,1)S(1)}, bf16[12,14,32,128]{3,2,1,0:T(8,128)(2,1)S(1)}, bf16[122,16,128]{2,1,0:T(8,128)(2,1)S(1)}, bf...) custom-call(s32[4]{0:T(128)S(1)} %pad_add_fusion.pos, ...), custom_call_target="tpu_custom_call" | custom-call | flops 4140000000 | bytes 1 | tf_op jit(solution)/shard_map/forward_kernel/pallas_call | solution.py:22
  18.9 3.8 %collective-permute-start.7 = (bf16[122,16,128]{2,1,0:T(8,128)(2,1)S(1)}, bf16[122,16,128]{2,1,0:T(8,128)(2,1)S(1)}, u32[]{:S(2)}, u32[]{:S(2)}) collective-permute-start(bf16[122,16,128]{2,1,0:T(8,128)(2,1)S(1)} %get-tuple-element.44), channel_id=1, source_target_pairs={{8,16},{24,32},{40,48},{56,64},{72,80},{88,96},{104,112},{120,128}... | collective-permute-start | bytes 1499144 | tf_op jit(solution)/shard_map/ppermute | solution.py:518
  22.7 9.5 %collective-permute-start.8 = (bf16[26,16,128]{2,1,0:T(8,128)(2,1)S(1)}, bf16[26,16,128]{2,1,0:T(8,128)(2,1)S(1)}, u32[]{:S(2)}, u32[]{:S(2)}) collective-permute-start(bf16[26,16,128]{2,1,0:T(8,128)(2,1)S(1)} %get-tuple-element.45), channel_id=1, source_target_pairs={{0,1},{1,0},{2,3},{3,2},{4,5},{5,4},{6,7},{7,6},{8,9},{9,8},{10,11... | collective-permute-start | bytes 319496 | tf_op jit(solution)/shard_map/ppermute | solution.py:519
  32.9 3.5 %inner_kernel.1 = (f32[10,12,16,128]{3,2,1,0:T(8,128)S(1)}, f32[16,128]{1,0:T(8,128)S(1)}) custom-call(bf16[10,12,16,128]{3,2,1,0:T(8,128)(2,1)S(1)} %get-tuple-element.39.emb, s32[10,12,128]{2,1,0:T(8,128)S(1)} %copy-done.2, bf16[76,16,128]{2,1,0:T(8,128)(2,1)S(1)} %collective-permute-done.4.ae.fe, bf16[76,16,128]{2,1,0:T(8,128)(2,1)S(1)} %collective-permute-done.5.ao.fo), custom_call_target="tpu_custom_call" | custom-call | flops 4600000000 | bytes 1 | tf_op jit(solution)/shard_map/inner_kernel/pallas_call | solution.py:22
  36.4 2.9 %outer_kernel.1 = (bf16[10,12,16,128]{3,2,1,0:T(8,128)(2,1)S(1)}, bf16[10,16,48,128]{3,2,1,0:T(8,128)(2,1)S(1)}, bf16[12,16,128]{2,1,0:T(8,128)(2,1)S(1)}, bf16[12,16,128]{2,1,0:T(8,128)(2,1)S(1)}, f32[8,128]{1,0:T(8,128)S(1)}) custom-call(s32[4]{0:T(128)S(1)} %pad_add_fusion.pos, bf16[10,12,16,128]{3,2,1,0:T(8,128)(2,1)S(1)} %get-tuple-element.39.emb, ...), custom_call_target="tpu_custom_call" | custom-call | flops 5750000128 | bytes 1 | tf_op jit(solution)/shard_map/outer_kernel/pallas_call | solution.py:22
  39.3 2.3 %weight_kernel.1 = f32[256,128]{1,0:T(8,128)} custom-call(bf16[10,16,48,128]{3,2,1,0:T(8,128)(2,1)S(1)} %get-tuple-element.53.shifted, bf16[12,14,32,128]{3,2,1,0:T(8,128)(2,1)S(1)} %get-tuple-element.54.ext, bf16[10,12,16,128]{3,2,1,0:T(8,128)(2,1)S(1)} %get-tuple-element.47.own, f32[8,128]{1,0:T(8,128)S(1)} %get-tuple-element.50.after.lost), custom_call_target="tpu_custom_call" | custom-call | flops 4369999872 | bytes 1 | tf_op jit(solution)/shard_map/weight_kernel/pallas_call | solution.py:22
  41.6 6.8 %all-to-all-start = ((f32[32,8,128]{2,1,0:T(8,128)}), f32[32,8,128]{2,1,0:T(8,128)S(1)}, u32[]{:S(2)}, u32[]{:S(2)}) async-start(f32[32,8,128]{2,1,0:T(8,128)} %bitcast.8), calls=%async_computation | async-start | bytes 262144 | tf_op jit(solution)/shard_map/all_to_all | solution.py:575
  49.1 3.4 %collective-permute-start.11 = (bf16[12,16,128]{2,1,0:T(8,128)(2,1)S(1)}, bf16[12,16,128]{2,1,0:T(8,128)(2,1)S(1)}, u32[]{:S(2)}, u32[]{:S(2)}) collective-permute-start(bf16[12,16,128]{2,1,0:T(8,128)(2,1)S(1)} %get-tuple-element.49), channel_id=1, source_target_pairs={{8,16},{24,32},{40,48},{56,64},{72,80},{88,96},{104,112},{120,128}... | collective-permute-start | bytes 147464 | tf_op jit(solution)/shard_map/ppermute | solution.py:555
  52.5 4.5 %all-to-all-done.parts = f32[32,8,128]{2,1,0:T(8,128)S(1)} async-done(((f32[32,8,128]{2,1,0:T(8,128)}), f32[32,8,128]{2,1,0:T(8,128)S(1)}, u32[]{:S(2)}, u32[]{:S(2)}) %all-to-all-start) | async-done | bytes 131104 | tf_op jit(solution)/shard_map/all_to_all | solution.py:575
  57.6 21.9 %all-to-all-start.1 = ((f32[8,8,128]{2,1,0:T(8,128)}), f32[8,8,128]{2,1,0:T(8,128)S(1)}, u32[]{:S(2)}, u32[]{:S(2)}) async-start(f32[8,8,128]{2,1,0:T(8,128)} %spread_kernel.2.after), calls=%async_computation.1 | async-start | bytes 65536 | tf_op jit(solution)/shard_map/all_to_all | solution.py:585
  80.1 1.5 %collective-permute-start.12 = (bf16[12,16,128]{2,1,0:T(8,128)(2,1)S(1)}, bf16[12,16,128]{2,1,0:T(8,128)(2,1)S(1)}, u32[]{:S(2)}, u32[]{:S(2)}) collective-permute-start(bf16[12,16,128]{2,1,0:T(8,128)(2,1)S(1)} %get-tuple-element.51), channel_id=1, source_target_pairs={{0,1},{1,0},{2,3},{3,2},{4,5},{5,4},{6,7},{7,6},{8,9},{9,8},{10,11... | collective-permute-start | bytes 147464 | tf_op jit(solution)/shard_map/ppermute | solution.py:572
  82.3 6.2 %all-to-all-done.1.parts = f32[8,8,128]{2,1,0:T(8,128)S(1)} async-done(((f32[8,8,128]{2,1,0:T(8,128)}), f32[8,8,128]{2,1,0:T(8,128)S(1)}, u32[]{:S(2)}, u32[]{:S(2)}) %all-to-all-start.1) | async-done | bytes 32800 | tf_op jit(solution)/shard_map/all_to_all | solution.py:585
  88.6 0.7 spread_kernel.3
  89.2 5.3 %all-to-all-start.2 = ((f32[32,8,128]{2,1,0:T(8,128)}), f32[32,8,128]{2,1,0:T(8,128)S(1)}, u32[]{:S(2)}, u32[]{:S(2)}) async-start(f32[32,8,128]{2,1,0:T(8,128)} %spread_kernel.3), calls=%async_computation.2 | async-start | bytes 262144 | tf_op jit(solution)/shard_map/all_to_all | solution.py:587
  94.6 2.8 %backward_kernel.1 = bf16[10,12,32,128]{3,2,1,0:T(8,128)(2,1)} custom-call(s32[4]{0:T(128)S(1)} %pad_add_fusion.pos, bf16[10,12,16,128]{3,2,1,0:T(8,128)(2,1)S(1)} %get-tuple-element.47.own, bf16[12,16,128]{2,1,0:T(8,128)(2,1)S(1)} %collective-permute-done.12.ye, bf16[12,16,128]{2,1,0:T(8,128)(2,1)S(1)} %collective-permute-done.13.yo, ...), custom_call_target="tpu_custom_call" | custom-call | flops 5634999808 | bytes 1 | tf_op jit(solution)/shard_map/backward_kernel/pallas_call | solution.py:22
  97.4 5.8 %all-to-all-done.2 = f32[32,8,128]{2,1,0:T(8,128)S(1)} async-done(((f32[32,8,128]{2,1,0:T(8,128)}), f32[32,8,128]{2,1,0:T(8,128)S(1)}, u32[]{:S(2)}, u32[]{:S(2)}) %all-to-all-start.2) | async-done | bytes 131104 | tf_op jit(solution)/shard_map/all_to_all | solution.py:587
  103.2 0.8 final_kernel.1
  (40 shorter events, 5.7 us)
Async XLA Ops:
  0.7 1.2 %copy-start = (bf16[32,10,12,128]{3,0,2,1:T(8,128)(2,1)S(1)}, bf16[32,10,12,128]{3,0,2,1:T(8,128)(2,1)}, u32[]{:S(2)}) copy-start(bf16[32,10,12,128]{3,0,2,1:T(8,128)(2,1)} %param.4) | copy-start | bytes 2949124
  1.9 6.1 %copy-start.3 = (bf16[16,32,3,3,3]{1,0,4,3,2:T(8,128)(2,1)S(1)}, bf16[16,32,3,3,3]{1,0,4,3,2:T(8,128)(2,1)}, u32[]{:S(2)}) copy-start(bf16[16,32,3,3,3]{1,0,4,3,2:T(8,128)(2,1)} %param.6) | copy-start | bytes 82948
  1.9 6.3 %copy-start.4 = (f32[16]{0:T(128)S(1)}, f32[16]{0:T(128)}, u32[]{:S(2)}) copy-start(f32[16]{0:T(128)} %param.7) | copy-start | bytes 196
  1.9 6.4 %copy-start.1 = (bf16[32,10,12,128]{3,0,2,1:T(8,128)(2,1)S(1)}, bf16[32,10,12,128]{3,0,2,1:T(8,128)(2,1)}, u32[]{:S(2)}) copy-start(bf16[32,10,12,128]{3,0,2,1:T(8,128)(2,1)} %param.4) | copy-start | bytes 2949124
  1.9 6.4 %copy-start.2 = (s32[10,12,128]{2,1,0:T(8,128)S(1)}, s32[10,12,128]{2,1,0:T(8,128)}, u32[]{:S(2)}) copy-start(s32[10,12,128]{2,1,0:T(8,128)} %lab.5) | copy-start | bytes 184324
  2.8 7.5 %collective-permute-start = (bf16[12,32,128]{2,1,0:T(8,128)(2,1)S(1)}, bf16[12,32,128]{2,1,0:T(8,128)(2,1)S(1)}, u32[]{:S(2)}, u32[]{:S(2)}) collective-permute-start(bf16[12,32,128]{2,1,0:T(8,128)(2,1)S(1)} %get-tuple-element.32), channel_id=1, source_target_pairs={{0,8},{8,0},{16,24},{24,16},{32,40},{40,32},{48,56},{56,48},{64,72... | collective-permute-start | bytes 294920 | tf_op jit(solution)/shard_map/ppermute | solution.py:480
  6.1 5.9 %collective-permute-start.1 = (bf16[12,32,128]{2,1,0:T(8,128)(2,1)S(1)}, bf16[12,32,128]{2,1,0:T(8,128)(2,1)S(1)}, u32[]{:S(2)}, u32[]{:S(2)}) collective-permute-start(bf16[12,32,128]{2,1,0:T(8,128)(2,1)S(1)} %get-tuple-element.33), channel_id=1, source_target_pairs={{8,16},{24,32},{40,48},{56,64},{72,80},{88,96},{104,112},{120,128}... | collective-permute-start | bytes 294920 | tf_op jit(solution)/shard_map/ppermute | solution.py:481
  12.6 4.7 %collective-permute-start.2 = (bf16[12,32,128]{2,1,0:T(8,128)(2,1)S(1)}, bf16[12,32,128]{2,1,0:T(8,128)(2,1)S(1)}, u32[]{:S(2)}, u32[]{:S(2)}) collective-permute-start(bf16[12,32,128]{2,1,0:T(8,128)(2,1)S(1)} %get-tuple-element.35), channel_id=1, source_target_pairs={{0,1},{1,0},{2,3},{3,2},{4,5},{5,4},{6,7},{7,6},{8,9},{9,8},{10,11... | collective-permute-start | bytes 294920 | tf_op jit(solution)/shard_map/ppermute | solution.py:505
  12.7 4.6 %collective-permute-start.3 = (bf16[12,32,128]{2,1,0:T(8,128)(2,1)S(1)}, bf16[12,32,128]{2,1,0:T(8,128)(2,1)S(1)}, u32[]{:S(2)}, u32[]{:S(2)}) collective-permute-start(bf16[12,32,128]{2,1,0:T(8,128)(2,1)S(1)} %get-tuple-element.36), channel_id=1, source_target_pairs={{1,2},{3,4},{5,6},{2,1},{4,3},{6,5},{9,10},{11,12},{13,14},{10,9},... | collective-permute-start | bytes 294920 | tf_op jit(solution)/shard_map/ppermute | solution.py:506
  13.4 18.8 %collective-permute-start.4 = (bf16[76,16,128]{2,1,0:T(8,128)(2,1)S(1)}, bf16[76,16,128]{2,1,0:T(8,128)(2,1)S(1)}, u32[]{:S(2)}, u32[]{:S(2)}) collective-permute-start(bf16[76,16,128]{2,1,0:T(8,128)(2,1)S(1)} %get-tuple-element.34.after), channel_id=1, source_target_pairs={{0,1},{1,0},{2,3},{3,2},{4,5},{5,4},{6,7},{7,6},{8,9},{9,8},{10,11... | collective-permute-start | bytes 933896 | tf_op jit(solution)/shard_map/ppermute | solution.py:499
  16.5 16.3 %collective-permute-start.5 = (bf16[76,16,128]{2,1,0:T(8,128)(2,1)S(1)}, bf16[76,16,128]{2,1,0:T(8,128)(2,1)S(1)}, u32[]{:S(2)}, u32[]{:S(2)}) collective-permute-start(bf16[76,16,128]{2,1,0:T(8,128)(2,1)S(1)} %get-tuple-element.40), channel_id=1, source_target_pairs={{1,2},{3,4},{5,6},{2,1},{4,3},{6,5},{9,10},{11,12},{13,14},{10,9},... | collective-permute-start | bytes 933896 | tf_op jit(solution)/shard_map/ppermute | solution.py:500
  18.8 17.6 %collective-permute-start.6 = (bf16[122,16,128]{2,1,0:T(8,128)(2,1)S(1)}, bf16[122,16,128]{2,1,0:T(8,128)(2,1)S(1)}, u32[]{:S(2)}, u32[]{:S(2)}) collective-permute-start(bf16[122,16,128]{2,1,0:T(8,128)(2,1)S(1)} %get-tuple-element.43), channel_id=1, source_target_pairs={{0,8},{8,0},{16,24},{24,16},{32,40},{40,32},{48,56},{56,48},{64,72... | collective-permute-start | bytes 1499144 | tf_op jit(solution)/shard_map/ppermute | solution.py:517
  18.9 17.5 %collective-permute-start.7 = (bf16[122,16,128]{2,1,0:T(8,128)(2,1)S(1)}, bf16[122,16,128]{2,1,0:T(8,128)(2,1)S(1)}, u32[]{:S(2)}, u32[]{:S(2)}) collective-permute-start(bf16[122,16,128]{2,1,0:T(8,128)(2,1)S(1)} %get-tuple-element.44), channel_id=1, source_target_pairs={{8,16},{24,32},{40,48},{56,64},{72,80},{88,96},{104,112},{120,128}... | collective-permute-start | bytes 1499144 | tf_op jit(solution)/shard_map/ppermute | solution.py:518
  22.7 13.6 %collective-permute-start.8 = (bf16[26,16,128]{2,1,0:T(8,128)(2,1)S(1)}, bf16[26,16,128]{2,1,0:T(8,128)(2,1)S(1)}, u32[]{:S(2)}, u32[]{:S(2)}) collective-permute-start(bf16[26,16,128]{2,1,0:T(8,128)(2,1)S(1)} %get-tuple-element.45), channel_id=1, source_target_pairs={{0,1},{1,0},{2,3},{3,2},{4,5},{5,4},{6,7},{7,6},{8,9},{9,8},{10,11... | collective-permute-start | bytes 319496 | tf_op jit(solution)/shard_map/ppermute | solution.py:519
  32.2 4.2 %collective-permute-start.9 = (bf16[26,16,128]{2,1,0:T(8,128)(2,1)S(1)}, bf16[26,16,128]{2,1,0:T(8,128)(2,1)S(1)}, u32[]{:S(2)}, u32[]{:S(2)}) collective-permute-start(bf16[26,16,128]{2,1,0:T(8,128)(2,1)S(1)} %get-tuple-element.46), channel_id=1, source_target_pairs={{1,2},{3,4},{5,6},{2,1},{4,3},{6,5},{9,10},{11,12},{13,14},{10,9},... | collective-permute-start | bytes 319496 | tf_op jit(solution)/shard_map/ppermute | solution.py:520
  41.6 15.4 %all-to-all-start = ((f32[32,8,128]{2,1,0:T(8,128)}), f32[32,8,128]{2,1,0:T(8,128)S(1)}, u32[]{:S(2)}, u32[]{:S(2)}) async-start(f32[32,8,128]{2,1,0:T(8,128)} %bitcast.8), calls=%async_computation | async-start | bytes 262144 | tf_op jit(solution)/shard_map/all_to_all | solution.py:575
  48.7 30.8 %collective-permute-start.10 = (bf16[12,16,128]{2,1,0:T(8,128)(2,1)S(1)}, bf16[12,16,128]{2,1,0:T(8,128)(2,1)S(1)}, u32[]{:S(2)}, u32[]{:S(2)}) collective-permute-start(bf16[12,16,128]{2,1,0:T(8,128)(2,1)S(1)} %get-tuple-element.48), channel_id=1, source_target_pairs={{0,8},{8,0},{16,24},{24,16},{32,40},{40,32},{48,56},{56,48},{64,72... | collective-permute-start | bytes 147464 | tf_op jit(solution)/shard_map/ppermute | solution.py:554
  49.1 30.5 %collective-permute-start.11 = (bf16[12,16,128]{2,1,0:T(8,128)(2,1)S(1)}, bf16[12,16,128]{2,1,0:T(8,128)(2,1)S(1)}, u32[]{:S(2)}, u32[]{:S(2)}) collective-permute-start(bf16[12,16,128]{2,1,0:T(8,128)(2,1)S(1)} %get-tuple-element.49), channel_id=1, source_target_pairs={{8,16},{24,32},{40,48},{56,64},{72,80},{88,96},{104,112},{120,128}... | collective-permute-start | bytes 147464 | tf_op jit(solution)/shard_map/ppermute | solution.py:555
  57.6 30.9 %all-to-all-start.1 = ((f32[8,8,128]{2,1,0:T(8,128)}), f32[8,8,128]{2,1,0:T(8,128)S(1)}, u32[]{:S(2)}, u32[]{:S(2)}) async-start(f32[8,8,128]{2,1,0:T(8,128)} %spread_kernel.2.after), calls=%async_computation.1 | async-start | bytes 65536 | tf_op jit(solution)/shard_map/all_to_all | solution.py:585
  80.1 14.4 %collective-permute-start.12 = (bf16[12,16,128]{2,1,0:T(8,128)(2,1)S(1)}, bf16[12,16,128]{2,1,0:T(8,128)(2,1)S(1)}, u32[]{:S(2)}, u32[]{:S(2)}) collective-permute-start(bf16[12,16,128]{2,1,0:T(8,128)(2,1)S(1)} %get-tuple-element.51), channel_id=1, source_target_pairs={{0,1},{1,0},{2,3},{3,2},{4,5},{5,4},{6,7},{7,6},{8,9},{9,8},{10,11... | collective-permute-start | bytes 147464 | tf_op jit(solution)/shard_map/ppermute | solution.py:572
  81.7 12.9 %collective-permute-start.13 = (bf16[12,16,128]{2,1,0:T(8,128)(2,1)S(1)}, bf16[12,16,128]{2,1,0:T(8,128)(2,1)S(1)}, u32[]{:S(2)}, u32[]{:S(2)}) collective-permute-start(bf16[12,16,128]{2,1,0:T(8,128)(2,1)S(1)} %get-tuple-element.52), channel_id=1, source_target_pairs={{1,2},{3,4},{5,6},{2,1},{4,3},{6,5},{9,10},{11,12},{13,14},{10,9},... | collective-permute-start | bytes 147464 | tf_op jit(solution)/shard_map/ppermute | solution.py:573
  89.2 14.0 %all-to-all-start.2 = ((f32[32,8,128]{2,1,0:T(8,128)}), f32[32,8,128]{2,1,0:T(8,128)S(1)}, u32[]{:S(2)}, u32[]{:S(2)}) async-start(f32[32,8,128]{2,1,0:T(8,128)} %spread_kernel.3), calls=%async_computation.2 | async-start | bytes 262144 | tf_op jit(solution)/shard_map/all_to_all | solution.py:587

commit v4 on v3

--- a/solution.py
+++ b/solution.py
@@ -251,43 +251,11 @@
             loss[:rows] += losses
 
 
-def outer_kernel(
-    pos,
-    emb,
-    lab,
-    grad_in,
-    loss_in,
-    ze,
-    zo,
-    fe,
-    fo,
-    ye,
-    yo,
-    out,
-    shifted,
-    ge,
-    go,
-    sums,
-    grad,
-    total,
-    laby,
-    wide,
-    halos,
-    labz,
-    widez,
-):
+def outer_z_kernel(pos, emb, lab, grad_in, loss_in, ze, zo, grad, total, labz, widez):
     planes, rows = emb.shape[0], emb.shape[1]
-    pz, py = pos[0], pos[1]
-    third = emb.shape[2]
-    cells = (planes - 2) * (REACH - 1)
+    pz = pos[0]
     grad[...] = grad_in[...]
     total[...] = loss_in[...]
-    for halo, side in ((fe, 1 - py), (fo, py)):
-        wide[...] = halo[cells:].reshape(wide.shape).astype(F32)
-        for z in range(planes):
-            at = 2 * REACH * z
-            laby[side, z] = wide[at : at + REACH] * 256.0 + wide[at + REACH : at + 2 * REACH]
-
     for halo, is_high in ((ze, 1 - pz), (zo, pz)):
         widez[...] = halo[REACH * rows :].reshape(widez.shape).astype(F32)
         for p in range(REACH):
@@ -307,6 +275,41 @@
                 )
                 grad[p] += slopes[:, None, :] * other
                 total[:rows] += losses * weight
+
+
+def outer_kernel(
+    pos,
+    emb,
+    lab,
+    grad,
+    loss_in,
+    fe,
+    fo,
+    ye,
+    yo,
+    ext,
+    out,
+    ge,
+    go,
+    packed,
+    shifted,
+    total,
+    laby,
+    wide,
+    halos,
+    acc,
+):
+    planes, rows = emb.shape[0], emb.shape[1]
+    pz, py = pos[0], pos[1]
+    channels, lanes = emb.shape[2], emb.shape[3]
+    third = channels
+    cells = (planes - 2) * (REACH - 1)
+    total[...] = loss_in[...]
+    for halo, side in ((fe, 1 - py), (fo, py)):
+        wide[...] = halo[cells:].reshape(wide.shape).astype(F32)
+        for z in range(planes):
+            at = 2 * REACH * z
+            laby[side, z] = wide[at : at + REACH] * 256.0 + wide[at + REACH : at + 2 * REACH]
 
     shifted[:, :2] = jnp.zeros((planes, 2) + shifted.shape[2:], BF)
     shifted[:, rows + 2 :] = jnp.zeros((planes, 2) + shifted.shape[2:], BF)
@@ -361,17 +364,12 @@
 
     ge[...] = out[(1 - pz) * (planes - 1)]
     go[...] = out[pz * (planes - 1)]
-    sums[...] = jnp.broadcast_to(jnp.sum(total[...], keepdims=True), sums.shape)
-
-
-def weight_kernel(shifted, ext, own, lost, out, acc):
-    planes, rows = own.shape[0], own.shape[1]
-    channels, lanes = own.shape[2], own.shape[3]
+
     acc[...] = jnp.zeros_like(acc)
 
     @pl.loop(0, planes, unroll=True)
     def _(z):
-        total = acc[...]
+        products = acc[...]
         for y in range(0, rows + 2, 2):
             left = jnp.concatenate(
                 [
@@ -387,21 +385,21 @@
                 ],
                 axis=1,
             )
-            total = total + lax.dot_general(
+            products = products + lax.dot_general(
                 left, right, (((1,), (1,)), ((), ())), preferred_element_type=F32
             )
-        acc[...] = total
+        acc[...] = products
 
     height, width = acc.shape
-    out[...] = jnp.zeros_like(out)
-    out[:height, :width] = acc[...]
-    tile = jnp.sum(own[...].astype(F32), axis=(0, 1))
+    packed[...] = jnp.zeros_like(packed)
+    packed[:height, :width] = acc[...]
+    tile = jnp.sum(out[...].astype(F32), axis=(0, 1))
     column = jnp.sum(tile, axis=1, keepdims=True)
     row = lax.broadcasted_iota(jnp.int32, (channels, lanes), 0)
     lane = lax.broadcasted_iota(jnp.int32, (channels, lanes), 1)
     line = jnp.sum(jnp.where(row == lane, column, 0.0), axis=0, keepdims=True)
     first = lax.broadcasted_iota(jnp.int32, (1, lanes), 1)
-    out[height : height + 1, :] = jnp.where(first == channels, lost[0:1, :], line)
+    packed[height : height + 1, :] = jnp.where(first == channels, jnp.sum(total[...], keepdims=True), line)
 
 
 def backward_kernel(pos, own, ye, yo, ze, zo, w, after, out, ext):
@@ -529,45 +527,46 @@
         [VM] * 2 + [HELD] * 2,
         micros=4.0,
     )
-    grad, shifted, ge, go, lost = call(
+    grad_b, loss_b = call(
+        outer_z_kernel,
+        (grad_shape, loss_shape),
+        (pos, emb, labels, grad_a, loss_a, eze, ezo),
+        [SM] + [VM] * 6,
+        scratch=[
+            pltpu.VMEM((REACH, rows, lanes), F32),
+            pltpu.VMEM((z_blocks * ch_in, lanes), F32),
+        ],
+        micros=1.5,
+    )
+    used = 9 * emb_ch + 1
+    padded = -(-used // (8 * gz)) * 8 * gz
+    share = padded // gz
+    grad, ge, go, partial = call(
         outer_kernel,
         (
             sds((planes, rows) + tile, BF),
-            sds((planes, rows + 4, 3 * emb_ch, lanes), BF),
             sds((rows,) + tile, BF),
             sds((rows,) + tile, BF),
-            sds((8, lanes), F32),
+            sds((padded, lanes), F32),
         ),
-        (pos, emb, labels, grad_a, loss_a, eze, ezo, aye, ayo, eye, eyo),
-        [SM] + [VM] * 10,
+        (pos, emb, labels, grad_b, loss_b, aye, ayo, eye, eyo, feat_ext),
+        [SM] + [VM] * 9,
         scratch=[
-            pltpu.VMEM((planes, rows) + tile, F32),
+            pltpu.VMEM((planes, rows + 4, 3 * emb_ch, lanes), BF),
             pltpu.VMEM((lost_rows, lanes), F32),
             pltpu.VMEM((2, planes, REACH, lanes), F32),
             pltpu.VMEM((y_blocks * ch_in, lanes), F32),
             pltpu.VMEM((2, planes, REACH) + tile, BF),
-            pltpu.VMEM((REACH, rows, lanes), F32),
-            pltpu.VMEM((z_blocks * ch_in, lanes), F32),
+            pltpu.VMEM((9 * emb_ch, 3 * ch_in), F32),
         ],
-        micros=5.0,
+        micros=3.7,
     )
     gze = lax.ppermute(ge, "gz", z_even)
     gzo = lax.ppermute(go, "gz", z_odd)
 
-    used = 9 * emb_ch + 1
-    padded = -(-used // (8 * gz)) * 8 * gz
-    share = padded // gz
-    partial = call(
-        weight_kernel,
-        sds((padded, lanes), F32),
-        (shifted, feat_ext, grad, lost),
-        [VM] * 4,
-        scratch=[pltpu.VMEM((9 * emb_ch, 3 * ch_in), F32)],
-        micros=3.8,
-    )
     y_edge = sds((planes + 2,) + tile, BF)
     me, mo = call(
-        edge_rows, (y_edge, y_edge), (pos, grad, gze, gzo, lost), [SM] + [VM] * 3 + [HELD]
+        edge_rows, (y_edge, y_edge), (pos, grad, gze, gzo, ge), [SM] + [VM] * 3 + [HELD]
     )
     gye = lax.ppermute(me, "gy", y_even)
     gyo = lax.ppermute(mo, "gy", y_odd)

time: 105 us -> 103 us (0.981)
  starting transfers between devices: 63.9 us -> 62.2 us
    all_to_all x1, starting transfers between devices: 21.9 us -> 20.3 us  [per_device(): parts = lax.all_to_all(mine, 'gy', 0, 0)]
  transfers between devices with their start and end apart: 17 -> 17, of which waited for: 5 -> 5; matrix products, arithmetic and copies ran while one was open for 1% -> 1% of each run, Pallas kernels for 11% -> 13%
where the time goes in v4:
time: 103 us; the launch traced here: 102 us
  starting transfers between devices  62.2 us (60%)
  Pallas kernels  19 us (18%)
  waiting for transfers between devices  18.3 us (18%)
  local copies, waits for them, and re-layouts  1.77 us (2%)
    all_to_all x1, starting transfers between devices, per_device(): parts = lax.all_to_all(mine, 'gy', 0, 0)  20.3 us
    pallas_call x12, Pallas kernels, call(): pl.pallas_call(body, out_shape=outs, in_specs=specs, out_specs=jax.tree.m...  19 us
    ppermute x1, starting transfers between devices, per_device(): eye = lax.ppermute(te, 'gy', y_even)  9.46 us
    all_to_all x1, starting transfers between devices, per_device(): parts = lax.all_to_all(partial.reshape(gz, share, lanes), 'gz', 0, 0)  6.82 us
    all_to_all x1, waiting for transfers between devices, per_device(): parts = lax.all_to_all(mine, 'gy', 0, 0)  6.23 us
    all_to_all x1, waiting for transfers between devices, per_device(): total = lax.all_to_all(mine, 'gz', 0, 0).reshape(padded, lanes)  5.8 us
    all_to_all x1, starting transfers between devices, per_device(): total = lax.all_to_all(mine, 'gz', 0, 0).reshape(padded, lanes)  5.33 us
    all_to_all x1, waiting for transfers between devices, per_device(): parts = lax.all_to_all(partial.reshape(gz, share, lanes), 'gz', 0, 0)  4.46 us
  transfers between devices with their start and end apart: 17, of which 5 were waited for; matrix products, arithmetic and copies ran while one was open for 1% of the time, Pallas kernels for 13%

profile of v4, /device:TPU:1, one launch (start us, length us, event | category | flops | bytes accessed | tf_op | source)
XLA Modules:
  0.0 102.3 jit_solution(13763101523644215755)
XLA Ops:
  0.7 1.2 %copy-done = bf16[32,10,12,128]{3,0,2,1:T(8,128)(2,1)S(1)} copy-done((bf16[32,10,12,128]{3,0,2,1:T(8,128)(2,1)S(1)}, bf16[32,10,12,128]{3,0,2,1:T(8,128)(2,1)}, u32[]{:S(2)}) %copy-start) | copy-done | bytes 983064
  1.9 0.8 first_kernel.1
  2.8 3.3 %collective-permute-start = (bf16[12,32,128]{2,1,0:T(8,128)(2,1)S(1)}, bf16[12,32,128]{2,1,0:T(8,128)(2,1)S(1)}, u32[]{:S(2)}, u32[]{:S(2)}) collective-permute-start(bf16[12,32,128]{2,1,0:T(8,128)(2,1)S(1)} %get-tuple-element.33), channel_id=1, source_target_pairs={{0,8},{8,0},{16,24},{24,16},{32,40},{40,32},{48,56},{56,48},{64,72... | collective-permute-start | bytes 294920 | tf_op jit(solution)/shard_map/ppermute | solution.py:478
  6.1 1.9 %collective-permute-start.1 = (bf16[12,32,128]{2,1,0:T(8,128)(2,1)S(1)}, bf16[12,32,128]{2,1,0:T(8,128)(2,1)S(1)}, u32[]{:S(2)}, u32[]{:S(2)}) collective-permute-start(bf16[12,32,128]{2,1,0:T(8,128)(2,1)S(1)} %get-tuple-element.34), channel_id=1, source_target_pairs={{8,16},{24,32},{40,48},{56,64},{72,80},{88,96},{104,112},{120,128}... | collective-permute-start | bytes 294920 | tf_op jit(solution)/shard_map/ppermute | solution.py:479
  8.3 2.0 %second_kernel.1 = (bf16[10,12,16,128]{3,2,1,0:T(8,128)(2,1)S(1)}, bf16[76,16,128]{2,1,0:T(8,128)(2,1)S(1)}, bf16[76,16,128]{2,1,0:T(8,128)(2,1)S(1)}, bf16[14,1...) custom-call(s32[4]{0:T(128)S(1)} %pad_add_fusion.pos, bf16[10,12,32,128]{3,2,1,0:T(8,128)(2,1)S(1)} %bitcast.21, ...), custom_call_target="tpu_custom_call" | custom-call | flops 3910000128 | bytes 1 | tf_op jit(solution)/shard_map/second_kernel/pallas_call | solution.py:22
  10.3 1.7 %collective-permute-done.1.zo = bf16[12,32,128]{2,1,0:T(8,128)(2,1)S(1)} collective-permute-done((bf16[12,32,128]{2,1,0:T(8,128)(2,1)S(1)}, bf16[12,32,128]{2,1,0:T(8,128)(2,1)S(1)}, u32[]{:S(2)}, u32[]{:S(2)}) %collective-permute-start.1) | collective-permute-done | bytes 98336 | tf_op jit(solution)/shard_map/ppermute | solution.py:479
  13.4 3.2 %collective-permute-start.4 = (bf16[76,16,128]{2,1,0:T(8,128)(2,1)S(1)}, bf16[76,16,128]{2,1,0:T(8,128)(2,1)S(1)}, u32[]{:S(2)}, u32[]{:S(2)}) collective-permute-start(bf16[76,16,128]{2,1,0:T(8,128)(2,1)S(1)} %get-tuple-element.35.after), channel_id=1, source_target_pairs={{0,1},{1,0},{2,3},{3,2},{4,5},{5,4},{6,7},{7,6},{8,9},{9,8},{10,11... | collective-permute-start | bytes 933896 | tf_op jit(solution)/shard_map/ppermute | solution.py:497
  17.3 1.5 %forward_kernel.1 = (bf16[10,12,16,128]{3,2,1,0:T(8,128)(2,1)S(1)}, bf16[12,14,32,128]{3,2,1,0:T(8,128)(2,1)S(1)}, bf16[122,16,128]{2,1,0:T(8,128)(2,1)S(1)}, bf...) custom-call(s32[4]{0:T(128)S(1)} %pad_add_fusion.pos, ...), custom_call_target="tpu_custom_call" | custom-call | flops 4140000000 | bytes 1 | tf_op jit(solution)/shard_map/forward_kernel/pallas_call | solution.py:22
  18.9 3.8 %collective-permute-start.7 = (bf16[122,16,128]{2,1,0:T(8,128)(2,1)S(1)}, bf16[122,16,128]{2,1,0:T(8,128)(2,1)S(1)}, u32[]{:S(2)}, u32[]{:S(2)}) collective-permute-start(bf16[122,16,128]{2,1,0:T(8,128)(2,1)S(1)} %get-tuple-element.45), channel_id=1, source_target_pairs={{8,16},{24,32},{40,48},{56,64},{72,80},{88,96},{104,112},{120,128}... | collective-permute-start | bytes 1499144 | tf_op jit(solution)/shard_map/ppermute | solution.py:516
  22.7 9.5 %collective-permute-start.8 = (bf16[26,16,128]{2,1,0:T(8,128)(2,1)S(1)}, bf16[26,16,128]{2,1,0:T(8,128)(2,1)S(1)}, u32[]{:S(2)}, u32[]{:S(2)}) collective-permute-start(bf16[26,16,128]{2,1,0:T(8,128)(2,1)S(1)} %get-tuple-element.48), channel_id=1, source_target_pairs={{0,1},{1,0},{2,3},{3,2},{4,5},{5,4},{6,7},{7,6},{8,9},{9,8},{10,11... | collective-permute-start | bytes 319496 | tf_op jit(solution)/shard_map/ppermute | solution.py:517
  32.9 3.5 %inner_kernel.1 = (f32[10,12,16,128]{3,2,1,0:T(8,128)S(1)}, f32[16,128]{1,0:T(8,128)S(1)}) custom-call(bf16[10,12,16,128]{3,2,1,0:T(8,128)(2,1)S(1)} %get-tuple-element.40.emb, s32[10,12,128]{2,1,0:T(8,128)S(1)} %copy-done.2, bf16[76,16,128]{2,1,0:T(8,128)(2,1)S(1)} %collective-permute-done.4.ae.fe, bf16[76,16,128]{2,1,0:T(8,128)(2,1)S(1)} %collective-permute-done.5.ao.fo), custom_call_target="tpu_custom_call" | custom-call | flops 4600000000 | bytes 1 | tf_op jit(solution)/shard_map/inner_kernel/pallas_call | solution.py:22
  36.4 1.7 %outer_z_kernel.1 = (f32[10,12,16,128]{3,2,1,0:T(8,128)S(1)}, f32[16,128]{1,0:T(8,128)S(1)}) custom-call(s32[4]{0:T(128)S(1)} %pad_add_fusion.pos, bf16[10,12,16,128]{3,2,1,0:T(8,128)(2,1)S(1)} %get-tuple-element.40.emb, s32[10,12,128]{2,1,0:T(8,128)S(1)} %copy-done.2, f32[10,12,16,128]{3,2,1,0:T(8,128)S(1)} %get-tuple-element.42.grad_in, ...), custom_call_target="tpu_custom_call" | custom-call | flops 1724999936 | bytes 1 | tf_op jit(solution)/shard_map/outer_z_kernel/pallas_call | solution.py:22
  38.1 3.5 %outer_kernel.1 = (bf16[10,12,16,128]{3,2,1,0:T(8,128)(2,1)S(1)}, bf16[12,16,128]{2,1,0:T(8,128)(2,1)S(1)}, bf16[12,16,128]{2,1,0:T(8,128)(2,1)S(1)}, f32[256,128]{1,0:T(8,128)}) custom-call(s32[4]{0:T(128)S(1)} %pad_add_fusion.pos, bf16[10,12,16,128]{3,2,1,0:T(8,128)(2,1)S(1)} %get-tuple-element.40.emb, s32[10,12,128]{2,1,0:T(8,128)S(1)} %copy-done.2, ...), custom_call_target="tpu_custom_call" | custom-call | flops 4255000064 | bytes 1 | tf_op jit(solution)/shard_map/outer_kernel/pallas_call | solution.py:22
  41.6 6.8 %all-to-all-start = ((f32[32,8,128]{2,1,0:T(8,128)}), f32[32,8,128]{2,1,0:T(8,128)S(1)}, u32[]{:S(2)}, u32[]{:S(2)}) async-start(f32[32,8,128]{2,1,0:T(8,128)} %bitcast.8), calls=%async_computation | async-start | bytes 262144 | tf_op jit(solution)/shard_map/all_to_all | solution.py:574
  49.0 3.4 %collective-permute-start.11 = (bf16[12,16,128]{2,1,0:T(8,128)(2,1)S(1)}, bf16[12,16,128]{2,1,0:T(8,128)(2,1)S(1)}, u32[]{:S(2)}, u32[]{:S(2)}) collective-permute-start(bf16[12,16,128]{2,1,0:T(8,128)(2,1)S(1)} %get-tuple-element.53), channel_id=1, source_target_pairs={{8,16},{24,32},{40,48},{56,64},{72,80},{88,96},{104,112},{120,128}... | collective-permute-start | bytes 147464 | tf_op jit(solution)/shard_map/ppermute | solution.py:565
  52.5 4.5 %all-to-all-done.parts = f32[32,8,128]{2,1,0:T(8,128)S(1)} async-done(((f32[32,8,128]{2,1,0:T(8,128)}), f32[32,8,128]{2,1,0:T(8,128)S(1)}, u32[]{:S(2)}, u32[]{:S(2)}) %all-to-all-start) | async-done | bytes 131104 | tf_op jit(solution)/shard_map/all_to_all | solution.py:574
  57.6 20.3 %all-to-all-start.1 = ((f32[8,8,128]{2,1,0:T(8,128)}), f32[8,8,128]{2,1,0:T(8,128)S(1)}, u32[]{:S(2)}, u32[]{:S(2)}) async-start(f32[8,8,128]{2,1,0:T(8,128)} %spread_kernel.2.after), calls=%async_computation.1 | async-start | bytes 65536 | tf_op jit(solution)/shard_map/all_to_all | solution.py:584
  78.4 1.5 %collective-permute-start.12 = (bf16[12,16,128]{2,1,0:T(8,128)(2,1)S(1)}, bf16[12,16,128]{2,1,0:T(8,128)(2,1)S(1)}, u32[]{:S(2)}, u32[]{:S(2)}) collective-permute-start(bf16[12,16,128]{2,1,0:T(8,128)(2,1)S(1)} %get-tuple-element.54), channel_id=1, source_target_pairs={{0,1},{1,0},{2,3},{3,2},{4,5},{5,4},{6,7},{7,6},{8,9},{9,8},{10,11... | collective-permute-start | bytes 147464 | tf_op jit(solution)/shard_map/ppermute | solution.py:571
  80.6 6.2 %all-to-all-done.1.parts = f32[8,8,128]{2,1,0:T(8,128)S(1)} async-done(((f32[8,8,128]{2,1,0:T(8,128)}), f32[8,8,128]{2,1,0:T(8,128)S(1)}, u32[]{:S(2)}, u32[]{:S(2)}) %all-to-all-start.1) | async-done | bytes 32800 | tf_op jit(solution)/shard_map/all_to_all | solution.py:584
  86.9 0.7 spread_kernel.3
  87.5 5.3 %all-to-all-start.2 = ((f32[32,8,128]{2,1,0:T(8,128)}), f32[32,8,128]{2,1,0:T(8,128)S(1)}, u32[]{:S(2)}, u32[]{:S(2)}) async-start(f32[32,8,128]{2,1,0:T(8,128)} %spread_kernel.3), calls=%async_computation.2 | async-start | bytes 262144 | tf_op jit(solution)/shard_map/all_to_all | solution.py:586
  92.9 2.8 %backward_kernel.1 = bf16[10,12,32,128]{3,2,1,0:T(8,128)(2,1)} custom-call(s32[4]{0:T(128)S(1)} %pad_add_fusion.pos, bf16[10,12,16,128]{3,2,1,0:T(8,128)(2,1)S(1)} %get-tuple-element.51.own, bf16[12,16,128]{2,1,0:T(8,128)(2,1)S(1)} %collective-permute-done.12.ye, bf16[12,16,128]{2,1,0:T(8,128)(2,1)S(1)} %collective-permute-done.13.yo, ...), custom_call_target="tpu_custom_call" | custom-call | flops 5634999808 | bytes 1 | tf_op jit(solution)/shard_map/backward_kernel/pallas_call | solution.py:22
  95.7 5.8 %all-to-all-done.2 = f32[32,8,128]{2,1,0:T(8,128)S(1)} async-done(((f32[32,8,128]{2,1,0:T(8,128)}), f32[32,8,128]{2,1,0:T(8,128)S(1)}, u32[]{:S(2)}, u32[]{:S(2)}) %all-to-all-start.2) | async-done | bytes 131104 | tf_op jit(solution)/shard_map/all_to_all | solution.py:586
  101.5 0.8 final_kernel.1
  (40 shorter events, 5.7 us)
Async XLA Ops:
  0.7 1.2 %copy-start = (bf16[32,10,12,128]{3,0,2,1:T(8,128)(2,1)S(1)}, bf16[32,10,12,128]{3,0,2,1:T(8,128)(2,1)}, u32[]{:S(2)}) copy-start(bf16[32,10,12,128]{3,0,2,1:T(8,128)(2,1)} %param.4) | copy-start | bytes 2949124
  1.9 6.1 %copy-start.3 = (bf16[16,32,3,3,3]{1,0,4,3,2:T(8,128)(2,1)S(1)}, bf16[16,32,3,3,3]{1,0,4,3,2:T(8,128)(2,1)}, u32[]{:S(2)}) copy-start(bf16[16,32,3,3,3]{1,0,4,3,2:T(8,128)(2,1)} %param.6) | copy-start | bytes 82948
  1.9 6.3 %copy-start.4 = (f32[16]{0:T(128)S(1)}, f32[16]{0:T(128)}, u32[]{:S(2)}) copy-start(f32[16]{0:T(128)} %param.7) | copy-start | bytes 196
  1.9 6.4 %copy-start.1 = (bf16[32,10,12,128]{3,0,2,1:T(8,128)(2,1)S(1)}, bf16[32,10,12,128]{3,0,2,1:T(8,128)(2,1)}, u32[]{:S(2)}) copy-start(bf16[32,10,12,128]{3,0,2,1:T(8,128)(2,1)} %param.4) | copy-start | bytes 2949124
  1.9 6.4 %copy-start.2 = (s32[10,12,128]{2,1,0:T(8,128)S(1)}, s32[10,12,128]{2,1,0:T(8,128)}, u32[]{:S(2)}) copy-start(s32[10,12,128]{2,1,0:T(8,128)} %lab.7) | copy-start | bytes 184324
  2.8 7.5 %collective-permute-start = (bf16[12,32,128]{2,1,0:T(8,128)(2,1)S(1)}, bf16[12,32,128]{2,1,0:T(8,128)(2,1)S(1)}, u32[]{:S(2)}, u32[]{:S(2)}) collective-permute-start(bf16[12,32,128]{2,1,0:T(8,128)(2,1)S(1)} %get-tuple-element.33), channel_id=1, source_target_pairs={{0,8},{8,0},{16,24},{24,16},{32,40},{40,32},{48,56},{56,48},{64,72... | collective-permute-start | bytes 294920 | tf_op jit(solution)/shard_map/ppermute | solution.py:478
  6.1 5.9 %collective-permute-start.1 = (bf16[12,32,128]{2,1,0:T(8,128)(2,1)S(1)}, bf16[12,32,128]{2,1,0:T(8,128)(2,1)S(1)}, u32[]{:S(2)}, u32[]{:S(2)}) collective-permute-start(bf16[12,32,128]{2,1,0:T(8,128)(2,1)S(1)} %get-tuple-element.34), channel_id=1, source_target_pairs={{8,16},{24,32},{40,48},{56,64},{72,80},{88,96},{104,112},{120,128}... | collective-permute-start | bytes 294920 | tf_op jit(solution)/shard_map/ppermute | solution.py:479
  12.6 4.7 %collective-permute-start.2 = (bf16[12,32,128]{2,1,0:T(8,128)(2,1)S(1)}, bf16[12,32,128]{2,1,0:T(8,128)(2,1)S(1)}, u32[]{:S(2)}, u32[]{:S(2)}) collective-permute-start(bf16[12,32,128]{2,1,0:T(8,128)(2,1)S(1)} %get-tuple-element.36), channel_id=1, source_target_pairs={{0,1},{1,0},{2,3},{3,2},{4,5},{5,4},{6,7},{7,6},{8,9},{9,8},{10,11... | collective-permute-start | bytes 294920 | tf_op jit(solution)/shard_map/ppermute | solution.py:503
  12.7 4.6 %collective-permute-start.3 = (bf16[12,32,128]{2,1,0:T(8,128)(2,1)S(1)}, bf16[12,32,128]{2,1,0:T(8,128)(2,1)S(1)}, u32[]{:S(2)}, u32[]{:S(2)}) collective-permute-start(bf16[12,32,128]{2,1,0:T(8,128)(2,1)S(1)} %get-tuple-element.37), channel_id=1, source_target_pairs={{1,2},{3,4},{5,6},{2,1},{4,3},{6,5},{9,10},{11,12},{13,14},{10,9},... | collective-permute-start | bytes 294920 | tf_op jit(solution)/shard_map/ppermute | solution.py:504
  13.4 18.8 %collective-permute-start.4 = (bf16[76,16,128]{2,1,0:T(8,128)(2,1)S(1)}, bf16[76,16,128]{2,1,0:T(8,128)(2,1)S(1)}, u32[]{:S(2)}, u32[]{:S(2)}) collective-permute-start(bf16[76,16,128]{2,1,0:T(8,128)(2,1)S(1)} %get-tuple-element.35.after), channel_id=1, source_target_pairs={{0,1},{1,0},{2,3},{3,2},{4,5},{5,4},{6,7},{7,6},{8,9},{9,8},{10,11... | collective-permute-start | bytes 933896 | tf_op jit(solution)/shard_map/ppermute | solution.py:497
  16.5 16.3 %collective-permute-start.5 = (bf16[76,16,128]{2,1,0:T(8,128)(2,1)S(1)}, bf16[76,16,128]{2,1,0:T(8,128)(2,1)S(1)}, u32[]{:S(2)}, u32[]{:S(2)}) collective-permute-start(bf16[76,16,128]{2,1,0:T(8,128)(2,1)S(1)} %get-tuple-element.41), channel_id=1, source_target_pairs={{1,2},{3,4},{5,6},{2,1},{4,3},{6,5},{9,10},{11,12},{13,14},{10,9},... | collective-permute-start | bytes 933896 | tf_op jit(solution)/shard_map/ppermute | solution.py:498
  18.8 17.6 %collective-permute-start.6 = (bf16[122,16,128]{2,1,0:T(8,128)(2,1)S(1)}, bf16[122,16,128]{2,1,0:T(8,128)(2,1)S(1)}, u32[]{:S(2)}, u32[]{:S(2)}) collective-permute-start(bf16[122,16,128]{2,1,0:T(8,128)(2,1)S(1)} %get-tuple-element.44), channel_id=1, source_target_pairs={{0,8},{8,0},{16,24},{24,16},{32,40},{40,32},{48,56},{56,48},{64,72... | collective-permute-start | bytes 1499144 | tf_op jit(solution)/shard_map/ppermute | solution.py:515
  18.9 17.5 %collective-permute-start.7 = (bf16[122,16,128]{2,1,0:T(8,128)(2,1)S(1)}, bf16[122,16,128]{2,1,0:T(8,128)(2,1)S(1)}, u32[]{:S(2)}, u32[]{:S(2)}) collective-permute-start(bf16[122,16,128]{2,1,0:T(8,128)(2,1)S(1)} %get-tuple-element.45), channel_id=1, source_target_pairs={{8,16},{24,32},{40,48},{56,64},{72,80},{88,96},{104,112},{120,128}... | collective-permute-start | bytes 1499144 | tf_op jit(solution)/shard_map/ppermute | solution.py:516
  22.7 15.3 %collective-permute-start.8 = (bf16[26,16,128]{2,1,0:T(8,128)(2,1)S(1)}, bf16[26,16,128]{2,1,0:T(8,128)(2,1)S(1)}, u32[]{:S(2)}, u32[]{:S(2)}) collective-permute-start(bf16[26,16,128]{2,1,0:T(8,128)(2,1)S(1)} %get-tuple-element.48), channel_id=1, source_target_pairs={{0,1},{1,0},{2,3},{3,2},{4,5},{5,4},{6,7},{7,6},{8,9},{9,8},{10,11... | collective-permute-start | bytes 319496 | tf_op jit(solution)/shard_map/ppermute | solution.py:517
  32.2 5.9 %collective-permute-start.9 = (bf16[26,16,128]{2,1,0:T(8,128)(2,1)S(1)}, bf16[26,16,128]{2,1,0:T(8,128)(2,1)S(1)}, u32[]{:S(2)}, u32[]{:S(2)}) collective-permute-start(bf16[26,16,128]{2,1,0:T(8,128)(2,1)S(1)} %get-tuple-element.49), channel_id=1, source_target_pairs={{1,2},{3,4},{5,6},{2,1},{4,3},{6,5},{9,10},{11,12},{13,14},{10,9},... | collective-permute-start | bytes 319496 | tf_op jit(solution)/shard_map/ppermute | solution.py:518
  41.6 15.4 %all-to-all-start = ((f32[32,8,128]{2,1,0:T(8,128)}), f32[32,8,128]{2,1,0:T(8,128)S(1)}, u32[]{:S(2)}, u32[]{:S(2)}) async-start(f32[32,8,128]{2,1,0:T(8,128)} %bitcast.8), calls=%async_computation | async-start | bytes 262144 | tf_op jit(solution)/shard_map/all_to_all | solution.py:574
  48.7 29.1 %collective-permute-start.10 = (bf16[12,16,128]{2,1,0:T(8,128)(2,1)S(1)}, bf16[12,16,128]{2,1,0:T(8,128)(2,1)S(1)}, u32[]{:S(2)}, u32[]{:S(2)}) collective-permute-start(bf16[12,16,128]{2,1,0:T(8,128)(2,1)S(1)} %get-tuple-element.52.after), channel_id=1, source_target_pairs={{0,8},{8,0},{16,24},{24,16},{32,40},{40,32},{48,56},{56,48},{64,72... | collective-permute-start | bytes 147464 | tf_op jit(solution)/shard_map/ppermute | solution.py:564
  49.0 28.8 %collective-permute-start.11 = (bf16[12,16,128]{2,1,0:T(8,128)(2,1)S(1)}, bf16[12,16,128]{2,1,0:T(8,128)(2,1)S(1)}, u32[]{:S(2)}, u32[]{:S(2)}) collective-permute-start(bf16[12,16,128]{2,1,0:T(8,128)(2,1)S(1)} %get-tuple-element.53), channel_id=1, source_target_pairs={{8,16},{24,32},{40,48},{56,64},{72,80},{88,96},{104,112},{120,128}... | collective-permute-start | bytes 147464 | tf_op jit(solution)/shard_map/ppermute | solution.py:565
  57.6 29.3 %all-to-all-start.1 = ((f32[8,8,128]{2,1,0:T(8,128)}), f32[8,8,128]{2,1,0:T(8,128)S(1)}, u32[]{:S(2)}, u32[]{:S(2)}) async-start(f32[8,8,128]{2,1,0:T(8,128)} %spread_kernel.2.after), calls=%async_computation.1 | async-start | bytes 65536 | tf_op jit(solution)/shard_map/all_to_all | solution.py:584
  78.4 14.4 %collective-permute-start.12 = (bf16[12,16,128]{2,1,0:T(8,128)(2,1)S(1)}, bf16[12,16,128]{2,1,0:T(8,128)(2,1)S(1)}, u32[]{:S(2)}, u32[]{:S(2)}) collective-permute-start(bf16[12,16,128]{2,1,0:T(8,128)(2,1)S(1)} %get-tuple-element.54), channel_id=1, source_target_pairs={{0,1},{1,0},{2,3},{3,2},{4,5},{5,4},{6,7},{7,6},{8,9},{9,8},{10,11... | collective-permute-start | bytes 147464 | tf_op jit(solution)/shard_map/ppermute | solution.py:571
  80.0 12.9 %collective-permute-start.13 = (bf16[12,16,128]{2,1,0:T(8,128)(2,1)S(1)}, bf16[12,16,128]{2,1,0:T(8,128)(2,1)S(1)}, u32[]{:S(2)}, u32[]{:S(2)}) collective-permute-start(bf16[12,16,128]{2,1,0:T(8,128)(2,1)S(1)} %get-tuple-element.55), channel_id=1, source_target_pairs={{1,2},{3,4},{5,6},{2,1},{4,3},{6,5},{9,10},{11,12},{13,14},{10,9},... | collective-permute-start | bytes 147464 | tf_op jit(solution)/shard_map/ppermute | solution.py:572
  87.5 14.0 %all-to-all-start.2 = ((f32[32,8,128]{2,1,0:T(8,128)}), f32[32,8,128]{2,1,0:T(8,128)S(1)}, u32[]{:S(2)}, u32[]{:S(2)}) async-start(f32[32,8,128]{2,1,0:T(8,128)} %spread_kernel.3), calls=%async_computation.2 | async-start | bytes 262144 | tf_op jit(solution)/shard_map/all_to_all | solution.py:586

commit v5 on v4

--- a/solution.py
+++ b/solution.py
@@ -56,7 +56,7 @@
     inverse = 1.0 / (1.0 + small)
     sigmoid = jnp.where(logits >= 0, inverse, small * inverse)
     slopes = (sigmoid - target) * 0.25
-    losses = jnp.maximum(logits, 0.0) + jnp.log(1.0 + small) - target * logits
+    losses = jnp.maximum(logits, 0.0) + jnp.log1p(small) - target * logits
     return slopes, losses
 
 

time: 103 us -> 103 us (level)
  no operation moved by 1% of the time
where the time goes in v5:
time: 103 us; the launch traced here: 102 us
  starting transfers between devices  62.1 us (60%)
  Pallas kernels  19.2 us (19%)
  waiting for transfers between devices  18.3 us (18%)
  local copies, waits for them, and re-layouts  1.77 us (2%)
    all_to_all x1, starting transfers between devices, per_device(): parts = lax.all_to_all(mine, 'gy', 0, 0)  20.1 us
    pallas_call x12, Pallas kernels, call(): pl.pallas_call(body, out_shape=outs, in_specs=specs, out_specs=jax.tree.m...  19.2 us
    ppermute x1, starting transfers between devices, per_device(): eye = lax.ppermute(te, 'gy', y_even)  9.46 us
    all_to_all x1, starting transfers between devices, per_device(): parts = lax.all_to_all(partial.reshape(gz, share, lanes), 'gz', 0, 0)  6.82 us
    all_to_all x1, waiting for transfers between devices, per_device(): parts = lax.all_to_all(mine, 'gy', 0, 0)  6.23 us
    all_to_all x1, waiting for transfers between devices, per_device(): total = lax.all_to_all(mine, 'gz', 0, 0).reshape(padded, lanes)  5.79 us
    all_to_all x1, starting transfers between devices, per_device(): total = lax.all_to_all(mine, 'gz', 0, 0).reshape(padded, lanes)  5.33 us
    all_to_all x1, waiting for transfers between devices, per_device(): parts = lax.all_to_all(partial.reshape(gz, share, lanes), 'gz', 0, 0)  4.46 us
  transfers between devices with their start and end apart: 17, of which 5 were waited for; matrix products, arithmetic and copies ran while one was open for 1% of the time, Pallas kernels for 13%

profile of v5, /device:TPU:1, one launch (start us, length us, event | category | flops | bytes accessed | tf_op | source)
XLA Modules:
  0.0 102.3 jit_solution(17239600267343819088)
XLA Ops:
  0.7 1.2 %copy-done = bf16[32,10,12,128]{3,0,2,1:T(8,128)(2,1)S(1)} copy-done((bf16[32,10,12,128]{3,0,2,1:T(8,128)(2,1)S(1)}, bf16[32,10,12,128]{3,0,2,1:T(8,128)(2,1)}, u32[]{:S(2)}) %copy-start) | copy-done | bytes 983064
  1.9 0.8 first_kernel.1
  2.8 3.3 %collective-permute-start = (bf16[12,32,128]{2,1,0:T(8,128)(2,1)S(1)}, bf16[12,32,128]{2,1,0:T(8,128)(2,1)S(1)}, u32[]{:S(2)}, u32[]{:S(2)}) collective-permute-start(bf16[12,32,128]{2,1,0:T(8,128)(2,1)S(1)} %get-tuple-element.33), channel_id=1, source_target_pairs={{0,8},{8,0},{16,24},{24,16},{32,40},{40,32},{48,56},{56,48},{64,72... | collective-permute-start | bytes 294920 | tf_op jit(solution)/shard_map/ppermute | solution.py:478
  6.1 1.9 %collective-permute-start.1 = (bf16[12,32,128]{2,1,0:T(8,128)(2,1)S(1)}, bf16[12,32,128]{2,1,0:T(8,128)(2,1)S(1)}, u32[]{:S(2)}, u32[]{:S(2)}) collective-permute-start(bf16[12,32,128]{2,1,0:T(8,128)(2,1)S(1)} %get-tuple-element.34), channel_id=1, source_target_pairs={{8,16},{24,32},{40,48},{56,64},{72,80},{88,96},{104,112},{120,128}... | collective-permute-start | bytes 294920 | tf_op jit(solution)/shard_map/ppermute | solution.py:479
  8.3 2.0 %second_kernel.1 = (bf16[10,12,16,128]{3,2,1,0:T(8,128)(2,1)S(1)}, bf16[76,16,128]{2,1,0:T(8,128)(2,1)S(1)}, bf16[76,16,128]{2,1,0:T(8,128)(2,1)S(1)}, bf16[14,1...) custom-call(s32[4]{0:T(128)S(1)} %pad_add_fusion.pos, bf16[10,12,32,128]{3,2,1,0:T(8,128)(2,1)S(1)} %bitcast.21, ...), custom_call_target="tpu_custom_call" | custom-call | flops 3910000128 | bytes 1 | tf_op jit(solution)/shard_map/second_kernel/pallas_call | solution.py:22
  10.3 1.7 %collective-permute-done.1.zo = bf16[12,32,128]{2,1,0:T(8,128)(2,1)S(1)} collective-permute-done((bf16[12,32,128]{2,1,0:T(8,128)(2,1)S(1)}, bf16[12,32,128]{2,1,0:T(8,128)(2,1)S(1)}, u32[]{:S(2)}, u32[]{:S(2)}) %collective-permute-start.1) | collective-permute-done | bytes 98336 | tf_op jit(solution)/shard_map/ppermute | solution.py:479
  13.4 3.2 %collective-permute-start.4 = (bf16[76,16,128]{2,1,0:T(8,128)(2,1)S(1)}, bf16[76,16,128]{2,1,0:T(8,128)(2,1)S(1)}, u32[]{:S(2)}, u32[]{:S(2)}) collective-permute-start(bf16[76,16,128]{2,1,0:T(8,128)(2,1)S(1)} %get-tuple-element.35.after), channel_id=1, source_target_pairs={{0,1},{1,0},{2,3},{3,2},{4,5},{5,4},{6,7},{7,6},{8,9},{9,8},{10,11... | collective-permute-start | bytes 933896 | tf_op jit(solution)/shard_map/ppermute | solution.py:497
  17.3 1.5 %forward_kernel.1 = (bf16[10,12,16,128]{3,2,1,0:T(8,128)(2,1)S(1)}, bf16[12,14,32,128]{3,2,1,0:T(8,128)(2,1)S(1)}, bf16[122,16,128]{2,1,0:T(8,128)(2,1)S(1)}, bf...) custom-call(s32[4]{0:T(128)S(1)} %pad_add_fusion.pos, ...), custom_call_target="tpu_custom_call" | custom-call | flops 4140000000 | bytes 1 | tf_op jit(solution)/shard_map/forward_kernel/pallas_call | solution.py:22
  18.9 3.8 %collective-permute-start.7 = (bf16[122,16,128]{2,1,0:T(8,128)(2,1)S(1)}, bf16[122,16,128]{2,1,0:T(8,128)(2,1)S(1)}, u32[]{:S(2)}, u32[]{:S(2)}) collective-permute-start(bf16[122,16,128]{2,1,0:T(8,128)(2,1)S(1)} %get-tuple-element.45), channel_id=1, source_target_pairs={{8,16},{24,32},{40,48},{56,64},{72,80},{88,96},{104,112},{120,128}... | collective-permute-start | bytes 1499144 | tf_op jit(solution)/shard_map/ppermute | solution.py:516
  22.7 9.5 %collective-permute-start.8 = (bf16[26,16,128]{2,1,0:T(8,128)(2,1)S(1)}, bf16[26,16,128]{2,1,0:T(8,128)(2,1)S(1)}, u32[]{:S(2)}, u32[]{:S(2)}) collective-permute-start(bf16[26,16,128]{2,1,0:T(8,128)(2,1)S(1)} %get-tuple-element.48), channel_id=1, source_target_pairs={{0,1},{1,0},{2,3},{3,2},{4,5},{5,4},{6,7},{7,6},{8,9},{9,8},{10,11... | collective-permute-start | bytes 319496 | tf_op jit(solution)/shard_map/ppermute | solution.py:517
  32.9 3.6 %inner_kernel.1 = (f32[10,12,16,128]{3,2,1,0:T(8,128)S(1)}, f32[16,128]{1,0:T(8,128)S(1)}) custom-call(bf16[10,12,16,128]{3,2,1,0:T(8,128)(2,1)S(1)} %get-tuple-element.40.emb, s32[10,12,128]{2,1,0:T(8,128)S(1)} %copy-done.2, bf16[76,16,128]{2,1,0:T(8,128)(2,1)S(1)} %collective-permute-done.4.ae.fe, bf16[76,16,128]{2,1,0:T(8,128)(2,1)S(1)} %collective-permute-done.5.ao.fo), custom_call_target="tpu_custom_call" | custom-call | flops 4600000000 | bytes 1 | tf_op jit(solution)/shard_map/inner_kernel/pallas_call | solution.py:22
  36.5 1.7 %outer_z_kernel.1 = (f32[10,12,16,128]{3,2,1,0:T(8,128)S(1)}, f32[16,128]{1,0:T(8,128)S(1)}) custom-call(s32[4]{0:T(128)S(1)} %pad_add_fusion.pos, bf16[10,12,16,128]{3,2,1,0:T(8,128)(2,1)S(1)} %get-tuple-element.40.emb, s32[10,12,128]{2,1,0:T(8,128)S(1)} %copy-done.2, f32[10,12,16,128]{3,2,1,0:T(8,128)S(1)} %get-tuple-element.42.grad_in, ...), custom_call_target="tpu_custom_call" | custom-call | flops 1724999936 | bytes 1 | tf_op jit(solution)/shard_map/outer_z_kernel/pallas_call | solution.py:22
  38.2 3.5 %outer_kernel.1 = (bf16[10,12,16,128]{3,2,1,0:T(8,128)(2,1)S(1)}, bf16[12,16,128]{2,1,0:T(8,128)(2,1)S(1)}, bf16[12,16,128]{2,1,0:T(8,128)(2,1)S(1)}, f32[256,128]{1,0:T(8,128)}) custom-call(s32[4]{0:T(128)S(1)} %pad_add_fusion.pos, bf16[10,12,16,128]{3,2,1,0:T(8,128)(2,1)S(1)} %get-tuple-element.40.emb, s32[10,12,128]{2,1,0:T(8,128)S(1)} %copy-done.2, ...), custom_call_target="tpu_custom_call" | custom-call | flops 4255000064 | bytes 1 | tf_op jit(solution)/shard_map/outer_kernel/pallas_call | solution.py:22
  41.7 6.8 %all-to-all-start = ((f32[32,8,128]{2,1,0:T(8,128)}), f32[32,8,128]{2,1,0:T(8,128)S(1)}, u32[]{:S(2)}, u32[]{:S(2)}) async-start(f32[32,8,128]{2,1,0:T(8,128)} %bitcast.8), calls=%async_computation | async-start | bytes 262144 | tf_op jit(solution)/shard_map/all_to_all | solution.py:574
  49.2 3.4 %collective-permute-start.11 = (bf16[12,16,128]{2,1,0:T(8,128)(2,1)S(1)}, bf16[12,16,128]{2,1,0:T(8,128)(2,1)S(1)}, u32[]{:S(2)}, u32[]{:S(2)}) collective-permute-start(bf16[12,16,128]{2,1,0:T(8,128)(2,1)S(1)} %get-tuple-element.53), channel_id=1, source_target_pairs={{8,16},{24,32},{40,48},{56,64},{72,80},{88,96},{104,112},{120,128}... | collective-permute-start | bytes 147464 | tf_op jit(solution)/shard_map/ppermute | solution.py:565
  52.6 4.5 %all-to-all-done.parts = f32[32,8,128]{2,1,0:T(8,128)S(1)} async-done(((f32[32,8,128]{2,1,0:T(8,128)}), f32[32,8,128]{2,1,0:T(8,128)S(1)}, u32[]{:S(2)}, u32[]{:S(2)}) %all-to-all-start) | async-done | bytes 131104 | tf_op jit(solution)/shard_map/all_to_all | solution.py:574
  57.7 20.1 %all-to-all-start.1 = ((f32[8,8,128]{2,1,0:T(8,128)}), f32[8,8,128]{2,1,0:T(8,128)S(1)}, u32[]{:S(2)}, u32[]{:S(2)}) async-start(f32[8,8,128]{2,1,0:T(8,128)} %spread_kernel.2.after), calls=%async_computation.1 | async-start | bytes 65536 | tf_op jit(solution)/shard_map/all_to_all | solution.py:584
  78.4 1.5 %collective-permute-start.12 = (bf16[12,16,128]{2,1,0:T(8,128)(2,1)S(1)}, bf16[12,16,128]{2,1,0:T(8,128)(2,1)S(1)}, u32[]{:S(2)}, u32[]{:S(2)}) collective-permute-start(bf16[12,16,128]{2,1,0:T(8,128)(2,1)S(1)} %get-tuple-element.54), channel_id=1, source_target_pairs={{0,1},{1,0},{2,3},{3,2},{4,5},{5,4},{6,7},{7,6},{8,9},{9,8},{10,11... | collective-permute-start | bytes 147464 | tf_op jit(solution)/shard_map/ppermute | solution.py:571
  80.6 6.2 %all-to-all-done.1.parts = f32[8,8,128]{2,1,0:T(8,128)S(1)} async-done(((f32[8,8,128]{2,1,0:T(8,128)}), f32[8,8,128]{2,1,0:T(8,128)S(1)}, u32[]{:S(2)}, u32[]{:S(2)}) %all-to-all-start.1) | async-done | bytes 32800 | tf_op jit(solution)/shard_map/all_to_all | solution.py:584
  86.9 0.7 spread_kernel.3
  87.5 5.3 %all-to-all-start.2 = ((f32[32,8,128]{2,1,0:T(8,128)}), f32[32,8,128]{2,1,0:T(8,128)S(1)}, u32[]{:S(2)}, u32[]{:S(2)}) async-start(f32[32,8,128]{2,1,0:T(8,128)} %spread_kernel.3), calls=%async_computation.2 | async-start | bytes 262144 | tf_op jit(solution)/shard_map/all_to_all | solution.py:586
  92.9 2.8 %backward_kernel.1 = bf16[10,12,32,128]{3,2,1,0:T(8,128)(2,1)} custom-call(s32[4]{0:T(128)S(1)} %pad_add_fusion.pos, bf16[10,12,16,128]{3,2,1,0:T(8,128)(2,1)S(1)} %get-tuple-element.51.own, bf16[12,16,128]{2,1,0:T(8,128)(2,1)S(1)} %collective-permute-done.12.ye, bf16[12,16,128]{2,1,0:T(8,128)(2,1)S(1)} %collective-permute-done.13.yo, ...), custom_call_target="tpu_custom_call" | custom-call | flops 5634999808 | bytes 1 | tf_op jit(solution)/shard_map/backward_kernel/pallas_call | solution.py:22
  95.7 5.8 %all-to-all-done.2 = f32[32,8,128]{2,1,0:T(8,128)S(1)} async-done(((f32[32,8,128]{2,1,0:T(8,128)}), f32[32,8,128]{2,1,0:T(8,128)S(1)}, u32[]{:S(2)}, u32[]{:S(2)}) %all-to-all-start.2) | async-done | bytes 131104 | tf_op jit(solution)/shard_map/all_to_all | solution.py:586
  101.5 0.8 final_kernel.1
  (40 shorter events, 5.7 us)
Async XLA Ops:
  0.7 1.2 %copy-start = (bf16[32,10,12,128]{3,0,2,1:T(8,128)(2,1)S(1)}, bf16[32,10,12,128]{3,0,2,1:T(8,128)(2,1)}, u32[]{:S(2)}) copy-start(bf16[32,10,12,128]{3,0,2,1:T(8,128)(2,1)} %param.4) | copy-start | bytes 2949124
  1.9 6.1 %copy-start.3 = (bf16[16,32,3,3,3]{1,0,4,3,2:T(8,128)(2,1)S(1)}, bf16[16,32,3,3,3]{1,0,4,3,2:T(8,128)(2,1)}, u32[]{:S(2)}) copy-start(bf16[16,32,3,3,3]{1,0,4,3,2:T(8,128)(2,1)} %param.6) | copy-start | bytes 82948
  1.9 6.3 %copy-start.4 = (f32[16]{0:T(128)S(1)}, f32[16]{0:T(128)}, u32[]{:S(2)}) copy-start(f32[16]{0:T(128)} %param.7) | copy-start | bytes 196
  1.9 6.4 %copy-start.1 = (bf16[32,10,12,128]{3,0,2,1:T(8,128)(2,1)S(1)}, bf16[32,10,12,128]{3,0,2,1:T(8,128)(2,1)}, u32[]{:S(2)}) copy-start(bf16[32,10,12,128]{3,0,2,1:T(8,128)(2,1)} %param.4) | copy-start | bytes 2949124
  1.9 6.4 %copy-start.2 = (s32[10,12,128]{2,1,0:T(8,128)S(1)}, s32[10,12,128]{2,1,0:T(8,128)}, u32[]{:S(2)}) copy-start(s32[10,12,128]{2,1,0:T(8,128)} %lab.7) | copy-start | bytes 184324
  2.8 7.5 %collective-permute-start = (bf16[12,32,128]{2,1,0:T(8,128)(2,1)S(1)}, bf16[12,32,128]{2,1,0:T(8,128)(2,1)S(1)}, u32[]{:S(2)}, u32[]{:S(2)}) collective-permute-start(bf16[12,32,128]{2,1,0:T(8,128)(2,1)S(1)} %get-tuple-element.33), channel_id=1, source_target_pairs={{0,8},{8,0},{16,24},{24,16},{32,40},{40,32},{48,56},{56,48},{64,72... | collective-permute-start | bytes 294920 | tf_op jit(solution)/shard_map/ppermute | solution.py:478
  6.1 5.9 %collective-permute-start.1 = (bf16[12,32,128]{2,1,0:T(8,128)(2,1)S(1)}, bf16[12,32,128]{2,1,0:T(8,128)(2,1)S(1)}, u32[]{:S(2)}, u32[]{:S(2)}) collective-permute-start(bf16[12,32,128]{2,1,0:T(8,128)(2,1)S(1)} %get-tuple-element.34), channel_id=1, source_target_pairs={{8,16},{24,32},{40,48},{56,64},{72,80},{88,96},{104,112},{120,128}... | collective-permute-start | bytes 294920 | tf_op jit(solution)/shard_map/ppermute | solution.py:479
  12.6 4.7 %collective-permute-start.2 = (bf16[12,32,128]{2,1,0:T(8,128)(2,1)S(1)}, bf16[12,32,128]{2,1,0:T(8,128)(2,1)S(1)}, u32[]{:S(2)}, u32[]{:S(2)}) collective-permute-start(bf16[12,32,128]{2,1,0:T(8,128)(2,1)S(1)} %get-tuple-element.36), channel_id=1, source_target_pairs={{0,1},{1,0},{2,3},{3,2},{4,5},{5,4},{6,7},{7,6},{8,9},{9,8},{10,11... | collective-permute-start | bytes 294920 | tf_op jit(solution)/shard_map/ppermute | solution.py:503
  12.7 4.6 %collective-permute-start.3 = (bf16[12,32,128]{2,1,0:T(8,128)(2,1)S(1)}, bf16[12,32,128]{2,1,0:T(8,128)(2,1)S(1)}, u32[]{:S(2)}, u32[]{:S(2)}) collective-permute-start(bf16[12,32,128]{2,1,0:T(8,128)(2,1)S(1)} %get-tuple-element.37), channel_id=1, source_target_pairs={{1,2},{3,4},{5,6},{2,1},{4,3},{6,5},{9,10},{11,12},{13,14},{10,9},... | collective-permute-start | bytes 294920 | tf_op jit(solution)/shard_map/ppermute | solution.py:504
  13.4 18.8 %collective-permute-start.4 = (bf16[76,16,128]{2,1,0:T(8,128)(2,1)S(1)}, bf16[76,16,128]{2,1,0:T(8,128)(2,1)S(1)}, u32[]{:S(2)}, u32[]{:S(2)}) collective-permute-start(bf16[76,16,128]{2,1,0:T(8,128)(2,1)S(1)} %get-tuple-element.35.after), channel_id=1, source_target_pairs={{0,1},{1,0},{2,3},{3,2},{4,5},{5,4},{6,7},{7,6},{8,9},{9,8},{10,11... | collective-permute-start | bytes 933896 | tf_op jit(solution)/shard_map/ppermute | solution.py:497
  16.5 16.3 %collective-permute-start.5 = (bf16[76,16,128]{2,1,0:T(8,128)(2,1)S(1)}, bf16[76,16,128]{2,1,0:T(8,128)(2,1)S(1)}, u32[]{:S(2)}, u32[]{:S(2)}) collective-permute-start(bf16[76,16,128]{2,1,0:T(8,128)(2,1)S(1)} %get-tuple-element.41), channel_id=1, source_target_pairs={{1,2},{3,4},{5,6},{2,1},{4,3},{6,5},{9,10},{11,12},{13,14},{10,9},... | collective-permute-start | bytes 933896 | tf_op jit(solution)/shard_map/ppermute | solution.py:498
  18.8 17.7 %collective-permute-start.6 = (bf16[122,16,128]{2,1,0:T(8,128)(2,1)S(1)}, bf16[122,16,128]{2,1,0:T(8,128)(2,1)S(1)}, u32[]{:S(2)}, u32[]{:S(2)}) collective-permute-start(bf16[122,16,128]{2,1,0:T(8,128)(2,1)S(1)} %get-tuple-element.44), channel_id=1, source_target_pairs={{0,8},{8,0},{16,24},{24,16},{32,40},{40,32},{48,56},{56,48},{64,72... | collective-permute-start | bytes 1499144 | tf_op jit(solution)/shard_map/ppermute | solution.py:515
  18.9 17.6 %collective-permute-start.7 = (bf16[122,16,128]{2,1,0:T(8,128)(2,1)S(1)}, bf16[122,16,128]{2,1,0:T(8,128)(2,1)S(1)}, u32[]{:S(2)}, u32[]{:S(2)}) collective-permute-start(bf16[122,16,128]{2,1,0:T(8,128)(2,1)S(1)} %get-tuple-element.45), channel_id=1, source_target_pairs={{8,16},{24,32},{40,48},{56,64},{72,80},{88,96},{104,112},{120,128}... | collective-permute-start | bytes 1499144 | tf_op jit(solution)/shard_map/ppermute | solution.py:516
  22.7 15.5 %collective-permute-start.8 = (bf16[26,16,128]{2,1,0:T(8,128)(2,1)S(1)}, bf16[26,16,128]{2,1,0:T(8,128)(2,1)S(1)}, u32[]{:S(2)}, u32[]{:S(2)}) collective-permute-start(bf16[26,16,128]{2,1,0:T(8,128)(2,1)S(1)} %get-tuple-element.48), channel_id=1, source_target_pairs={{0,1},{1,0},{2,3},{3,2},{4,5},{5,4},{6,7},{7,6},{8,9},{9,8},{10,11... | collective-permute-start | bytes 319496 | tf_op jit(solution)/shard_map/ppermute | solution.py:517
  32.2 6.0 %collective-permute-start.9 = (bf16[26,16,128]{2,1,0:T(8,128)(2,1)S(1)}, bf16[26,16,128]{2,1,0:T(8,128)(2,1)S(1)}, u32[]{:S(2)}, u32[]{:S(2)}) collective-permute-start(bf16[26,16,128]{2,1,0:T(8,128)(2,1)S(1)} %get-tuple-element.49), channel_id=1, source_target_pairs={{1,2},{3,4},{5,6},{2,1},{4,3},{6,5},{9,10},{11,12},{13,14},{10,9},... | collective-permute-start | bytes 319496 | tf_op jit(solution)/shard_map/ppermute | solution.py:518
  41.7 15.4 %all-to-all-start = ((f32[32,8,128]{2,1,0:T(8,128)}), f32[32,8,128]{2,1,0:T(8,128)S(1)}, u32[]{:S(2)}, u32[]{:S(2)}) async-start(f32[32,8,128]{2,1,0:T(8,128)} %bitcast.8), calls=%async_computation | async-start | bytes 262144 | tf_op jit(solution)/shard_map/all_to_all | solution.py:574
  48.8 29.0 %collective-permute-start.10 = (bf16[12,16,128]{2,1,0:T(8,128)(2,1)S(1)}, bf16[12,16,128]{2,1,0:T(8,128)(2,1)S(1)}, u32[]{:S(2)}, u32[]{:S(2)}) collective-permute-start(bf16[12,16,128]{2,1,0:T(8,128)(2,1)S(1)} %get-tuple-element.52.after), channel_id=1, source_target_pairs={{0,8},{8,0},{16,24},{24,16},{32,40},{40,32},{48,56},{56,48},{64,72... | collective-permute-start | bytes 147464 | tf_op jit(solution)/shard_map/ppermute | solution.py:564
  49.2 28.7 %collective-permute-start.11 = (bf16[12,16,128]{2,1,0:T(8,128)(2,1)S(1)}, bf16[12,16,128]{2,1,0:T(8,128)(2,1)S(1)}, u32[]{:S(2)}, u32[]{:S(2)}) collective-permute-start(bf16[12,16,128]{2,1,0:T(8,128)(2,1)S(1)} %get-tuple-element.53), channel_id=1, source_target_pairs={{8,16},{24,32},{40,48},{56,64},{72,80},{88,96},{104,112},{120,128}... | collective-permute-start | bytes 147464 | tf_op jit(solution)/shard_map/ppermute | solution.py:565
  57.7 29.2 %all-to-all-start.1 = ((f32[8,8,128]{2,1,0:T(8,128)}), f32[8,8,128]{2,1,0:T(8,128)S(1)}, u32[]{:S(2)}, u32[]{:S(2)}) async-start(f32[8,8,128]{2,1,0:T(8,128)} %spread_kernel.2.after), calls=%async_computation.1 | async-start | bytes 65536 | tf_op jit(solution)/shard_map/all_to_all | solution.py:584
  78.4 14.4 %collective-permute-start.12 = (bf16[12,16,128]{2,1,0:T(8,128)(2,1)S(1)}, bf16[12,16,128]{2,1,0:T(8,128)(2,1)S(1)}, u32[]{:S(2)}, u32[]{:S(2)}) collective-permute-start(bf16[12,16,128]{2,1,0:T(8,128)(2,1)S(1)} %get-tuple-element.54), channel_id=1, source_target_pairs={{0,1},{1,0},{2,3},{3,2},{4,5},{5,4},{6,7},{7,6},{8,9},{9,8},{10,11... | collective-permute-start | bytes 147464 | tf_op jit(solution)/shard_map/ppermute | solution.py:571
  80.0 12.9 %collective-permute-start.13 = (bf16[12,16,128]{2,1,0:T(8,128)(2,1)S(1)}, bf16[12,16,128]{2,1,0:T(8,128)(2,1)S(1)}, u32[]{:S(2)}, u32[]{:S(2)}) collective-permute-start(bf16[12,16,128]{2,1,0:T(8,128)(2,1)S(1)} %get-tuple-element.55), channel_id=1, source_target_pairs={{1,2},{3,4},{5,6},{2,1},{4,3},{6,5},{9,10},{11,12},{13,14},{10,9},... | collective-permute-start | bytes 147464 | tf_op jit(solution)/shard_map/ppermute | solution.py:572
  87.5 14.0 %all-to-all-start.2 = ((f32[32,8,128]{2,1,0:T(8,128)}), f32[32,8,128]{2,1,0:T(8,128)S(1)}, u32[]{:S(2)}, u32[]{:S(2)}) async-start(f32[32,8,128]{2,1,0:T(8,128)} %spread_kernel.3), calls=%async_computation.2 | async-start | bytes 262144 | tf_op jit(solution)/shard_map/all_to_all | solution.py:586

commit v6 on v5

--- a/solution.py
+++ b/solution.py
@@ -175,7 +175,7 @@
 
 
 def forward_kernel(
-    pos, part, feat, ze, zo, ye, yo, w, bias, lze, lzo, emb, ext, se, so, te, to
+    pos, part, feat, ze, zo, yo, ye, w, bias, lze, lzo, emb, ext, se, so, te, to
 ):
     planes, rows = emb.shape[0], emb.shape[1]
     pz, py = pos[0], pos[1]
@@ -206,7 +206,7 @@
         out[2 * REACH :] = emb[1 : planes - 1, high * (rows - 1)]
 
 
-def inner_kernel(emb, lab, ae, ao, grad, loss):
+def inner_kernel(emb, lab, ao, ae, grad, loss):
     planes, rows = emb.shape[0], emb.shape[1]
     lanes = emb.shape[3]
     lane = lax.broadcasted_iota(jnp.int32, (rows, lanes), 1)
@@ -283,10 +283,10 @@
     lab,
     grad,
     loss_in,
+    fo,
     fe,
-    fo,
+    yo,
     ye,
-    yo,
     ext,
     out,
     ge,
@@ -402,7 +402,7 @@
     packed[height : height + 1, :] = jnp.where(first == channels, jnp.sum(total[...], keepdims=True), line)
 
 
-def backward_kernel(pos, own, ye, yo, ze, zo, w, after, out, ext):
+def backward_kernel(pos, own, yo, ye, ze, zo, w, after, out, ext):
     planes, rows = own.shape[0], own.shape[1]
     ext[1 : planes + 1, 1 : rows + 1] = own[...]
     fill_rim(ext, ze, zo, ye, yo, pos[0], pos[1])
@@ -508,7 +508,7 @@
     emb, feat_ext, se, so, te, to = call(
         forward_kernel,
         (emb_shape, ext_shape, z_halo, z_halo, y_late, y_late),
-        (pos, emb_part, feat, fze, fzo, fye, fyo, w_fwd, bias, lze, lzo),
+        (pos, emb_part, feat, fze, fzo, fyo, fye, w_fwd, bias, lze, lzo),
         [SM] + [VM] * 10,
         micros=3.6,
     )
@@ -523,7 +523,7 @@
     grad_a, loss_a = call(
         inner_kernel,
         (grad_shape, loss_shape),
-        (emb, labels, aye, ayo),
+        (emb, labels, ayo, aye),
         [VM] * 2 + [HELD] * 2,
         micros=4.0,
     )
@@ -549,7 +549,7 @@
             sds((rows,) + tile, BF),
             sds((padded, lanes), F32),
         ),
-        (pos, emb, labels, grad_b, loss_b, aye, ayo, eye, eyo, feat_ext),
+        (pos, emb, labels, grad_b, loss_b, ayo, aye, eyo, eye, feat_ext),
         [SM] + [VM] * 9,
         scratch=[
             pltpu.VMEM((planes, rows + 4, 3 * emb_ch, lanes), BF),
@@ -576,7 +576,7 @@
     feature_grad = call(
         backward_kernel,
         sds((planes, rows) + cells, BF),
-        (pos, grad, gye, gyo, gze, gzo, w_bwd, mine),
+        (pos, grad, gyo, gye, gze, gzo, w_bwd, mine),
         [SM] + [VM] * 6 + [HELD],
         scratch=[pltpu.VMEM((planes + 2, rows + 2) + tile, BF)],
         micros=4.9,

time: 103 us -> 103 us (level)
    ppermute x1, starting transfers between devices: 3.16 us -> 0.1 us  [per_device(): aye = lax.ppermute(me, 'gy', y_even)]
    all_to_all x1, waiting for transfers between devices: 6.23 us -> 3.79 us  [per_device(): parts = lax.all_to_all(mine, 'gy', 0, 0)]
    ppermute x1, starting transfers between devices: 1.54 us -> 3.97 us  [per_device(): gye = lax.ppermute(me, 'gy', y_even)]
    ppermute x1, waiting for transfers between devices: 0.07 us -> 2.48 us  [per_device(): fye = lax.ppermute(me, 'gy', y_even)]
    ppermute x1, starting transfers between devices: 0.09 us -> 2.19 us  [per_device(): fye = lax.ppermute(me, 'gy', y_even)]
    all_to_all x1, starting transfers between devices: 20.1 us -> 18.8 us  [per_device(): parts = lax.all_to_all(mine, 'gy', 0, 0)]
where the time goes in v6:
time: 103 us; the launch traced here: 102 us
  starting transfers between devices  62 us (60%)
  Pallas kernels  19.2 us (19%)
  waiting for transfers between devices  18.3 us (18%)
  local copies, waits for them, and re-layouts  1.77 us (2%)
    pallas_call x12, Pallas kernels, call(): pl.pallas_call(body, out_shape=outs, in_specs=specs, out_specs=jax.tree.m...  19.2 us
    all_to_all x1, starting transfers between devices, per_device(): parts = lax.all_to_all(mine, 'gy', 0, 0)  18.8 us
    ppermute x1, starting transfers between devices, per_device(): eye = lax.ppermute(te, 'gy', y_even)  8.9 us
    all_to_all x1, starting transfers between devices, per_device(): parts = lax.all_to_all(partial.reshape(gz, share, lanes), 'gz', 0, 0)  7.14 us
    all_to_all x1, waiting for transfers between devices, per_device(): total = lax.all_to_all(mine, 'gz', 0, 0).reshape(padded, lanes)  5.79 us
    all_to_all x1, starting transfers between devices, per_device(): total = lax.all_to_all(mine, 'gz', 0, 0).reshape(padded, lanes)  5.33 us
    all_to_all x1, waiting for transfers between devices, per_device(): parts = lax.all_to_all(partial.reshape(gz, share, lanes), 'gz', 0, 0)  4.46 us
    ppermute x1, starting transfers between devices, per_device(): gye = lax.ppermute(me, 'gy', y_even)  3.97 us
  transfers between devices with their start and end apart: 17, of which 5 were waited for; matrix products, arithmetic and copies ran while one was open for 1% of the time, Pallas kernels for 13%

profile of v6, /device:TPU:1, one launch (start us, length us, event | category | flops | bytes accessed | tf_op | source)
XLA Modules:
  0.0 102.2 jit_solution(2047968233189129570)
XLA Ops:
  0.7 1.2 %copy-done = bf16[32,10,12,128]{3,0,2,1:T(8,128)(2,1)S(1)} copy-done((bf16[32,10,12,128]{3,0,2,1:T(8,128)(2,1)S(1)}, bf16[32,10,12,128]{3,0,2,1:T(8,128)(2,1)}, u32[]{:S(2)}) %copy-start) | copy-done | bytes 983064
  1.9 0.8 first_kernel.1
  2.8 3.3 %collective-permute-start = (bf16[12,32,128]{2,1,0:T(8,128)(2,1)S(1)}, bf16[12,32,128]{2,1,0:T(8,128)(2,1)S(1)}, u32[]{:S(2)}, u32[]{:S(2)}) collective-permute-start(bf16[12,32,128]{2,1,0:T(8,128)(2,1)S(1)} %get-tuple-element.33), channel_id=1, source_target_pairs={{0,8},{8,0},{16,24},{24,16},{32,40},{40,32},{48,56},{56,48},{64,72... | collective-permute-start | bytes 294920 | tf_op jit(solution)/shard_map/ppermute | solution.py:478
  6.1 1.9 %collective-permute-start.1 = (bf16[12,32,128]{2,1,0:T(8,128)(2,1)S(1)}, bf16[12,32,128]{2,1,0:T(8,128)(2,1)S(1)}, u32[]{:S(2)}, u32[]{:S(2)}) collective-permute-start(bf16[12,32,128]{2,1,0:T(8,128)(2,1)S(1)} %get-tuple-element.34), channel_id=1, source_target_pairs={{8,16},{24,32},{40,48},{56,64},{72,80},{88,96},{104,112},{120,128}... | collective-permute-start | bytes 294920 | tf_op jit(solution)/shard_map/ppermute | solution.py:479
  8.3 2.0 %second_kernel.1 = (bf16[10,12,16,128]{3,2,1,0:T(8,128)(2,1)S(1)}, bf16[76,16,128]{2,1,0:T(8,128)(2,1)S(1)}, bf16[76,16,128]{2,1,0:T(8,128)(2,1)S(1)}, bf16[14,1...) custom-call(s32[4]{0:T(128)S(1)} %pad_add_fusion.pos, bf16[10,12,32,128]{3,2,1,0:T(8,128)(2,1)S(1)} %bitcast.21, ...), custom_call_target="tpu_custom_call" | custom-call | flops 3910000128 | bytes 1 | tf_op jit(solution)/shard_map/second_kernel/pallas_call | solution.py:22
  10.3 1.7 %collective-permute-done.1.zo = bf16[12,32,128]{2,1,0:T(8,128)(2,1)S(1)} collective-permute-done((bf16[12,32,128]{2,1,0:T(8,128)(2,1)S(1)}, bf16[12,32,128]{2,1,0:T(8,128)(2,1)S(1)}, u32[]{:S(2)}, u32[]{:S(2)}) %collective-permute-start.1) | collective-permute-done | bytes 98336 | tf_op jit(solution)/shard_map/ppermute | solution.py:479
  13.3 2.2 %collective-permute-start.3 = (bf16[12,32,128]{2,1,0:T(8,128)(2,1)S(1)}, bf16[12,32,128]{2,1,0:T(8,128)(2,1)S(1)}, u32[]{:S(2)}, u32[]{:S(2)}) collective-permute-start(bf16[12,32,128]{2,1,0:T(8,128)(2,1)S(1)} %get-tuple-element.37), channel_id=1, source_target_pairs={{0,1},{1,0},{2,3},{3,2},{4,5},{5,4},{6,7},{7,6},{8,9},{9,8},{10,11... | collective-permute-start | bytes 294920 | tf_op jit(solution)/shard_map/ppermute | solution.py:503
  16.2 2.5 %collective-permute-done.3.ye = bf16[12,32,128]{2,1,0:T(8,128)(2,1)S(1)} collective-permute-done((bf16[12,32,128]{2,1,0:T(8,128)(2,1)S(1)}, bf16[12,32,128]{2,1,0:T(8,128)(2,1)S(1)}, u32[]{:S(2)}, u32[]{:S(2)}) %collective-permute-start.3) | collective-permute-done | bytes 98336 | tf_op jit(solution)/shard_map/ppermute | solution.py:503
  18.7 1.5 %forward_kernel.1 = (bf16[10,12,16,128]{3,2,1,0:T(8,128)(2,1)S(1)}, bf16[12,14,32,128]{3,2,1,0:T(8,128)(2,1)S(1)}, bf16[122,16,128]{2,1,0:T(8,128)(2,1)S(1)}, bf...) custom-call(s32[4]{0:T(128)S(1)} %pad_add_fusion.pos, ...), custom_call_target="tpu_custom_call" | custom-call | flops 4140000000 | bytes 1 | tf_op jit(solution)/shard_map/forward_kernel/pallas_call | solution.py:22
  20.3 3.9 %collective-permute-start.7 = (bf16[122,16,128]{2,1,0:T(8,128)(2,1)S(1)}, bf16[122,16,128]{2,1,0:T(8,128)(2,1)S(1)}, u32[]{:S(2)}, u32[]{:S(2)}) collective-permute-start(bf16[122,16,128]{2,1,0:T(8,128)(2,1)S(1)} %get-tuple-element.45), channel_id=1, source_target_pairs={{8,16},{24,32},{40,48},{56,64},{72,80},{88,96},{104,112},{120,128}... | collective-permute-start | bytes 1499144 | tf_op jit(solution)/shard_map/ppermute | solution.py:516
  24.9 8.9 %collective-permute-start.9 = (bf16[26,16,128]{2,1,0:T(8,128)(2,1)S(1)}, bf16[26,16,128]{2,1,0:T(8,128)(2,1)S(1)}, u32[]{:S(2)}, u32[]{:S(2)}) collective-permute-start(bf16[26,16,128]{2,1,0:T(8,128)(2,1)S(1)} %get-tuple-element.49), channel_id=1, source_target_pairs={{0,1},{1,0},{2,3},{3,2},{4,5},{5,4},{6,7},{7,6},{8,9},{9,8},{10,11... | collective-permute-start | bytes 319496 | tf_op jit(solution)/shard_map/ppermute | solution.py:517
  33.8 3.6 %inner_kernel.1 = (f32[10,12,16,128]{3,2,1,0:T(8,128)S(1)}, f32[16,128]{1,0:T(8,128)S(1)}) custom-call(bf16[10,12,16,128]{3,2,1,0:T(8,128)(2,1)S(1)} %get-tuple-element.40.emb, s32[10,12,128]{2,1,0:T(8,128)S(1)} %copy-done.2, bf16[76,16,128]{2,1,0:T(8,128)(2,1)S(1)} %collective-permute-done.4.ao.fo, bf16[76,16,128]{2,1,0:T(8,128)(2,1)S(1)} %collective-permute-done.5.ae.fe), custom_call_target="tpu_custom_call" | custom-call | flops 4600000000 | bytes 1 | tf_op jit(solution)/shard_map/inner_kernel/pallas_call | solution.py:22
  37.4 1.7 %outer_z_kernel.1 = (f32[10,12,16,128]{3,2,1,0:T(8,128)S(1)}, f32[16,128]{1,0:T(8,128)S(1)}) custom-call(s32[4]{0:T(128)S(1)} %pad_add_fusion.pos, bf16[10,12,16,128]{3,2,1,0:T(8,128)(2,1)S(1)} %get-tuple-element.40.emb, s32[10,12,128]{2,1,0:T(8,128)S(1)} %copy-done.2, f32[10,12,16,128]{3,2,1,0:T(8,128)S(1)} %get-tuple-element.42.grad_in, ...), custom_call_target="tpu_custom_call" | custom-call | flops 1724999936 | bytes 1 | tf_op jit(solution)/shard_map/outer_z_kernel/pallas_call | solution.py:22
  39.1 3.5 %outer_kernel.1 = (bf16[10,12,16,128]{3,2,1,0:T(8,128)(2,1)S(1)}, bf16[12,16,128]{2,1,0:T(8,128)(2,1)S(1)}, bf16[12,16,128]{2,1,0:T(8,128)(2,1)S(1)}, f32[256,128]{1,0:T(8,128)}) custom-call(s32[4]{0:T(128)S(1)} %pad_add_fusion.pos, bf16[10,12,16,128]{3,2,1,0:T(8,128)(2,1)S(1)} %get-tuple-element.40.emb, s32[10,12,128]{2,1,0:T(8,128)S(1)} %copy-done.2, ...), custom_call_target="tpu_custom_call" | custom-call | flops 4255000064 | bytes 1 | tf_op jit(solution)/shard_map/outer_kernel/pallas_call | solution.py:22
  42.7 7.1 %all-to-all-start = ((f32[32,8,128]{2,1,0:T(8,128)}), f32[32,8,128]{2,1,0:T(8,128)S(1)}, u32[]{:S(2)}, u32[]{:S(2)}) async-start(f32[32,8,128]{2,1,0:T(8,128)} %bitcast.8), calls=%async_computation | async-start | bytes 262144 | tf_op jit(solution)/shard_map/all_to_all | solution.py:574
  50.4 3.4 %collective-permute-start.11 = (bf16[12,16,128]{2,1,0:T(8,128)(2,1)S(1)}, bf16[12,16,128]{2,1,0:T(8,128)(2,1)S(1)}, u32[]{:S(2)}, u32[]{:S(2)}) collective-permute-start(bf16[12,16,128]{2,1,0:T(8,128)(2,1)S(1)} %get-tuple-element.53), channel_id=1, source_target_pairs={{8,16},{24,32},{40,48},{56,64},{72,80},{88,96},{104,112},{120,128}... | collective-permute-start | bytes 147464 | tf_op jit(solution)/shard_map/ppermute | solution.py:565
  53.9 4.5 %all-to-all-done.parts = f32[32,8,128]{2,1,0:T(8,128)S(1)} async-done(((f32[32,8,128]{2,1,0:T(8,128)}), f32[32,8,128]{2,1,0:T(8,128)S(1)}, u32[]{:S(2)}, u32[]{:S(2)}) %all-to-all-start) | async-done | bytes 131104 | tf_op jit(solution)/shard_map/all_to_all | solution.py:574
  59.0 18.8 %all-to-all-start.1 = ((f32[8,8,128]{2,1,0:T(8,128)}), f32[8,8,128]{2,1,0:T(8,128)S(1)}, u32[]{:S(2)}, u32[]{:S(2)}) async-start(f32[8,8,128]{2,1,0:T(8,128)} %spread_kernel.2.after), calls=%async_computation.1 | async-start | bytes 65536 | tf_op jit(solution)/shard_map/all_to_all | solution.py:584
  79.0 4.0 %collective-permute-start.13 = (bf16[12,16,128]{2,1,0:T(8,128)(2,1)S(1)}, bf16[12,16,128]{2,1,0:T(8,128)(2,1)S(1)}, u32[]{:S(2)}, u32[]{:S(2)}) collective-permute-start(bf16[12,16,128]{2,1,0:T(8,128)(2,1)S(1)} %get-tuple-element.55), channel_id=1, source_target_pairs={{0,1},{1,0},{2,3},{3,2},{4,5},{5,4},{6,7},{7,6},{8,9},{9,8},{10,11... | collective-permute-start | bytes 147464 | tf_op jit(solution)/shard_map/ppermute | solution.py:571
  83.0 3.8 %all-to-all-done.1.parts = f32[8,8,128]{2,1,0:T(8,128)S(1)} async-done(((f32[8,8,128]{2,1,0:T(8,128)}), f32[8,8,128]{2,1,0:T(8,128)S(1)}, u32[]{:S(2)}, u32[]{:S(2)}) %all-to-all-start.1) | async-done | bytes 32800 | tf_op jit(solution)/shard_map/all_to_all | solution.py:584
  87.4 5.3 %all-to-all-start.2 = ((f32[32,8,128]{2,1,0:T(8,128)}), f32[32,8,128]{2,1,0:T(8,128)S(1)}, u32[]{:S(2)}, u32[]{:S(2)}) async-start(f32[32,8,128]{2,1,0:T(8,128)} %spread_kernel.3), calls=%async_computation.2 | async-start | bytes 262144 | tf_op jit(solution)/shard_map/all_to_all | solution.py:586
  92.8 2.8 %backward_kernel.1 = bf16[10,12,32,128]{3,2,1,0:T(8,128)(2,1)} custom-call(s32[4]{0:T(128)S(1)} %pad_add_fusion.pos, bf16[10,12,16,128]{3,2,1,0:T(8,128)(2,1)S(1)} %get-tuple-element.51.own, bf16[12,16,128]{2,1,0:T(8,128)(2,1)S(1)} %collective-permute-done.12.yo, bf16[12,16,128]{2,1,0:T(8,128)(2,1)S(1)} %collective-permute-done.13.ye, ...), custom_call_target="tpu_custom_call" | custom-call | flops 5634999808 | bytes 1 | tf_op jit(solution)/shard_map/backward_kernel/pallas_call | solution.py:22
  95.6 5.8 %all-to-all-done.2 = f32[32,8,128]{2,1,0:T(8,128)S(1)} async-done(((f32[32,8,128]{2,1,0:T(8,128)}), f32[32,8,128]{2,1,0:T(8,128)S(1)}, u32[]{:S(2)}, u32[]{:S(2)}) %all-to-all-start.2) | async-done | bytes 131104 | tf_op jit(solution)/shard_map/all_to_all | solution.py:586
  101.4 0.8 final_kernel.1
  (40 shorter events, 6.3 us)
Async XLA Ops:
  0.7 1.2 %copy-start = (bf16[32,10,12,128]{3,0,2,1:T(8,128)(2,1)S(1)}, bf16[32,10,12,128]{3,0,2,1:T(8,128)(2,1)}, u32[]{:S(2)}) copy-start(bf16[32,10,12,128]{3,0,2,1:T(8,128)(2,1)} %param.4) | copy-start | bytes 2949124
  1.9 6.1 %copy-start.3 = (bf16[16,32,3,3,3]{1,0,4,3,2:T(8,128)(2,1)S(1)}, bf16[16,32,3,3,3]{1,0,4,3,2:T(8,128)(2,1)}, u32[]{:S(2)}) copy-start(bf16[16,32,3,3,3]{1,0,4,3,2:T(8,128)(2,1)} %param.6) | copy-start | bytes 82948
  1.9 6.3 %copy-start.4 = (f32[16]{0:T(128)S(1)}, f32[16]{0:T(128)}, u32[]{:S(2)}) copy-start(f32[16]{0:T(128)} %param.7) | copy-start | bytes 196
  1.9 6.4 %copy-start.1 = (bf16[32,10,12,128]{3,0,2,1:T(8,128)(2,1)S(1)}, bf16[32,10,12,128]{3,0,2,1:T(8,128)(2,1)}, u32[]{:S(2)}) copy-start(bf16[32,10,12,128]{3,0,2,1:T(8,128)(2,1)} %param.4) | copy-start | bytes 2949124
  1.9 6.4 %copy-start.2 = (s32[10,12,128]{2,1,0:T(8,128)S(1)}, s32[10,12,128]{2,1,0:T(8,128)}, u32[]{:S(2)}) copy-start(s32[10,12,128]{2,1,0:T(8,128)} %lab.7) | copy-start | bytes 184324
  2.8 7.5 %collective-permute-start = (bf16[12,32,128]{2,1,0:T(8,128)(2,1)S(1)}, bf16[12,32,128]{2,1,0:T(8,128)(2,1)S(1)}, u32[]{:S(2)}, u32[]{:S(2)}) collective-permute-start(bf16[12,32,128]{2,1,0:T(8,128)(2,1)S(1)} %get-tuple-element.33), channel_id=1, source_target_pairs={{0,8},{8,0},{16,24},{24,16},{32,40},{40,32},{48,56},{56,48},{64,72... | collective-permute-start | bytes 294920 | tf_op jit(solution)/shard_map/ppermute | solution.py:478
  6.1 5.9 %collective-permute-start.1 = (bf16[12,32,128]{2,1,0:T(8,128)(2,1)S(1)}, bf16[12,32,128]{2,1,0:T(8,128)(2,1)S(1)}, u32[]{:S(2)}, u32[]{:S(2)}) collective-permute-start(bf16[12,32,128]{2,1,0:T(8,128)(2,1)S(1)} %get-tuple-element.34), channel_id=1, source_target_pairs={{8,16},{24,32},{40,48},{56,64},{72,80},{88,96},{104,112},{120,128}... | collective-permute-start | bytes 294920 | tf_op jit(solution)/shard_map/ppermute | solution.py:479
  12.6 3.6 %collective-permute-start.2 = (bf16[12,32,128]{2,1,0:T(8,128)(2,1)S(1)}, bf16[12,32,128]{2,1,0:T(8,128)(2,1)S(1)}, u32[]{:S(2)}, u32[]{:S(2)}) collective-permute-start(bf16[12,32,128]{2,1,0:T(8,128)(2,1)S(1)} %get-tuple-element.36), channel_id=1, source_target_pairs={{1,2},{3,4},{5,6},{2,1},{4,3},{6,5},{9,10},{11,12},{13,14},{10,9},... | collective-permute-start | bytes 294920 | tf_op jit(solution)/shard_map/ppermute | solution.py:504
  13.3 5.5 %collective-permute-start.3 = (bf16[12,32,128]{2,1,0:T(8,128)(2,1)S(1)}, bf16[12,32,128]{2,1,0:T(8,128)(2,1)S(1)}, u32[]{:S(2)}, u32[]{:S(2)}) collective-permute-start(bf16[12,32,128]{2,1,0:T(8,128)(2,1)S(1)} %get-tuple-element.37), channel_id=1, source_target_pairs={{0,1},{1,0},{2,3},{3,2},{4,5},{5,4},{6,7},{7,6},{8,9},{9,8},{10,11... | collective-permute-start | bytes 294920 | tf_op jit(solution)/shard_map/ppermute | solution.py:503
  15.4 9.5 %collective-permute-start.5 = (bf16[76,16,128]{2,1,0:T(8,128)(2,1)S(1)}, bf16[76,16,128]{2,1,0:T(8,128)(2,1)S(1)}, u32[]{:S(2)}, u32[]{:S(2)}) collective-permute-start(bf16[76,16,128]{2,1,0:T(8,128)(2,1)S(1)} %get-tuple-element.35.after), channel_id=1, source_target_pairs={{0,1},{1,0},{2,3},{3,2},{4,5},{5,4},{6,7},{7,6},{8,9},{9,8},{10,11... | collective-permute-start | bytes 933896 | tf_op jit(solution)/shard_map/ppermute | solution.py:497
  15.5 18.3 %collective-permute-start.4 = (bf16[76,16,128]{2,1,0:T(8,128)(2,1)S(1)}, bf16[76,16,128]{2,1,0:T(8,128)(2,1)S(1)}, u32[]{:S(2)}, u32[]{:S(2)}) collective-permute-start(bf16[76,16,128]{2,1,0:T(8,128)(2,1)S(1)} %get-tuple-element.41), channel_id=1, source_target_pairs={{1,2},{3,4},{5,6},{2,1},{4,3},{6,5},{9,10},{11,12},{13,14},{10,9},... | collective-permute-start | bytes 933896 | tf_op jit(solution)/shard_map/ppermute | solution.py:498
  20.2 17.2 %collective-permute-start.6 = (bf16[122,16,128]{2,1,0:T(8,128)(2,1)S(1)}, bf16[122,16,128]{2,1,0:T(8,128)(2,1)S(1)}, u32[]{:S(2)}, u32[]{:S(2)}) collective-permute-start(bf16[122,16,128]{2,1,0:T(8,128)(2,1)S(1)} %get-tuple-element.44), channel_id=1, source_target_pairs={{0,8},{8,0},{16,24},{24,16},{32,40},{40,32},{48,56},{56,48},{64,72... | collective-permute-start | bytes 1499144 | tf_op jit(solution)/shard_map/ppermute | solution.py:515
  20.3 17.1 %collective-permute-start.7 = (bf16[122,16,128]{2,1,0:T(8,128)(2,1)S(1)}, bf16[122,16,128]{2,1,0:T(8,128)(2,1)S(1)}, u32[]{:S(2)}, u32[]{:S(2)}) collective-permute-start(bf16[122,16,128]{2,1,0:T(8,128)(2,1)S(1)} %get-tuple-element.45), channel_id=1, source_target_pairs={{8,16},{24,32},{40,48},{56,64},{72,80},{88,96},{104,112},{120,128}... | collective-permute-start | bytes 1499144 | tf_op jit(solution)/shard_map/ppermute | solution.py:516
  24.2 14.9 %collective-permute-start.8 = (bf16[26,16,128]{2,1,0:T(8,128)(2,1)S(1)}, bf16[26,16,128]{2,1,0:T(8,128)(2,1)S(1)}, u32[]{:S(2)}, u32[]{:S(2)}) collective-permute-start(bf16[26,16,128]{2,1,0:T(8,128)(2,1)S(1)} %get-tuple-element.48), channel_id=1, source_target_pairs={{1,2},{3,4},{5,6},{2,1},{4,3},{6,5},{9,10},{11,12},{13,14},{10,9},... | collective-permute-start | bytes 319496 | tf_op jit(solution)/shard_map/ppermute | solution.py:518
  24.9 14.2 %collective-permute-start.9 = (bf16[26,16,128]{2,1,0:T(8,128)(2,1)S(1)}, bf16[26,16,128]{2,1,0:T(8,128)(2,1)S(1)}, u32[]{:S(2)}, u32[]{:S(2)}) collective-permute-start(bf16[26,16,128]{2,1,0:T(8,128)(2,1)S(1)} %get-tuple-element.49), channel_id=1, source_target_pairs={{0,1},{1,0},{2,3},{3,2},{4,5},{5,4},{6,7},{7,6},{8,9},{9,8},{10,11... | collective-permute-start | bytes 319496 | tf_op jit(solution)/shard_map/ppermute | solution.py:517
  42.7 15.7 %all-to-all-start = ((f32[32,8,128]{2,1,0:T(8,128)}), f32[32,8,128]{2,1,0:T(8,128)S(1)}, u32[]{:S(2)}, u32[]{:S(2)}) async-start(f32[32,8,128]{2,1,0:T(8,128)} %bitcast.8), calls=%async_computation | async-start | bytes 262144 | tf_op jit(solution)/shard_map/all_to_all | solution.py:574
  50.1 27.6 %collective-permute-start.10 = (bf16[12,16,128]{2,1,0:T(8,128)(2,1)S(1)}, bf16[12,16,128]{2,1,0:T(8,128)(2,1)S(1)}, u32[]{:S(2)}, u32[]{:S(2)}) collective-permute-start(bf16[12,16,128]{2,1,0:T(8,128)(2,1)S(1)} %get-tuple-element.52.after), channel_id=1, source_target_pairs={{0,8},{8,0},{16,24},{24,16},{32,40},{40,32},{48,56},{56,48},{64,72... | collective-permute-start | bytes 147464 | tf_op jit(solution)/shard_map/ppermute | solution.py:564
  50.4 27.3 %collective-permute-start.11 = (bf16[12,16,128]{2,1,0:T(8,128)(2,1)S(1)}, bf16[12,16,128]{2,1,0:T(8,128)(2,1)S(1)}, u32[]{:S(2)}, u32[]{:S(2)}) collective-permute-start(bf16[12,16,128]{2,1,0:T(8,128)(2,1)S(1)} %get-tuple-element.53), channel_id=1, source_target_pairs={{8,16},{24,32},{40,48},{56,64},{72,80},{88,96},{104,112},{120,128}... | collective-permute-start | bytes 147464 | tf_op jit(solution)/shard_map/ppermute | solution.py:565
  59.0 27.8 %all-to-all-start.1 = ((f32[8,8,128]{2,1,0:T(8,128)}), f32[8,8,128]{2,1,0:T(8,128)S(1)}, u32[]{:S(2)}, u32[]{:S(2)}) async-start(f32[8,8,128]{2,1,0:T(8,128)} %spread_kernel.2.after), calls=%async_computation.1 | async-start | bytes 65536 | tf_op jit(solution)/shard_map/all_to_all | solution.py:584
  78.3 14.4 %collective-permute-start.12 = (bf16[12,16,128]{2,1,0:T(8,128)(2,1)S(1)}, bf16[12,16,128]{2,1,0:T(8,128)(2,1)S(1)}, u32[]{:S(2)}, u32[]{:S(2)}) collective-permute-start(bf16[12,16,128]{2,1,0:T(8,128)(2,1)S(1)} %get-tuple-element.54), channel_id=1, source_target_pairs={{1,2},{3,4},{5,6},{2,1},{4,3},{6,5},{9,10},{11,12},{13,14},{10,9},... | collective-permute-start | bytes 147464 | tf_op jit(solution)/shard_map/ppermute | solution.py:572
  79.0 13.8 %collective-permute-start.13 = (bf16[12,16,128]{2,1,0:T(8,128)(2,1)S(1)}, bf16[12,16,128]{2,1,0:T(8,128)(2,1)S(1)}, u32[]{:S(2)}, u32[]{:S(2)}) collective-permute-start(bf16[12,16,128]{2,1,0:T(8,128)(2,1)S(1)} %get-tuple-element.55), channel_id=1, source_target_pairs={{0,1},{1,0},{2,3},{3,2},{4,5},{5,4},{6,7},{7,6},{8,9},{9,8},{10,11... | collective-permute-start | bytes 147464 | tf_op jit(solution)/shard_map/ppermute | solution.py:571
  87.4 14.0 %all-to-all-start.2 = ((f32[32,8,128]{2,1,0:T(8,128)}), f32[32,8,128]{2,1,0:T(8,128)S(1)}, u32[]{:S(2)}, u32[]{:S(2)}) async-start(f32[32,8,128]{2,1,0:T(8,128)} %spread_kernel.3), calls=%async_computation.2 | async-start | bytes 262144 | tf_op jit(solution)/shard_map/all_to_all | solution.py:586
